TPU v7x, 32 devices: a whole 2x2x4 slice. The times are simulated.
32 devices in a mesh: dp: 8 (over y, x, core), tensor: 4 (over z).
Axes of the slice: x: 2, y: 2, z: 4, core: 2. Of those that a mesh axis runs over, the one named last changes fastest.
Arguments:
- tokens: bfloat16 [8, 4, 256, 1024], P('dp', None, 'tensor'), may hold values from -6 to 6
- cotangent: bfloat16 [8, 4, 256, 1024], P('dp', None, 'tensor'), may hold values from -6 to 6
- lengths: int32 [16], replicated, may hold values from 1 to 1024, as said below
- groups: int32 [16], replicated, may hold values from 0 to 7, as said below
- offsets: int32 [16], replicated, may hold values from 0 to 7
- attention_gain: float32 [1024], replicated, may hold values from 0.25 to 1.75
- feed_gain: float32 [1024], replicated, may hold values from 0.25 to 1.75
- query_gain: float32 [64], replicated, may hold values from 0.25 to 1.75
- key_gain: float32 [64], replicated, may hold values from 0.25 to 1.75
- query_weight: bfloat16 [1024, 1024], P('dp', 'tensor'), may hold values from -0.1875 to 0.1875
- key_weight: bfloat16 [1024, 512], P('dp', 'tensor'), may hold values from -0.1875 to 0.1875
- value_weight: bfloat16 [1024, 512], P('dp', 'tensor'), may hold values from -0.1875 to 0.1875
- out_weight: bfloat16 [1024, 1024], P('tensor', 'dp'), may hold values from -3 to 3
- gate_weight: bfloat16 [1024, 4608], P('dp', 'tensor'), may hold values from -0.1875 to 0.1875
- up_weight: bfloat16 [1024, 4608], P('dp', 'tensor'), may hold values from -0.1875 to 0.1875
- down_weight: bfloat16 [4608, 1024], P('tensor', 'dp'), may hold values from -0.09375 to 0.09375
Outputs:
- output: bfloat16 [8, 4, 256, 1024], P('dp', None, 'tensor')
- grad_tokens: bfloat16 [8, 4, 256, 1024], P('dp', None, 'tensor')
- grad_attention_gain: float32 [1024], replicated
- grad_feed_gain: float32 [1024], replicated
- grad_query_gain: float32 [64], replicated
- grad_key_gain: float32 [64], replicated
- grad_query_weight: float32 [1024, 1024], P('dp', 'tensor')
- grad_key_weight: float32 [1024, 512], P('dp', 'tensor')
- grad_value_weight: float32 [1024, 512], P('dp', 'tensor')
- grad_out_weight: float32 [1024, 1024], P('tensor', 'dp')
- grad_gate_weight: float32 [1024, 4608], P('dp', 'tensor')
- grad_up_weight: float32 [1024, 4608], P('dp', 'tensor')
- grad_down_weight: float32 [4608, 1024], P('tensor', 'dp')
Inputs may be any that keep to these rules, and one draw needn't show every extreme that they name: `lengths`: each sequence lies inside its dp index's 1024 rows, starts on a block and intersections no other; some sequence has exactly 1024 tokens. `groups`: each dp index holds one or three sequences.
All inputs are finite; a program needn't handle non-finite values.
Results may differ from a plain program's by a relative error of at most 0.018.
Values may be sent and summed in bfloat16 or wider, within the bound.
No kernel may reach another device: no remote copies, remote signals or barrier semaphores. Data moves between devices by JAX's collectives and lax.ppermute only.
A program may use at most 128 MiB of HBM per device.

v0:
```python
import jax
import jax.numpy as jnp
from jax import lax
from jax.sharding import PartitionSpec as P

BLOCK = 128
QROWS = 512


EPS = 1e-05
THETA = 1000000.0
NEG = -1e30


def norm_rows(values, gain):
    return values * lax.rsqrt(jnp.mean(values * values, axis=-1, keepdims=True) + EPS) * gain


def turn_half(values):
    half = values.shape[-1] // 2
    return jnp.concatenate([-values[..., half:], values[..., :half]], axis=-1)


def rotated(values, gain, cosine, sine):
    normed = norm_rows(values, gain)
    return normed * cosine + turn_half(normed) * sine


def on_device(
    tokens,
    cotangent,
    lengths,
    groups,
    offsets,
    attention_gain,
    feed_gain,
    query_gain,
    key_gain,
    query_weight,
    key_weight,
    value_weight,
    out_weight,
    gate_weight,
    up_weight,
    down_weight,
):
    shard_shape = tokens.shape
    width = shard_shape[3]
    tensor_count = lax.axis_size("tensor")
    local_rows = shard_shape[1] * shard_shape[2]
    group_rows = local_rows * tensor_count
    gathered_shape = (1, shard_shape[1], shard_shape[2] * tensor_count, width)
    head_dim = query_gain.shape[0]
    full = (
        lax.all_gather(query_weight, "dp", axis=0, tiled=True),
        lax.all_gather(key_weight, "dp", axis=0, tiled=True),
        lax.all_gather(value_weight, "dp", axis=0, tiled=True),
        lax.all_gather(out_weight, "dp", axis=1, tiled=True),
        lax.all_gather(gate_weight, "dp", axis=0, tiled=True),
        lax.all_gather(up_weight, "dp", axis=0, tiled=True),
        lax.all_gather(down_weight, "dp", axis=1, tiled=True),
    )
    query_full, key_full, value_full, out_full, gate_full, up_full, down_full = full
    heads = query_full.shape[1] // head_dim
    value_heads = key_full.shape[1] // head_dim
    repeat = heads // value_heads
    query_cols = query_full.shape[1]
    key_cols = key_full.shape[1]
    hidden_cols = gate_full.shape[1]
    project = jnp.concatenate([query_full, key_full, value_full], axis=1)
    gate_up = jnp.concatenate([gate_full, up_full], axis=1)
    group = lax.axis_index("dp")
    position = jnp.arange(group_rows, dtype=jnp.int32)
    start = offsets * BLOCK
    finish = start + lengths
    number = jnp.arange(lengths.shape[0], dtype=jnp.int32)
    inside = (
        (groups[None, :] == group)
        & (position[:, None] >= start[None, :])
        & (position[:, None] < finish[None, :])
    ).astype(jnp.int32)
    segment = jnp.sum(inside * (number + 1)[None, :], axis=1) - 1
    segment = jnp.where(segment >= 0, segment, -1 - position)
    inner_pos = jnp.sum(inside * (position[:, None] - start[None, :]), axis=1)
    freq = THETA ** (-(jnp.arange(head_dim // 2, dtype=jnp.float32) * 2.0) / head_dim)
    angle = inner_pos.astype(jnp.float32)[:, None] * freq[None, :]
    cosine = jnp.concatenate([jnp.cos(angle), jnp.cos(angle)], axis=1)[:, None, :]
    sine = jnp.concatenate([jnp.sin(angle), jnp.sin(angle)], axis=1)[:, None, :]
    local_x = tokens.reshape(local_rows, width).astype(jnp.float32)
    attn_in = norm_rows(local_x, attention_gain).astype(jnp.bfloat16)
    attn_rows = lax.all_gather(attn_in.reshape(shard_shape), "tensor", axis=2, tiled=True).reshape(
        group_rows, width
    )
    projected = jnp.dot(attn_rows, project, preferred_element_type=jnp.float32)
    query_pre = projected[:, :query_cols].reshape(group_rows, heads, head_dim)
    key_pre = projected[:, query_cols : query_cols + key_cols].reshape(
        group_rows, value_heads, head_dim
    )
    value_pre = projected[:, query_cols + key_cols :]
    queries = (
        rotated(query_pre, query_gain, cosine, sine)
        .astype(jnp.bfloat16)
        .reshape(group_rows, value_heads, repeat, head_dim)
    )
    keys = rotated(key_pre, key_gain, cosine, sine).astype(jnp.bfloat16)
    values = value_pre.astype(jnp.bfloat16).reshape(group_rows, value_heads, head_dim)
    scale = head_dim ** (-0.5)
    block_count = group_rows // QROWS

    def block_scores(index):
        first = index * QROWS
        last = first + QROWS
        scores = (
            jnp.einsum(
                "qkgd,pkd->kgqp",
                queries[first:last],
                keys[:last],
                preferred_element_type=jnp.float32,
            )
            * scale
        )
        allowed = (segment[first:last, None] == segment[None, :last]) & (
            position[None, :last] <= position[first:last, None]
        )
        return jnp.where(allowed, scores, NEG)

    mixed_parts = []
    log_totals = []
    for index in range(block_count):
        last = (index + 1) * QROWS
        scores = block_scores(index)
        summit = jnp.max(scores, axis=-1, keepdims=True)
        shifted = jnp.exp(scores - summit)
        total = jnp.sum(shifted, axis=-1, keepdims=True)
        attend = (shifted / total).astype(jnp.bfloat16)
        log_totals.append(summit + jnp.log(total))
        mixed_parts.append(
            jnp.einsum("kgqp,pkd->qkgd", attend, values[:last], preferred_element_type=jnp.float32)
        )
    mixed = (
        jnp.concatenate(mixed_parts, axis=0)
        .reshape(group_rows, heads * head_dim)
        .astype(jnp.bfloat16)
    )
    attn_part = jnp.dot(mixed, out_full, preferred_element_type=jnp.float32)
    attn_out = lax.psum_scatter(
        attn_part.reshape(gathered_shape), "tensor", scatter_dimension=2, tiled=True
    ).reshape(local_rows, width)
    middle = local_x + attn_out
    feed_in = norm_rows(middle, feed_gain).astype(jnp.bfloat16)
    feed_rows = lax.all_gather(feed_in.reshape(shard_shape), "tensor", axis=2, tiled=True).reshape(
        group_rows, width
    )
    gate_up_out = jnp.dot(feed_rows, gate_up, preferred_element_type=jnp.float32)
    gate = gate_up_out[:, :hidden_cols]
    up = gate_up_out[:, hidden_cols:]
    hidden = (jax.nn.silu(gate) * up).astype(jnp.bfloat16)
    feed_part = jnp.dot(hidden, down_full, preferred_element_type=jnp.float32)
    feed_out = (
        lax.psum_scatter(
            feed_part.reshape(gathered_shape).astype(jnp.bfloat16),
            "tensor",
            scatter_dimension=2,
            tiled=True,
        )
        .astype(jnp.float32)
        .reshape(local_rows, width)
    )
    output = (middle + feed_out).astype(jnp.bfloat16).reshape(shard_shape)
    back_rows = lax.all_gather(cotangent, "tensor", axis=2, tiled=True).reshape(group_rows, width)
    grad_hidden = jnp.einsum("gd,fd->gf", back_rows, down_full, preferred_element_type=jnp.float32)
    grad_down = jnp.einsum("gf,gd->fd", hidden, back_rows, preferred_element_type=jnp.float32)

    def gated(gate_in, up_in):
        return jax.nn.silu(gate_in) * up_in

    _, gated_pull = jax.vjp(gated, gate, up)
    grad_gate, grad_up = gated_pull(grad_hidden)
    grad_gate_up = jnp.concatenate([grad_gate, grad_up], axis=1).astype(jnp.bfloat16)
    grad_feed_part = jnp.einsum(
        "gf,df->gd", grad_gate_up, gate_up, preferred_element_type=jnp.float32
    )
    grad_gate_up_weight = jnp.einsum(
        "gd,gf->df", feed_rows, grad_gate_up, preferred_element_type=jnp.float32
    )
    grad_gate_w = grad_gate_up_weight[:, :hidden_cols]
    grad_up_w = grad_gate_up_weight[:, hidden_cols:]
    grad_feed_in = (
        lax.psum_scatter(
            grad_feed_part.reshape(gathered_shape).astype(jnp.bfloat16),
            "tensor",
            scatter_dimension=2,
            tiled=True,
        )
        .astype(jnp.float32)
        .reshape(local_rows, width)
    )
    _, feed_pull = jax.vjp(norm_rows, middle, feed_gain)
    grad_middle_norm, grad_feed_gain = feed_pull(grad_feed_in)
    grad_middle = cotangent.reshape(local_rows, width).astype(jnp.float32) + grad_middle_norm
    back_attn = lax.all_gather(
        grad_middle.astype(jnp.bfloat16).reshape(shard_shape), "tensor", axis=2, tiled=True
    ).reshape(group_rows, width)
    grad_out_w = jnp.einsum("gh,gd->hd", mixed, back_attn, preferred_element_type=jnp.float32)
    grad_mixed = (
        jnp.einsum("gd,hd->gh", back_attn, out_full, preferred_element_type=jnp.float32)
        .astype(jnp.bfloat16)
        .reshape(group_rows, value_heads, repeat, head_dim)
    )
    grad_keys = jnp.zeros((group_rows, value_heads, head_dim), jnp.float32)
    grad_values = jnp.zeros((group_rows, value_heads, head_dim), jnp.float32)
    query_parts = []
    for index in range(block_count):
        first = index * QROWS
        last = first + QROWS
        scores = block_scores(index)
        attend = jnp.exp(scores - log_totals[index])
        attend_low = attend.astype(jnp.bfloat16)
        grad_here = grad_mixed[first:last]
        grad_values = grad_values.at[:last].add(
            jnp.einsum("kgqp,qkgd->pkd", attend_low, grad_here, preferred_element_type=jnp.float32)
        )
        grad_attend = jnp.einsum(
            "qkgd,pkd->kgqp", grad_here, values[:last], preferred_element_type=jnp.float32
        )
        inner = jnp.sum(attend * grad_attend, axis=-1, keepdims=True)
        grad_scores = (attend * (grad_attend - inner)).astype(jnp.bfloat16)
        query_parts.append(
            jnp.einsum(
                "kgqp,pkd->qkgd", grad_scores, keys[:last], preferred_element_type=jnp.float32
            )
            * scale
        )
        grad_keys = grad_keys.at[:last].add(
            jnp.einsum(
                "kgqp,qkgd->pkd",
                grad_scores,
                queries[first:last],
                preferred_element_type=jnp.float32,
            )
            * scale
        )
    grad_queries = jnp.concatenate(query_parts, axis=0).reshape(group_rows, heads, head_dim)

    def query_side(values_in, gain_in):
        return rotated(values_in, gain_in, cosine, sine)

    _, query_pull = jax.vjp(query_side, query_pre, query_gain)
    grad_query_pre, grad_query_gain = query_pull(grad_queries)
    _, key_pull = jax.vjp(query_side, key_pre, key_gain)
    grad_key_pre, grad_key_gain = key_pull(grad_keys)
    grad_project = jnp.concatenate(
        [
            grad_query_pre.reshape(group_rows, query_cols),
            grad_key_pre.reshape(group_rows, key_cols),
            grad_values.reshape(group_rows, key_cols),
        ],
        axis=1,
    ).astype(jnp.bfloat16)
    grad_attn_part = jnp.einsum(
        "gc,dc->gd", grad_project, project, preferred_element_type=jnp.float32
    )
    grad_project_w = jnp.einsum(
        "gd,gc->dc", attn_rows, grad_project, preferred_element_type=jnp.float32
    )
    grad_query_w = grad_project_w[:, :query_cols]
    grad_key_w = grad_project_w[:, query_cols : query_cols + key_cols]
    grad_value_w = grad_project_w[:, query_cols + key_cols :]
    grad_attn_in = (
        lax.psum_scatter(
            grad_attn_part.reshape(gathered_shape).astype(jnp.bfloat16),
            "tensor",
            scatter_dimension=2,
            tiled=True,
        )
        .astype(jnp.float32)
        .reshape(local_rows, width)
    )
    _, attn_pull = jax.vjp(norm_rows, local_x, attention_gain)
    grad_x_norm, grad_attention_gain = attn_pull(grad_attn_in)
    grad_tokens = (grad_middle + grad_x_norm).astype(jnp.bfloat16).reshape(shard_shape)
    gains = lax.psum(
        (grad_attention_gain, grad_feed_gain, grad_query_gain, grad_key_gain), ("dp", "tensor")
    )
    weight_grads = (
        lax.psum_scatter(
            grad_query_w.astype(jnp.bfloat16), "dp", scatter_dimension=0, tiled=True
        ).astype(jnp.float32),
        lax.psum_scatter(
            grad_key_w.astype(jnp.bfloat16), "dp", scatter_dimension=0, tiled=True
        ).astype(jnp.float32),
        lax.psum_scatter(
            grad_value_w.astype(jnp.bfloat16), "dp", scatter_dimension=0, tiled=True
        ).astype(jnp.float32),
        lax.psum_scatter(
            grad_out_w.astype(jnp.bfloat16), "dp", scatter_dimension=1, tiled=True
        ).astype(jnp.float32),
        lax.psum_scatter(
            grad_gate_w.astype(jnp.bfloat16), "dp", scatter_dimension=0, tiled=True
        ).astype(jnp.float32),
        lax.psum_scatter(
            grad_up_w.astype(jnp.bfloat16), "dp", scatter_dimension=0, tiled=True
        ).astype(jnp.float32),
        lax.psum_scatter(
            grad_down.astype(jnp.bfloat16), "dp", scatter_dimension=1, tiled=True
        ).astype(jnp.float32),
    )
    return (output, grad_tokens) + tuple(gains) + tuple(weight_grads)


def solution(mesh):
    in_specs = (
        P("dp", None, "tensor", None),
        P("dp", None, "tensor", None),
        P(),
        P(),
        P(),
        P(),
        P(),
        P(),
        P(),
        P("dp", "tensor"),
        P("dp", "tensor"),
        P("dp", "tensor"),
        P("tensor", "dp"),
        P("dp", "tensor"),
        P("dp", "tensor"),
        P("tensor", "dp"),
    )
    out_specs = (
        P("dp", None, "tensor", None),
        P("dp", None, "tensor", None),
        P(),
        P(),
        P(),
        P(),
        P("dp", "tensor"),
        P("dp", "tensor"),
        P("dp", "tensor"),
        P("tensor", "dp"),
        P("dp", "tensor"),
        P("dp", "tensor"),
        P("tensor", "dp"),
    )
    return jax.shard_map(
        on_device, mesh=mesh, in_specs=in_specs, out_specs=out_specs, check_vma=False
    )
```

profile of v0, /device:TPU:0, one launch (start us, length us, event | category | flops | bytes accessed | tf_op | source)
XLA Modules:
  0.0 746.3 jit_solution(5498011736017088241)
XLA Ops:
  12.9 11.0 %all_gather.35 = bf16[1024,128]{1,0:T(8,128)(2,1)S(1)} all-gather(bf16[128,128]{1,0:T(8,128)(2,1)} %param.38), channel_id=1, replica_groups=mesh['dp'=8,'tensor'=4] {'dp'}, dimensions={0}, use_global_device_ids=true | all-gather | bytes 294912 | tf_op jit(solution)/shard_map/all_gather | solution.py:56
  23.9 9.1 %all_gather.36 = bf16[1024,128]{1,0:T(8,128)(2,1)S(1)} all-gather(bf16[128,128]{1,0:T(8,128)(2,1)} %param.39), channel_id=1, replica_groups=mesh['dp'=8,'tensor'=4] {'dp'}, dimensions={0}, use_global_device_ids=true | all-gather | bytes 294912 | tf_op jit(solution)/shard_map/all_gather | solution.py:57
  33.0 9.2 %all_gather.34 = bf16[1024,256]{1,0:T(8,128)(2,1)S(1)} all-gather(bf16[128,256]{1,0:T(8,128)(2,1)} %param.37), channel_id=1, replica_groups=mesh['dp'=8,'tensor'=4] {'dp'}, dimensions={0}, use_global_device_ids=true | all-gather | bytes 589824 | tf_op jit(solution)/shard_map/all_gather | solution.py:55
  42.2 9.8 %all_gather.37 = bf16[256,1024]{1,0:T(8,128)(2,1)S(1)} all-gather(bf16[256,128]{1,0:T(8,128)(2,1)} %param.40), channel_id=1, replica_groups=mesh['dp'=8,'tensor'=4] {'dp'}, dimensions={1}, use_global_device_ids=true | all-gather | bytes 589824 | tf_op jit(solution)/shard_map/all_gather | solution.py:58
  55.1 5.1 all-gather.8.cloned.1.call-done
  60.2 3.2 fusion.94
  78.0 3.8 convolution_bitcast_fusion
  83.5 74.0 %reduce-scatter.16.cloned.1.call-done = f32[1,4,64,1024]{3,2,1,0:T(8,128)} async-done(((f32[1,4,256,1024]{3,2,1,0:T(8,128)}), f32[1,4,64,1024]{3,2,1,0:T(8,128)}) %reduce-scatter.16.cloned.1.call-update) | async-done | bytes 1048592 | tf_op jit(solution)/shard_map/reduce_scatter | solution.py:146
  163.4 3.3 constant_dynamic-update-slice_fusion.4
  166.7 3.3 constant_dynamic-update-slice_fusion.3
  170.0 38.0 %all-gather.10.cloned.1.call-done = bf16[1,4,256,1024]{3,2,1,0:T(8,128)(2,1)} async-done(((bf16[1,4,64,1024]{3,2,1,0:T(8,128)(2,1)}), bf16[1,4,256,1024]{3,2,1,0:T(8,128)(2,1)}) %all-gather.10.cloned.1.call-update) | async-done | bytes 2097168 | tf_op jit(solution)/shard_map/all_gather | solution.py:151
  208.1 10.1 %fusion.97 = f32[1024,2304]{1,0:T(8,128)} fusion(bf16[1024,1024]{1,0:T(8,128)(2,1)} %bitcast.212, bf16[1024,2304]{1,0:T(8,128)(2,1)} %constant_dynamic-update-slice_fusion.3), kind=kOutput, calls=%fused_computation.183 | convolution fusion | flops 4831838208 | bytes 16252928 | tf_op jit(solution)/shard_map/dot_general | solution.py:154
  218.1 36.0 %all-gather.18.cloned.1.call-done = bf16[1,4,256,1024]{3,2,1,0:T(8,128)(2,1)} async-done(((bf16[1,4,64,1024]{3,2,1,0:T(8,128)(2,1)}), bf16[1,4,256,1024]{3,2,1,0:T(8,128)(2,1)}) %all-gather.18.cloned.1.call-update) | async-done | bytes 2097168 | tf_op jit(solution)/shard_map/all_gather | solution.py:170
  254.1 30.1 %all-gather.16.cloned.1.call-done = bf16[1152,1024]{1,0:T(8,128)(2,1)} async-done(((bf16[1152,128]{1,0:T(8,128)(2,1)}), bf16[1152,1024]{1,0:T(8,128)(2,1)}) %all-gather.16.cloned.1.call-update) | async-done | bytes 2359312 | tf_op jit(solution)/shard_map/all_gather | solution.py:61
  284.2 10.8 %fusion.7 = (bf16[1024,1152]{1,0:T(8,128)(2,1)S(1)}, bf16[1024,1152]{1,0:T(8,128)(2,1)S(1)}, bf16[1024,1152]{1,0:T(8,128)(2,1)}) fusion(f32[1024,2304]{1,0:T(8,128)} %fusion.97, bf16[1024,1024]{1,0:T(8,128)(2,1)} %bitcast.214, bf16[1152,1024]{1,0:T(8,128)(2,1)} %all-gather.16.cloned.1.call-done), kind=kOutput, calls=%fused_computation.15 | convolution fusion | flops 2434793472 | bytes 20971520 | tf_op jit(solution)/shard_map/gd,fd->gf/dot_general | solution.py:171
  295.0 6.4 fusion.24
  301.5 44.0 %reduce-scatter.20.cloned.1.call-done = bf16[1,4,64,1024]{3,2,1,0:T(8,128)(2,1)} async-done(((bf16[1,4,256,1024]{3,2,1,0:T(8,128)(2,1)}), bf16[1,4,64,1024]{3,2,1,0:T(8,128)(2,1)}) %reduce-scatter.20.cloned.1.call-update) | async-done | bytes 524304 | tf_op jit(solution)/shard_map/reduce_scatter | solution.py:189
  351.1 6.4 convolution_convert_fusion.1
  357.5 4.4 copy.74
  362.1 8.1 %convolution_convert_fusion = bf16[1024,2304]{1,0:T(8,128)(2,1)S(1)} fusion(bf16[1024,1024]{1,0:T(8,128)(2,1)} %bitcast.213, bf16[1024,1152]{1,0:T(8,128)(2,1)} %copy-done.60, bf16[1024,1152]{1,0:T(8,128)(2,1)} %copy-done.59), kind=kOutput, calls=%fused_computation.12 | convolution fusion | flops 4843634688 | bytes 11534336 | tf_op jit(solution)/shard_map/gd,gf->df/dot_general | solution.py:183
  377.5 19.0 %all-gather.20.cloned.1.call-done = bf16[1,4,256,1024]{3,2,1,0:T(8,128)(2,1)} async-done(((bf16[1,4,64,1024]{3,2,1,0:T(8,128)(2,1)}), bf16[1,4,256,1024]{3,2,1,0:T(8,128)(2,1)}) %all-gather.20.cloned.1.call-update) | async-done | bytes 2097168 | tf_op jit(solution)/shard_map/all_gather | solution.py:201
  424.0 4.0 convolution_convert_fusion.3
  428.1 6.7 convolution_convert_fusion.2
  437.0 12.3 %reduce-scatter.30.cloned.1.call-done = bf16[128,1152]{1,0:T(8,128)(2,1)} async-done(((bf16[1024,1152]{1,0:T(8,128)(2,1)}), bf16[128,1152]{1,0:T(8,128)(2,1)}) %reduce-scatter.30.cloned.1.call-update) | async-done | bytes 294928 | tf_op jit(solution)/shard_map/reduce_scatter | solution.py:298
  451.2 44.2 %reduce-scatter.32.cloned.1.call-done = bf16[128,1152]{1,0:T(8,128)(2,1)} async-done(((bf16[1024,1152]{1,0:T(8,128)(2,1)}), bf16[128,1152]{1,0:T(8,128)(2,1)}) %reduce-scatter.32.cloned.1.call-update) | async-done | bytes 294928 | tf_op jit(solution)/shard_map/reduce_scatter | solution.py:301
  497.1 35.0 %reduce-scatter.26.cloned.1.call-done = bf16[128,128]{1,0:T(8,128)(2,1)} async-done(((bf16[1024,128]{1,0:T(8,128)(2,1)}), bf16[128,128]{1,0:T(8,128)(2,1)}) %reduce-scatter.26.cloned.1.call-update) | async-done | bytes 32784 | tf_op jit(solution)/shard_map/reduce_scatter | solution.py:289
  533.5 35.3 %reduce-scatter.28.cloned.1.call-done = bf16[128,128]{1,0:T(8,128)(2,1)} async-done(((bf16[1024,128]{1,0:T(8,128)(2,1)}), bf16[128,128]{1,0:T(8,128)(2,1)}) %reduce-scatter.28.cloned.1.call-update) | async-done | bytes 32784 | tf_op jit(solution)/shard_map/reduce_scatter | solution.py:292
  570.2 36.0 %reduce-scatter.34.cloned.1.call-done = bf16[128,256]{1,0:T(8,128)(2,1)} async-done(((bf16[1024,256]{1,0:T(8,128)(2,1)}), bf16[128,256]{1,0:T(8,128)(2,1)}) %reduce-scatter.34.cloned.1.call-update) | async-done | bytes 65552
  607.9 36.2 %reduce-scatter.24.cloned.1.call-done = bf16[128,256]{1,0:T(8,128)(2,1)} async-done(((bf16[1024,256]{1,0:T(8,128)(2,1)}), bf16[128,256]{1,0:T(8,128)(2,1)}) %reduce-scatter.24.cloned.1.call-update) | async-done | bytes 65552 | tf_op jit(solution)/shard_map/reduce_scatter | solution.py:286
  645.6 44.2 %reduce-scatter.22.cloned.1.call-done = bf16[1,4,64,1024]{3,2,1,0:T(8,128)(2,1)} async-done(((bf16[1,4,256,1024]{3,2,1,0:T(8,128)(2,1)}), bf16[1,4,64,1024]{3,2,1,0:T(8,128)(2,1)}) %reduce-scatter.22.cloned.1.call-update) | async-done | bytes 524304 | tf_op jit(solution)/shard_map/reduce_scatter | solution.py:270
  691.4 42.4 %all-reduce.6 = (f32[1024]{0:T(1024)}, f32[1024]{0:T(1024)}, f32[64]{0:T(128)}, f32[64]{0:T(128)}) all-reduce(f32[1024]{0:T(1024)S(1)} %get-tuple-element.81, f32[1024]{0:T(1024)S(1)} %copy-done.53, f32[64]{0:T(128)S(1)} %get-tuple-element.79, f32[64]{0:T(128)S(1)} %get-tuple-element.83), channel_id=1, replica_groups=mesh['dp'=8,'tensor'=4] {'dp','tensor'}, use_global_device_ids=true, to_apply=%region_21.22 | all-reduce | flops 2176 | bytes 17408 | tf_op jit(solution)/shard_map/psum | solution.py:282
  736.0 2.8 fusion.57
  (259 shorter events, 85.5 us)
Async XLA Ops:
  8.0 52.2 %all-gather.8.cloned.1.call-start = ((), (), s32[]{:S(2)}) async-start(), calls=%async_computation.11 | async-start | bytes 2621440 | tf_op jit(solution)/shard_map/all_gather | solution.py:91
  9.3 43.2 %copy-start.50 = (f32[4,64]{1,0:T(4,128)}, f32[4,64]{1,0:T(4,128)S(1)}, u32[]{:S(2)}) copy-start(f32[4,64]{1,0:T(4,128)S(1)} %fusion.58) | copy-start | bytes 3076
  9.3 43.2 %copy-start.42 = (f32[4,64]{1,0:T(4,128)}, f32[4,64]{1,0:T(4,128)S(1)}, u32[]{:S(2)}) copy-start(f32[4,64]{1,0:T(4,128)S(1)} %fusion.78) | copy-start | bytes 3076
  11.4 146.1 %reduce-scatter.16.cloned.1.call-start = ((), (), s32[]{:S(2)}) async-start(), calls=%async_computation.12 | async-start | bytes 5242880 | tf_op jit(solution)/shard_map/reduce_scatter | solution.py:146
  52.0 26.1 %copy-start.9 = (bf16[256,1024]{1,0:T(8,128)(2,1)}, bf16[256,1024]{1,0:T(8,128)(2,1)S(1)}, u32[]{:S(2)}) copy-start(bf16[256,1024]{1,0:T(8,128)(2,1)S(1)} %all_gather.37) | copy-start | bytes 1572868
  52.6 12.2 %copy-start.4 = (f32[1024,64]{0,1:T(8,128)}, f32[1024,64]{0,1:T(8,128)S(1)}, u32[]{:S(2)}) copy-start(f32[1024,64]{0,1:T(8,128)S(1)} %pad_maximum_fusion.10) | copy-start | bytes 786436
  81.9 81.5 %all-gather.12.cloned.1.call-start = ((), (), s32[]{:S(2)}) async-start(), calls=%async_computation.14 | async-start | bytes 2654208 | tf_op jit(solution)/shard_map/all_gather | solution.py:59
  82.5 84.3 %all-gather.14.cloned.1.call-start = ((), (), s32[]{:S(2)}) async-start(), calls=%async_computation.15 | async-start | bytes 2654208 | tf_op jit(solution)/shard_map/all_gather | solution.py:60
  83.0 125.0 %all-gather.10.cloned.1.call-start = ((), (), s32[]{:S(2)}) async-start(), calls=%async_computation.13 | async-start | bytes 2621440 | tf_op jit(solution)/shard_map/all_gather | solution.py:151
  161.9 92.3 %all-gather.18.cloned.1.call-start = ((), (), s32[]{:S(2)}) async-start(), calls=%async_computation.18 | async-start | bytes 2621440 | tf_op jit(solution)/shard_map/all_gather | solution.py:170
  162.6 121.6 %all-gather.16.cloned.1.call-start = ((), (), s32[]{:S(2)}) async-start(), calls=%async_computation.16 | async-start | bytes 2654208 | tf_op jit(solution)/shard_map/all_gather | solution.py:61
  163.3 182.1 %reduce-scatter.20.cloned.1.call-start = ((), (), s32[]{:S(2)}) async-start(), calls=%async_computation.19 | async-start | bytes 2621440 | tf_op jit(solution)/shard_map/reduce_scatter | solution.py:189
  301.4 95.1 %all-gather.20.cloned.1.call-start = ((), (), s32[]{:S(2)}) async-start(), calls=%async_computation.20 | async-start | bytes 2621440 | tf_op jit(solution)/shard_map/all_gather | solution.py:201
  351.1 83.8 %reduce-scatter.36.cloned.1.call-start = ((), (), s32[]{:S(2)}) async-start(), calls=%async_computation.28 | async-start | bytes 2654208
  361.9 87.5 %reduce-scatter.30.cloned.1.call-start = ((), (), s32[]{:S(2)}) async-start(), calls=%async_computation.25 | async-start | bytes 2654208 | tf_op jit(solution)/shard_map/reduce_scatter | solution.py:298
  372.7 122.6 %reduce-scatter.32.cloned.1.call-start = ((), (), s32[]{:S(2)}) async-start(), calls=%async_computation.26 | async-start | bytes 2654208 | tf_op jit(solution)/shard_map/reduce_scatter | solution.py:301
  377.4 154.7 %reduce-scatter.26.cloned.1.call-start = ((), (), s32[]{:S(2)}) async-start(), calls=%async_computation.23 | async-start | bytes 294912 | tf_op jit(solution)/shard_map/reduce_scatter | solution.py:289
  418.5 150.4 %reduce-scatter.28.cloned.1.call-start = ((), (), s32[]{:S(2)}) async-start(), calls=%async_computation.24 | async-start | bytes 294912 | tf_op jit(solution)/shard_map/reduce_scatter | solution.py:292
  419.2 187.0 %reduce-scatter.34.cloned.1.call-start = ((), (), s32[]{:S(2)}) async-start(), calls=%async_computation.27 | async-start | bytes 589824
  423.0 221.1 %reduce-scatter.24.cloned.1.call-start = ((), (), s32[]{:S(2)}) async-start(), calls=%async_computation.22 | async-start | bytes 589824 | tf_op jit(solution)/shard_map/reduce_scatter | solution.py:286
  423.9 265.9 %reduce-scatter.22.cloned.1.call-start = ((), (), s32[]{:S(2)}) async-start(), calls=%async_computation.21 | async-start | bytes 2621440 | tf_op jit(solution)/shard_map/reduce_scatter | solution.py:270
  428.0 308.0 %reduce-scatter.18.cloned.1.call-start = ((), (), s32[]{:S(2)}) async-start(), calls=%async_computation.17 | async-start | bytes 2621440 | tf_op jit(solution)/shard_map/reduce_scatter | solution.py:160
  434.7 255.1 %copy-start.3 = (bf16[1,4,64,1024]{3,2,1,0:T(8,128)(2,1)S(1)}, bf16[1,4,64,1024]{3,2,1,0:T(8,128)(2,1)}, u32[]{:S(2)}) copy-start(bf16[1,4,64,1024]{3,2,1,0:T(8,128)(2,1)} %param.28) | copy-start | bytes 1572868
  434.7 255.1 %copy-start.41 = (f32[1024]{0:T(1024)S(1)}, f32[1024]{0:T(1024)}, u32[]{:S(2)}) copy-start(f32[1024]{0:T(1024)} %param.33) | copy-start | bytes 12292
  434.7 255.1 %copy-start.43 = (f32[4,64]{1,0:T(4,128)S(1)}, f32[4,64]{1,0:T(4,128)}, u32[]{:S(2)}) copy-start(f32[4,64]{1,0:T(4,128)} %copy-done.42) | copy-start | bytes 3076
  434.7 256.6 %copy-start.53 = (f32[1024]{0:T(1024)S(1)}, f32[1024]{0:T(1024)}, u32[]{:S(2)}) copy-start(f32[1024]{0:T(1024)} %get-tuple-element.77) | copy-start | bytes 12292
  434.7 299.1 %copy-start.51 = (f32[4,64]{1,0:T(4,128)S(1)}, f32[4,64]{1,0:T(4,128)}, u32[]{:S(2)}) copy-start(f32[4,64]{1,0:T(4,128)} %copy-done.50) | copy-start | bytes 3076
  434.8 301.2 %copy-start.6 = (bf16[1,4,64,1024]{3,2,1,0:T(8,128)(2,1)S(1)}, bf16[1,4,64,1024]{3,2,1,0:T(8,128)(2,1)}, u32[]{:S(2)}) copy-start(bf16[1,4,64,1024]{3,2,1,0:T(8,128)(2,1)} %reduce-scatter.20.cloned.1.call-done) | copy-start | bytes 1572868
  434.8 301.2 %copy-start.7 = (bf16[1,4,64,1024]{3,2,1,0:T(8,128)(2,1)S(1)}, bf16[1,4,64,1024]{3,2,1,0:T(8,128)(2,1)}, u32[]{:S(2)}) copy-start(bf16[1,4,64,1024]{3,2,1,0:T(8,128)(2,1)} %param.29) | copy-start | bytes 1572868
  434.8 301.2 %copy-start.38 = (f32[1024]{0:T(1024)S(1)}, f32[1024]{0:T(1024)}, u32[]{:S(2)}) copy-start(f32[1024]{0:T(1024)} %param.34) | copy-start | bytes 12292
  434.8 301.2 %copy-start.40 = (f32[4,64]{1,0:T(4,128)S(1)}, f32[4,64]{1,0:T(4,128)}, u32[]{:S(2)}) copy-start(f32[4,64]{1,0:T(4,128)} %copy-done.39) | copy-start | bytes 3076
  434.8 301.2 %copy-start.49 = (f32[4,64]{1,0:T(4,128)S(1)}, f32[4,64]{1,0:T(4,128)}, u32[]{:S(2)}) copy-start(f32[4,64]{1,0:T(4,128)} %copy-done.48) | copy-start | bytes 3076
  (49 other events, 145.2 us)
Sparse Core Ops, SparseCore 0:
  11.5 48.6 all-gather.7
  82.0 75.4 reduce-scatter.15
  301.6 43.8 reduce-scatter.19
  351.2 45.2 all-gather.19
Sparse Core Ops, SparseCore 1:
  84.2 27.5 all-gather.11
  113.6 28.8 all-gather.13
  161.9 46.1 all-gather.9
  209.7 44.3 all-gather.17
  256.2 27.9 all-gather.15
  362.0 41.7 reduce-scatter.35
  406.9 42.4 reduce-scatter.29
  452.9 42.3 reduce-scatter.31
  498.5 33.6 reduce-scatter.25
  535.2 33.6 reduce-scatter.27
  572.1 34.1 reduce-scatter.33
  609.9 34.1 reduce-scatter.23
  646.4 43.4 reduce-scatter.21
  692.2 43.7 reduce-scatter.17
where the time goes:
time: 751 us; the launch traced here: 746 us
  waiting for transfers between devices  495 us (66%)
  blocking collectives  81.5 us (11%)
  matrix products  79.2 us (11%)
  other arithmetic  41.4 us (6%)
  local copies, waits for them, and re-layouts  30.8 us (4%)
  between operations  16.9 us (2%)
    reduce_scatter x1, waiting for transfers between devices, on_device(): lax.psum_scatter(attn_part.reshape(gathered_shape), 'tensor', scatter_dim...  74 us
    reduce_scatter x1, waiting for transfers between devices, on_device(): lax.psum_scatter(grad_attn_part.reshape(gathered_shape).astype(jnp.bfloat...  44.2 us
    reduce_scatter x1, waiting for transfers between devices, on_device(): lax.psum_scatter(grad_up_w.astype(jnp.bfloat16), 'dp', scatter_dimension=...  44.2 us
    reduce_scatter x1, waiting for transfers between devices, on_device(): lax.psum_scatter(grad_feed_part.reshape(gathered_shape).astype(jnp.bfloat...  44 us
    psum x1, blocking collectives, on_device(): lax.psum((grad_attention_gain, grad_feed_gain, grad_query_gain, grad_key_...  42.4 us
    unnamed x20, waiting for transfers between devices  39.4 us
    all_gather x1, waiting for transfers between devices, on_device(): lax.all_gather(feed_in.reshape(shard_shape), 'tensor', axis=2, tiled=True)  38 us
    reduce_scatter x1, waiting for transfers between devices, on_device(): lax.psum_scatter(grad_query_w.astype(jnp.bfloat16), 'dp', scatter_dimensi...  36.2 us
  transfers between devices with their start and end apart: 18, of which 15 were waited for; matrix products, arithmetic and copies ran while one was open for 13% of the time, Pallas kernels for 0%

commit v1 on v0

v1 whole, which is shorter than its diff:
```python
import jax
import jax.numpy as jnp
from jax import lax
from jax.sharding import PartitionSpec as P

BLOCK = 128
QROWS = 512


EPS = 1e-05
THETA = 1000000.0
NEG = -1e30


def norm_rows(values, gain):
    return values * lax.rsqrt(jnp.mean(values * values, axis=-1, keepdims=True) + EPS) * gain


def norm_pull(values, gain, grad):
    inverse = lax.rsqrt(jnp.mean(values * values, axis=-1, keepdims=True) + EPS)
    scaled = grad * gain
    inner = jnp.mean(values * scaled, axis=-1, keepdims=True)
    grad_values = inverse * scaled - values * (inverse * inverse * inverse * inner)
    return grad_values, jnp.sum(grad * values * inverse, axis=0)


def turn_half(values):
    half = values.shape[-1] // 2
    return jnp.concatenate([-values[..., half:], values[..., :half]], axis=-1)


def rotated(values, gain, cosine, sine):
    normed = norm_rows(values, gain)
    return normed * cosine + turn_half(normed) * sine


def swap(values, axis, bit):
    count = lax.axis_size(axis)
    return lax.ppermute(values, axis, [(index, index ^ bit) for index in range(count)])


def bits_of(count):
    bits = []
    bit = 1
    while bit < count:
        bits.append(bit)
        bit *= 2
    return bits


def dot(left, right):
    return jnp.dot(left, right, preferred_element_type=jnp.float32)


def dot_t(left, right):
    return lax.dot_general(
        left, right, (((1,), (1,)), ((), ())), preferred_element_type=jnp.float32
    )


def dot_tl(left, right):
    return lax.dot_general(
        left, right, (((0,), (0,)), ((), ())), preferred_element_type=jnp.float32
    )


def spread(pieces, axis, bits):
    pieces = dict(pieces)
    for bit in bits:
        for key in sorted(pieces):
            pieces[key | bit] = swap(pieces[key], axis, bit)
    return pieces


def fold(pieces, axis, bits):
    pieces = dict(pieces)
    for bit in bits:
        for key in sorted(pieces, reverse=True):
            if key & bit:
                got = swap(pieces.pop(key).astype(jnp.bfloat16), axis, bit)
                pieces[key ^ bit] = pieces[key ^ bit] + got.astype(jnp.float32)
    return pieces


def place(pieces, index, dim, count):
    first = pieces[0]
    shape = list(first.shape)
    size = shape[dim]
    shape[dim] = size * count
    whole = jnp.zeros(shape, first.dtype)
    for key, block in pieces.items():
        whole = lax.dynamic_update_slice_in_dim(whole, block, (index ^ key) * size, dim)
    return whole


def cut(whole, index, dim, count, keys):
    size = whole.shape[dim] // count
    return {
        key: lax.dynamic_slice_in_dim(whole, (index ^ key) * size, size, dim) for key in keys
    }


def on_device(
    tokens,
    cotangent,
    lengths,
    groups,
    offsets,
    attention_gain,
    feed_gain,
    query_gain,
    key_gain,
    query_weight,
    key_weight,
    value_weight,
    out_weight,
    gate_weight,
    up_weight,
    down_weight,
):
    shard_shape = tokens.shape
    units, unit, width = shard_shape[1:]
    tensor_count = lax.axis_size("tensor")
    dp_count = lax.axis_size("dp")
    tensor_at = lax.axis_index("tensor")
    group = lax.axis_index("dp")
    first_core = (group & 1) == 0
    far = tensor_count // 2
    local_rows = units * unit
    group_rows = local_rows * tensor_count
    head_dim = query_gain.shape[0]
    tensor_bits = bits_of(tensor_count)
    near_bits = tensor_bits[:-1]
    dp_bits = bits_of(dp_count)
    plane_bits = dp_bits[1:]
    plane_back = plane_bits[::-1]
    low = jnp.bfloat16

    def rows_of_group(block):
        pieces = spread({0: block.reshape(units, unit, width)}, "tensor", tensor_bits[::-1])
        return place(pieces, tensor_at, 1, tensor_count).reshape(group_rows, width)

    def sum_to_rows(make):
        pieces = {key: make(key) for key in range(tensor_count - 1, -1, -1)}
        return fold(pieces, "tensor", tensor_bits)[0]

    def group_slice(whole, key):
        cube = whole.reshape(units, unit * tensor_count, whole.shape[-1])
        part = lax.dynamic_slice_in_dim(cube, (tensor_at ^ key) * unit, unit, 1)
        return part.reshape(local_rows, whole.shape[-1])

    def feed_spread(block):
        pieces = spread({0: block}, "tensor", near_bits[::-1])
        both = {2 * key: piece for key, piece in pieces.items()}
        for key in sorted(both):
            both[key | 1] = swap(both[key], "dp", 1)
        return jnp.concatenate([both[key] for key in sorted(both)], axis=0)

    def feed_fold(make):
        pieces = {key: make(key) for key in range(2 * far - 1, -1, -1)}
        pieces = fold(pieces, "dp", [1])
        pieces = {key // 2: piece for key, piece in pieces.items()}
        return fold(pieces, "tensor", near_bits)[0]

    def feed_weight(shard, dim, order):
        other = swap(shard, "tensor", far)
        keep = jnp.where(first_core, shard, other)
        got = swap(jnp.where(first_core, other, shard), "dp", 1)
        pieces = spread({0: keep, 1: got}, "dp", order)
        return place(pieces, group, dim, dp_count)

    def feed_weight_grad(whole, dim, order):
        pieces = cut(whole, group, dim, dp_count, range(dp_count))
        pieces = fold(pieces, "dp", order)
        got = swap(pieces[1].astype(low), "dp", 1).astype(jnp.float32)
        mine = jnp.where(first_core, pieces[0], got)
        away = jnp.where(first_core, got, pieces[0]).astype(low)
        return mine + swap(away, "tensor", far).astype(jnp.float32)

    def plane_weight(shard, dim, order):
        return place(spread({0: shard}, "dp", order + [1]), group, dim, dp_count)

    def plane_weight_grad(whole, dim, order):
        pieces = cut(whole, group, dim, dp_count, range(dp_count))
        return fold(pieces, "dp", [1] + order)[0]

    local_x = tokens.reshape(local_rows, width).astype(jnp.float32)
    attn_rows = rows_of_group(norm_rows(local_x, attention_gain).astype(low))
    query_cols = query_weight.shape[1]
    key_cols = key_weight.shape[1]
    heads = query_cols // head_dim
    value_heads = key_cols // head_dim
    repeat = heads // value_heads
    hidden_cols = gate_weight.shape[1]
    half_hidden = hidden_cols // 2
    project = plane_weight(
        jnp.concatenate([query_weight, key_weight, value_weight], axis=1), 0, plane_bits
    )
    out_full = plane_weight(out_weight, 1, plane_back)
    gate_full = feed_weight(gate_weight, 0, plane_bits)
    up_full = feed_weight(up_weight, 0, plane_back)
    down_full = jnp.concatenate(
        [
            feed_weight(down_weight[:half_hidden], 1, plane_bits),
            feed_weight(down_weight[half_hidden:], 1, plane_back),
        ],
        axis=0,
    )
    local_back = cotangent.reshape(local_rows, width)
    back_rows = feed_spread(local_back)

    position = jnp.arange(group_rows, dtype=jnp.int32)
    start = offsets * BLOCK
    finish = start + lengths
    number = jnp.arange(lengths.shape[0], dtype=jnp.int32)
    inside = (
        (groups[None, :] == group)
        & (position[:, None] >= start[None, :])
        & (position[:, None] < finish[None, :])
    ).astype(jnp.int32)
    segment = jnp.sum(inside * (number + 1)[None, :], axis=1) - 1
    segment = jnp.where(segment >= 0, segment, -1 - position)
    inner_pos = jnp.sum(inside * (position[:, None] - start[None, :]), axis=1)
    freq = THETA ** (-(jnp.arange(head_dim // 2, dtype=jnp.float32) * 2.0) / head_dim)
    angle = inner_pos.astype(jnp.float32)[:, None] * freq[None, :]
    cosine = jnp.concatenate([jnp.cos(angle), jnp.cos(angle)], axis=1)[:, None, :]
    sine = jnp.concatenate([jnp.sin(angle), jnp.sin(angle)], axis=1)[:, None, :]

    projected = dot(attn_rows, project)
    query_pre = projected[:, :query_cols].reshape(group_rows, heads, head_dim)
    key_pre = projected[:, query_cols : query_cols + key_cols].reshape(
        group_rows, value_heads, head_dim
    )
    value_pre = projected[:, query_cols + key_cols :]
    queries = (
        rotated(query_pre, query_gain, cosine, sine)
        .astype(jnp.bfloat16)
        .reshape(group_rows, value_heads, repeat, head_dim)
    )
    keys = rotated(key_pre, key_gain, cosine, sine).astype(jnp.bfloat16)
    values = value_pre.astype(jnp.bfloat16).reshape(group_rows, value_heads, head_dim)
    scale = head_dim ** (-0.5)
    block_count = group_rows // QROWS

    def block_scores(index):
        first = index * QROWS
        last = first + QROWS
        scores = (
            jnp.einsum(
                "qkgd,pkd->kgqp",
                queries[first:last],
                keys[:last],
                preferred_element_type=jnp.float32,
            )
            * scale
        )
        allowed = (segment[first:last, None] == segment[None, :last]) & (
            position[None, :last] <= position[first:last, None]
        )
        return jnp.where(allowed, scores, NEG)

    mixed_parts = []
    log_totals = []
    for index in range(block_count):
        last = (index + 1) * QROWS
        scores = block_scores(index)
        summit = jnp.max(scores, axis=-1, keepdims=True)
        shifted = jnp.exp(scores - summit)
        total = jnp.sum(shifted, axis=-1, keepdims=True)
        attend = (shifted / total).astype(jnp.bfloat16)
        log_totals.append(summit + jnp.log(total))
        mixed_parts.append(
            jnp.einsum("kgqp,pkd->qkgd", attend, values[:last], preferred_element_type=jnp.float32)
        )
    mixed = (
        jnp.concatenate(mixed_parts, axis=0)
        .reshape(group_rows, heads * head_dim)
        .astype(jnp.bfloat16)
    )
    attn_out = sum_to_rows(lambda key: dot(group_slice(mixed, key), out_full))
    middle = local_x + attn_out
    feed_rows = feed_spread(norm_rows(middle, feed_gain).astype(low))
    gate = dot(feed_rows, gate_full)
    up = dot(feed_rows, up_full)
    grad_hidden = dot_t(back_rows, down_full)
    sigmoid = jax.nn.sigmoid(gate)
    silu = gate * sigmoid
    hidden = (silu * up).astype(low)
    grad_gate = (grad_hidden * up * sigmoid * (1.0 + gate * (1.0 - sigmoid))).astype(low)
    grad_up = (grad_hidden * silu).astype(low)

    def block_of(whole, key):
        return lax.slice_in_dim(whole, key * local_rows, (key + 1) * local_rows, axis=0)

    grad_feed_in = feed_fold(
        lambda key: dot_t(block_of(grad_gate, key), gate_full)
        + dot_t(block_of(grad_up, key), up_full)
    )
    feed_out = feed_fold(lambda key: dot(block_of(hidden, key), down_full))
    output = (middle + feed_out).astype(low).reshape(shard_shape)
    grad_middle_norm, grad_feed_gain = norm_pull(middle, feed_gain, grad_feed_in)
    grad_middle = local_back.astype(jnp.float32) + grad_middle_norm
    back_attn = rows_of_group(grad_middle.astype(low))
    grad_gate_w = feed_weight_grad(dot_tl(feed_rows, grad_gate).astype(low), 0, plane_bits)
    grad_up_w = feed_weight_grad(dot_tl(feed_rows, grad_up).astype(low), 0, plane_back)
    grad_down = dot_tl(hidden, back_rows).astype(low)
    grad_down_w = jnp.concatenate(
        [
            feed_weight_grad(grad_down[:half_hidden], 1, plane_bits),
            feed_weight_grad(grad_down[half_hidden:], 1, plane_back),
        ],
        axis=0,
    )
    grad_out_w = plane_weight_grad(dot_tl(mixed, back_attn).astype(low), 1, plane_back)
    grad_mixed = (
        dot_t(back_attn, out_full)
        .astype(low)
        .reshape(group_rows, value_heads, repeat, head_dim)
    )
    grad_keys = jnp.zeros((group_rows, value_heads, head_dim), jnp.float32)
    grad_values = jnp.zeros((group_rows, value_heads, head_dim), jnp.float32)
    query_parts = []
    for index in range(block_count):
        first = index * QROWS
        last = first + QROWS
        scores = block_scores(index)
        attend = jnp.exp(scores - log_totals[index])
        attend_low = attend.astype(jnp.bfloat16)
        grad_here = grad_mixed[first:last]
        grad_values = grad_values.at[:last].add(
            jnp.einsum("kgqp,qkgd->pkd", attend_low, grad_here, preferred_element_type=jnp.float32)
        )
        grad_attend = jnp.einsum(
            "qkgd,pkd->kgqp", grad_here, values[:last], preferred_element_type=jnp.float32
        )
        inner = jnp.sum(attend * grad_attend, axis=-1, keepdims=True)
        grad_scores = (attend * (grad_attend - inner)).astype(jnp.bfloat16)
        query_parts.append(
            jnp.einsum(
                "kgqp,pkd->qkgd", grad_scores, keys[:last], preferred_element_type=jnp.float32
            )
            * scale
        )
        grad_keys = grad_keys.at[:last].add(
            jnp.einsum(
                "kgqp,qkgd->pkd",
                grad_scores,
                queries[first:last],
                preferred_element_type=jnp.float32,
            )
            * scale
        )
    grad_queries = jnp.concatenate(query_parts, axis=0).reshape(group_rows, heads, head_dim)

    def query_side(values_in, gain_in):
        return rotated(values_in, gain_in, cosine, sine)

    _, query_pull = jax.vjp(query_side, query_pre, query_gain)
    grad_query_pre, grad_query_gain = query_pull(grad_queries)
    _, key_pull = jax.vjp(query_side, key_pre, key_gain)
    grad_key_pre, grad_key_gain = key_pull(grad_keys)
    grad_project = jnp.concatenate(
        [
            grad_query_pre.reshape(group_rows, query_cols),
            grad_key_pre.reshape(group_rows, key_cols),
            grad_values.reshape(group_rows, key_cols),
        ],
        axis=1,
    ).astype(jnp.bfloat16)
    grad_project_w = plane_weight_grad(dot_tl(attn_rows, grad_project).astype(low), 0, plane_bits)
    gain_parts = []

    def grad_rows_part(key):
        part = dot_t(group_slice(grad_project, key), project)
        rows = group_slice(attn_rows, key).astype(jnp.float32)
        gain_parts.append(jnp.sum(part * rows, axis=0))
        return part

    grad_attn_in = sum_to_rows(grad_rows_part)
    grad_attention_gain = sum(gain_parts) / attention_gain
    grad_x_norm, _ = norm_pull(local_x, attention_gain, grad_attn_in)
    grad_tokens = (grad_middle + grad_x_norm).astype(low).reshape(shard_shape)
    gains = jnp.concatenate([grad_attention_gain, grad_feed_gain, grad_query_gain, grad_key_gain])
    for axis, bits in (("tensor", tensor_bits), ("dp", dp_bits)):
        for bit in bits:
            gains = gains + swap(gains, axis, bit)
    sizes = (width, width, head_dim, head_dim)
    gain_outs = []
    at = 0
    for size in sizes:
        gain_outs.append(gains[at : at + size])
        at += size
    return (
        output,
        grad_tokens,
        *gain_outs,
        grad_project_w[:, :query_cols],
        grad_project_w[:, query_cols : query_cols + key_cols],
        grad_project_w[:, query_cols + key_cols :],
        grad_out_w,
        grad_gate_w,
        grad_up_w,
        grad_down_w,
    )


def solution(mesh):
    in_specs = (
        P("dp", None, "tensor", None),
        P("dp", None, "tensor", None),
        P(),
        P(),
        P(),
        P(),
        P(),
        P(),
        P(),
        P("dp", "tensor"),
        P("dp", "tensor"),
        P("dp", "tensor"),
        P("tensor", "dp"),
        P("dp", "tensor"),
        P("dp", "tensor"),
        P("tensor", "dp"),
    )
    out_specs = (
        P("dp", None, "tensor", None),
        P("dp", None, "tensor", None),
        P(),
        P(),
        P(),
        P(),
        P("dp", "tensor"),
        P("dp", "tensor"),
        P("dp", "tensor"),
        P("tensor", "dp"),
        P("dp", "tensor"),
        P("dp", "tensor"),
        P("tensor", "dp"),
    )
    return jax.shard_map(
        on_device, mesh=mesh, in_specs=in_specs, out_specs=out_specs, check_vma=False
    )
```

time: 751 us -> 549 us (0.73)
  waiting for transfers between devices: 495 us -> 250 us
  starting transfers between devices: 1.56 us -> 101 us
  blocking collectives: 81.5 us -> 0 us
  local copies, waits for them, and re-layouts: 30.8 us -> 55.8 us
  matrix products: 79.2 us -> 93.9 us
  between operations: 16.9 us -> 3.15 us
    reduce_scatter x9 -> x0, waiting for transfers between devices: 327 us -> none  [the longest x1 74 us: on_device(): lax.psum_scatter(attn_part.reshape(gathered_shape), 'tensor', scatter_dim...]
    ppermute x0 -> x121, waiting for transfers between devices: none -> 250 us  [swap(): lax.ppermute(values, axis, [(index, index ^ bit) for index in range(count)])]
    all_gather x7 -> x0, waiting for transfers between devices: 128 us -> none  [the longest x1 38 us: on_device(): lax.all_gather(feed_in.reshape(shard_shape), 'tensor', axis=2, tiled=True)]
    ppermute x0 -> x121, starting transfers between devices: none -> 101 us  [swap(): lax.ppermute(values, axis, [(index, index ^ bit) for index in range(count)])]
    psum x1 -> x0, blocking collectives: 42.4 us -> none  [on_device(): lax.psum((grad_attention_gain, grad_feed_gain, grad_query_gain, grad_key_...]
    unnamed x20 -> x0, waiting for transfers between devices: 39.4 us -> none
    all_gather x4 -> x0, blocking collectives: 39 us -> none  [the longest x1 11 us: on_device(): lax.all_gather(key_weight, 'dp', axis=0, tiled=True)]
    dynamic_update_slice x0 -> x51, local copies, waits for them, and re-layouts: none -> 15.2 us  [place(): lax.dynamic_update_slice_in_dim(whole, block, (index ^ key) * size, dim)]
  transfers between devices with their start and end apart: 18 -> 121, of which waited for: 15 -> 52; matrix products, arithmetic and copies ran while one was open for 13% -> 24% of each run, Pallas kernels for 0% -> 0%
where the time goes in v1:
time: 549 us; the launch traced here: 543 us
  waiting for transfers between devices  250 us (46%)
  starting transfers between devices  101 us (18%)
  matrix products  93.9 us (17%)
  local copies, waits for them, and re-layouts  55.8 us (10%)
  other arithmetic  40.1 us (7%)
    ppermute x121, waiting for transfers between devices, swap(): lax.ppermute(values, axis, [(index, index ^ bit) for index in range(count)])  250 us
    ppermute x121, starting transfers between devices, swap(): lax.ppermute(values, axis, [(index, index ^ bit) for index in range(count)])  101 us
    dot_general x11, matrix products, dot(): return jnp.dot(left, right, preferred_element_type=jnp.float32)  36.5 us
    dot_general x14, matrix products, dot_t(): lax.dot_general(left, right, (((1,), (1,)), ((), ())), preferred_element_...  29.2 us
    dynamic_update_slice x51, local copies, waits for them, and re-layouts, place(): lax.dynamic_update_slice_in_dim(whole, block, (index ^ key) * size, dim)  15.2 us
    unnamed x182, local copies, waits for them, and re-layouts  14.9 us
    dot_general x5, matrix products, dot_tl(): lax.dot_general(left, right, (((0,), (0,)), ((), ())), preferred_element_...  14.7 us
  transfers between devices with their start and end apart: 121, of which 52 were waited for; matrix products, arithmetic and copies ran while one was open for 24% of the time, Pallas kernels for 0%

profile of v1, /device:TPU:0, one launch (start us, length us, event | category | flops | bytes accessed | tf_op | source)
XLA Modules:
  0.0 543.1 jit_solution(2799142268773610799)
XLA Ops:
  30.9 17.9 %collective-permute-done.39 = bf16[576,128]{1,0:T(8,128)(2,1)S(1)} collective-permute-done((bf16[576,128]{1,0:T(8,128)(2,1)S(1)}, bf16[576,128]{1,0:T(8,128)(2,1)S(1)}, u32[]{:S(2)}, u32[]{:S(2)}) %collective-permute-start.39) | collective-permute-done | bytes 147488 | tf_op jit(solution)/shard_map/ppermute | solution.py:39
  51.5 4.0 collective-permute-start.59
  55.7 11.5 %collective-permute-done.31 = bf16[128,1152]{1,0:T(8,128)(2,1)S(1)} collective-permute-done((bf16[128,1152]{1,0:T(8,128)(2,1)S(1)}, bf16[128,1152]{1,0:T(8,128)(2,1)S(1)}, u32[]{:S(2)}, u32[]{:S(2)}) %collective-permute-start.31) | collective-permute-done | bytes 294944 | tf_op jit(solution)/shard_map/ppermute | solution.py:39
  69.6 13.3 %collective-permute-done.23 = bf16[128,1152]{1,0:T(8,128)(2,1)S(1)} collective-permute-done((bf16[128,1152]{1,0:T(8,128)(2,1)S(1)}, bf16[128,1152]{1,0:T(8,128)(2,1)S(1)}, u32[]{:S(2)}, u32[]{:S(2)}) %collective-permute-start.23) | collective-permute-done | bytes 294944 | tf_op jit(solution)/shard_map/ppermute | solution.py:39
  87.3 3.2 collective-permute-done.41
  99.4 4.3 collective-permute-done.43
  122.2 5.0 collective-permute-done.25
  137.2 4.7 collective-permute-done.54
  146.9 5.5 %collective-permute-done.36 = bf16[128,1152]{1,0:T(8,128)(2,1)S(1)} collective-permute-done((bf16[128,1152]{1,0:T(8,128)(2,1)S(1)}, bf16[128,1152]{1,0:T(8,128)(2,1)S(1)}, u32[]{:S(2)}, u32[]{:S(2)}) %collective-permute-start.36) | collective-permute-done | bytes 294944 | tf_op jit(solution)/shard_map/ppermute | solution.py:39
  185.3 10.3 %collective-permute-done.18 = bf16[256,1024]{1,0:T(8,128)(2,1)} collective-permute-done((bf16[256,1024]{1,0:T(8,128)(2,1)}, bf16[256,1024]{1,0:T(8,128)(2,1)}, u32[]{:S(2)}, u32[]{:S(2)}) %collective-permute-start.18) | collective-permute-done | bytes 524320 | tf_op jit(solution)/shard_map/ppermute | solution.py:39
  209.0 4.9 collective-permute-done.19
  218.0 6.7 %fusion.100 = f32[1024,1152]{1,0:T(8,128)} fusion(bf16[256,1024]{1,0:T(8,128)(2,1)} %collective-permute-done.60, bf16[256,1024]{1,0:T(8,128)(2,1)} %collective-permute-done.59, bf16[256,1024]{1,0:T(8,128)(2,1)} %collective-permute-done.58, bf16[256,1024]{1,0:T(8,128)(2,1)} %bitcast.26, bf16[576,1024]{1,0:T(8,128)(2,1)S(1)} %copy-done.32, ...), kind=kOutput, calls=%fused_computation.184 | convolution fusion | flops 2429026304 | bytes 9175040 | tf_op jit(solution)/shard_map/dot_general | solution.py:56
  230.4 4.5 fusion.119
  235.0 17.8 %multiply_convert_fusion.1 = (bf16[1024,1152]{1,0:T(8,128)(2,1)S(1)}, bf16[1024,1152]{1,0:T(8,128)(2,1)S(1)}, bf16[1024,1152]{1,0:T(8,128)(2,1)S(1)}) fusion(f32[1024,1152]{1,0:T(8,128)} %fusion.100, f32[1024,1152]{1,0:T(8,128)S(1)} %fusion.119, bf16[1024,1152]{1,0:T(8,128)(2,1)S(1)} %constant_dynamic-update-slice_fusion.28, ...), kind=kOutput, calls=%fused_computation.12 | convolution fusion | flops 2442002432 | bytes 20971520 | tf_op jit(solution)/shard_map/dot_general | solution.py:52
  264.7 4.2 convolution_convert_fusion
  279.1 3.6 convolution_convert_fusion.2
  288.3 4.5 collective-permute-done.101
  294.4 4.3 collective-permute-done.98
  307.7 3.3 collective-permute-done.110
  320.3 3.8 collective-permute-done.115
  329.0 8.1 %collective-permute-done.112 = bf16[576,128]{1,0:T(8,128)(2,1)S(1)} collective-permute-done((bf16[576,128]{1,0:T(8,128)(2,1)S(1)}, bf16[576,128]{1,0:T(8,128)(2,1)S(1)}, u32[]{:S(2)}, u32[]{:S(2)}) %collective-permute-start.112) | collective-permute-done | bytes 147488 | tf_op jit(solution)/shard_map/ppermute | solution.py:39
  337.2 8.9 %collective-permute-done.120 = bf16[576,128]{1,0:T(8,128)(2,1)S(1)} collective-permute-done((bf16[576,128]{1,0:T(8,128)(2,1)S(1)}, bf16[576,128]{1,0:T(8,128)(2,1)S(1)}, u32[]{:S(2)}, u32[]{:S(2)}) %collective-permute-start.120) | collective-permute-done | bytes 147488 | tf_op jit(solution)/shard_map/ppermute | solution.py:39
  348.5 6.6 %collective-permute-done.102 = bf16[128,1152]{1,0:T(8,128)(2,1)S(1)} collective-permute-done((bf16[128,1152]{1,0:T(8,128)(2,1)S(1)}, bf16[128,1152]{1,0:T(8,128)(2,1)S(1)}, u32[]{:S(2)}, u32[]{:S(2)}) %collective-permute-start.102) | collective-permute-done | bytes 294944 | tf_op jit(solution)/shard_map/ppermute | solution.py:39
  357.1 6.2 %collective-permute-done.94 = bf16[128,1152]{1,0:T(8,128)(2,1)S(1)} collective-permute-done((bf16[128,1152]{1,0:T(8,128)(2,1)S(1)}, bf16[128,1152]{1,0:T(8,128)(2,1)S(1)}, u32[]{:S(2)}, u32[]{:S(2)}) %collective-permute-start.94) | collective-permute-done | bytes 294944 | tf_op jit(solution)/shard_map/ppermute | solution.py:39
  365.5 7.3 %collective-permute-done.91 = bf16[128,1152]{1,0:T(8,128)(2,1)S(1)} collective-permute-done((bf16[128,1152]{1,0:T(8,128)(2,1)S(1)}, bf16[128,1152]{1,0:T(8,128)(2,1)S(1)}, u32[]{:S(2)}, u32[]{:S(2)}) %collective-permute-start.91) | collective-permute-done | bytes 294944 | tf_op jit(solution)/shard_map/ppermute | solution.py:39
  376.0 15.3 %collective-permute-done.63 = bf16[256,1024]{1,0:T(8,128)(2,1)S(1)} collective-permute-done((bf16[256,1024]{1,0:T(8,128)(2,1)S(1)}, bf16[256,1024]{1,0:T(8,128)(2,1)S(1)}, u32[]{:S(2)}, u32[]{:S(2)}) %collective-permute-start.63) | collective-permute-done | bytes 524320 | tf_op jit(solution)/shard_map/ppermute | solution.py:39
  397.9 4.8 collective-permute-done.57
  405.4 19.1 %collective-permute-done.64 = bf16[4,64,1024]{2,1,0:T(8,128)(2,1)S(1)} collective-permute-done((bf16[4,64,1024]{2,1,0:T(8,128)(2,1)S(1)}, bf16[4,64,1024]{2,1,0:T(8,128)(2,1)S(1)}, u32[]{:S(2)}, u32[]{:S(2)}) %collective-permute-start.64) | collective-permute-done | bytes 524320 | tf_op jit(solution)/shard_map/ppermute | solution.py:39
  425.7 12.7 %collective-permute-done.66 = bf16[4,64,1024]{2,1,0:T(8,128)(2,1)S(1)} collective-permute-done((bf16[4,64,1024]{2,1,0:T(8,128)(2,1)S(1)}, bf16[4,64,1024]{2,1,0:T(8,128)(2,1)S(1)}, u32[]{:S(2)}, u32[]{:S(2)}) %collective-permute-start.66) | collective-permute-done | bytes 524320 | tf_op jit(solution)/shard_map/ppermute | solution.py:39
  485.8 5.0 collective-permute-done.68
  503.7 7.7 %collective-permute-done.67 = bf16[256,1024]{1,0:T(8,128)(2,1)S(1)} collective-permute-done((bf16[256,1024]{1,0:T(8,128)(2,1)S(1)}, bf16[256,1024]{1,0:T(8,128)(2,1)S(1)}, u32[]{:S(2)}, u32[]{:S(2)}) %collective-permute-start.67) | collective-permute-done | bytes 524320 | tf_op jit(solution)/shard_map/ppermute | solution.py:39
  512.5 6.4 %collective-permute-done.69 = bf16[256,1024]{1,0:T(8,128)(2,1)S(1)} collective-permute-done((bf16[256,1024]{1,0:T(8,128)(2,1)S(1)}, bf16[256,1024]{1,0:T(8,128)(2,1)S(1)}, u32[]{:S(2)}, u32[]{:S(2)}) %collective-permute-start.69) | collective-permute-done | bytes 524320 | tf_op jit(solution)/shard_map/ppermute | solution.py:39
  (612 shorter events, 294.3 us)
Async XLA Ops:
  7.5 42.8 %collective-permute-start.6 = (bf16[128,512]{1,0:T(8,128)(2,1)S(1)}, bf16[128,512]{1,0:T(8,128)(2,1)S(1)}, u32[]{:S(2)}, u32[]{:S(2)}) collective-permute-start(bf16[128,512]{1,0:T(8,128)(2,1)S(1)} %constant_dynamic-update-slice_fusion.56), channel_id=1, source_target_pairs={{0,4},{4,0},{8,12},{12,8},{16,20},{20,16},{24,28},{28,24},{1,5},{5... | collective-permute-start | bytes 393224 | tf_op jit(solution)/shard_map/ppermute | solution.py:39
  16.0 94.4 %collective-permute-start = (bf16[4,64,1024]{2,1,0:T(8,128)(2,1)S(1)}, bf16[4,64,1024]{2,1,0:T(8,128)(2,1)S(1)}, u32[]{:S(2)}, u32[]{:S(2)}) collective-permute-start(bf16[4,64,1024]{2,1,0:T(8,128)(2,1)S(1)} %get-tuple-element.98), channel_id=1, source_target_pairs={{0,2},{1,3},{2,0},{3,1},{4,6},{5,7},{6,4},{7,5},{8,10},{9,11},{10,... | collective-permute-start | bytes 1572872 | tf_op jit(solution)/shard_map/ppermute | solution.py:39
  19.2 92.8 %collective-permute-start.1 = (bf16[4,64,1024]{2,1,0:T(8,128)(2,1)S(1)}, bf16[4,64,1024]{2,1,0:T(8,128)(2,1)S(1)}, u32[]{:S(2)}, u32[]{:S(2)}) collective-permute-start(bf16[4,64,1024]{2,1,0:T(8,128)(2,1)S(1)} %get-tuple-element.98), channel_id=1, source_target_pairs={{0,1},{1,0},{2,3},{3,2},{4,5},{5,4},{6,7},{7,6},{8,9},{9,8},{10,11... | collective-permute-start | bytes 1572872 | tf_op jit(solution)/shard_map/ppermute | solution.py:39
  51.5 149.7 %collective-permute-start.59 = (bf16[256,1024]{1,0:T(8,128)(2,1)}, bf16[256,1024]{1,0:T(8,128)(2,1)}, u32[]{:S(2)}, u32[]{:S(2)}) collective-permute-start(bf16[256,1024]{1,0:T(8,128)(2,1)} %bitcast.26), channel_id=1, source_target_pairs={{0,1},{1,0},{2,3},{3,2},{4,5},{5,4},{6,7},{7,6},{8,9},{9,8},{10,11... | collective-permute-start | bytes 1572872 | tf_op jit(solution)/shard_map/ppermute | solution.py:39
  55.6 27.4 %collective-permute-start.23 = (bf16[128,1152]{1,0:T(8,128)(2,1)S(1)}, bf16[128,1152]{1,0:T(8,128)(2,1)S(1)}, u32[]{:S(2)}, u32[]{:S(2)}) collective-permute-start(bf16[128,1152]{1,0:T(8,128)(2,1)S(1)} %copy-done.51), channel_id=1, source_target_pairs={{0,2},{1,3},{2,0},{3,1},{4,6},{5,7},{6,4},{7,5},{8,10},{9,11},{10,... | collective-permute-start | bytes 884744 | tf_op jit(solution)/shard_map/ppermute | solution.py:39
  110.4 35.2 %collective-permute-start.35 = (bf16[128,1152]{1,0:T(8,128)(2,1)S(1)}, bf16[128,1152]{1,0:T(8,128)(2,1)S(1)}, u32[]{:S(2)}, u32[]{:S(2)}) collective-permute-start(bf16[128,1152]{1,0:T(8,128)(2,1)S(1)} %get-tuple-element.96), channel_id=1, source_target_pairs={{0,8},{4,12},{8,0},{12,4},{16,24},{20,28},{24,16},{28,20},{1,9},{5... | collective-permute-start | bytes 884744 | tf_op jit(solution)/shard_map/ppermute | solution.py:39
  136.5 61.3 %collective-permute-start.27 = (bf16[128,1152]{1,0:T(8,128)(2,1)}, bf16[128,1152]{1,0:T(8,128)(2,1)}, u32[]{:S(2)}, u32[]{:S(2)}) collective-permute-start(bf16[128,1152]{1,0:T(8,128)(2,1)} %get-tuple-element.94), channel_id=1, source_target_pairs={{0,16},{4,20},{8,24},{12,28},{16,0},{20,4},{24,8},{28,12},{1,17},{... | collective-permute-start | bytes 884744 | tf_op jit(solution)/shard_map/ppermute | solution.py:39
  145.6 31.4 %collective-permute-start.37 = (bf16[128,1152]{1,0:T(8,128)(2,1)}, bf16[128,1152]{1,0:T(8,128)(2,1)}, u32[]{:S(2)}, u32[]{:S(2)}) collective-permute-start(bf16[128,1152]{1,0:T(8,128)(2,1)} %collective-permute-done.33), channel_id=1, source_target_pairs={{0,8},{4,12},{8,0},{12,4},{16,24},{20,28},{24,16},{28,20},{1,9},{5... | collective-permute-start | bytes 884744 | tf_op jit(solution)/shard_map/ppermute | solution.py:39
  152.4 26.8 %collective-permute-start.26 = (bf16[128,1152]{1,0:T(8,128)(2,1)}, bf16[128,1152]{1,0:T(8,128)(2,1)}, u32[]{:S(2)}, u32[]{:S(2)}) collective-permute-start(bf16[128,1152]{1,0:T(8,128)(2,1)} %collective-permute-done.24), channel_id=1, source_target_pairs={{0,8},{4,12},{8,0},{12,4},{16,24},{20,28},{24,16},{28,20},{1,9},{5... | collective-permute-start | bytes 884744 | tf_op jit(solution)/shard_map/ppermute | solution.py:39
  154.6 46.7 %collective-permute-start.28 = (bf16[128,1152]{1,0:T(8,128)(2,1)}, bf16[128,1152]{1,0:T(8,128)(2,1)}, u32[]{:S(2)}, u32[]{:S(2)}) collective-permute-start(bf16[128,1152]{1,0:T(8,128)(2,1)} %collective-permute-done.24), channel_id=1, source_target_pairs={{0,16},{4,20},{8,24},{12,28},{16,0},{20,4},{24,8},{28,12},{1,17},{... | collective-permute-start | bytes 884744 | tf_op jit(solution)/shard_map/ppermute | solution.py:39
  202.8 25.8 %collective-permute-start.38 = (bf16[128,1152]{1,0:T(8,128)(2,1)}, bf16[128,1152]{1,0:T(8,128)(2,1)}, u32[]{:S(2)}, u32[]{:S(2)}) collective-permute-start(bf16[128,1152]{1,0:T(8,128)(2,1)} %collective-permute-done.34), channel_id=1, source_target_pairs={{0,8},{4,12},{8,0},{12,4},{16,24},{20,28},{24,16},{28,20},{1,9},{5... | collective-permute-start | bytes 884744 | tf_op jit(solution)/shard_map/ppermute | solution.py:39
  271.4 36.3 %collective-permute-start.108 = (bf16[576,128]{1,0:T(8,128)(2,1)S(1)}, bf16[576,128]{1,0:T(8,128)(2,1)S(1)}, u32[]{:S(2)}, u32[]{:S(2)}) collective-permute-start(bf16[576,128]{1,0:T(8,128)(2,1)S(1)} %get-tuple-element.122), channel_id=1, source_target_pairs={{0,8},{4,12},{8,0},{12,4},{16,24},{20,28},{24,16},{28,20},{1,9},{5... | collective-permute-start | bytes 442376 | tf_op jit(solution)/shard_map/ppermute | solution.py:39
  285.0 31.2 %collective-permute-start.105 = (bf16[576,128]{1,0:T(8,128)(2,1)S(1)}, bf16[576,128]{1,0:T(8,128)(2,1)S(1)}, u32[]{:S(2)}, u32[]{:S(2)}) collective-permute-start(bf16[576,128]{1,0:T(8,128)(2,1)S(1)} %get-tuple-element.120), channel_id=1, source_target_pairs={{0,8},{4,12},{8,0},{12,4},{16,24},{20,28},{24,16},{28,20},{1,9},{5... | collective-permute-start | bytes 442376 | tf_op jit(solution)/shard_map/ppermute | solution.py:39
  286.7 26.0 %collective-permute-start.116 = (bf16[576,128]{1,0:T(8,128)(2,1)S(1)}, bf16[576,128]{1,0:T(8,128)(2,1)S(1)}, u32[]{:S(2)}, u32[]{:S(2)}) collective-permute-start(bf16[576,128]{1,0:T(8,128)(2,1)S(1)} %get-tuple-element.128), channel_id=1, source_target_pairs={{0,16},{4,20},{8,24},{12,28},{16,0},{20,4},{24,8},{28,12},{1,17},{... | collective-permute-start | bytes 442376 | tf_op jit(solution)/shard_map/ppermute | solution.py:39
  316.2 32.3 %collective-permute-start.100 = (bf16[128,1152]{1,0:T(8,128)(2,1)S(1)}, bf16[128,1152]{1,0:T(8,128)(2,1)S(1)}, u32[]{:S(2)}, u32[]{:S(2)}) collective-permute-start(bf16[128,1152]{1,0:T(8,128)(2,1)S(1)} %get-tuple-element.106), channel_id=1, source_target_pairs={{0,16},{4,20},{8,24},{12,28},{16,0},{20,4},{24,8},{28,12},{1,17},{... | collective-permute-start | bytes 884744 | tf_op jit(solution)/shard_map/ppermute | solution.py:39
  319.9 43.4 %collective-permute-start.97 = (bf16[128,1152]{1,0:T(8,128)(2,1)S(1)}, bf16[128,1152]{1,0:T(8,128)(2,1)S(1)}, u32[]{:S(2)}, u32[]{:S(2)}) collective-permute-start(bf16[128,1152]{1,0:T(8,128)(2,1)S(1)} %get-tuple-element.104), channel_id=1, source_target_pairs={{0,16},{4,20},{8,24},{12,28},{16,0},{20,4},{24,8},{28,12},{1,17},{... | collective-permute-start | bytes 884744 | tf_op jit(solution)/shard_map/ppermute | solution.py:39
  324.1 31.7 %collective-permute-start.92 = (bf16[128,1152]{1,0:T(8,128)(2,1)S(1)}, bf16[128,1152]{1,0:T(8,128)(2,1)S(1)}, u32[]{:S(2)}, u32[]{:S(2)}) collective-permute-start(bf16[128,1152]{1,0:T(8,128)(2,1)S(1)} %get-tuple-element.112), channel_id=1, source_target_pairs={{0,8},{4,12},{8,0},{12,4},{16,24},{20,28},{24,16},{28,20},{1,9},{5... | collective-permute-start | bytes 884744 | tf_op jit(solution)/shard_map/ppermute | solution.py:39
  325.9 39.2 %collective-permute-start.89 = (bf16[128,1152]{1,0:T(8,128)(2,1)S(1)}, bf16[128,1152]{1,0:T(8,128)(2,1)S(1)}, u32[]{:S(2)}, u32[]{:S(2)}) collective-permute-start(bf16[128,1152]{1,0:T(8,128)(2,1)S(1)} %get-tuple-element.110), channel_id=1, source_target_pairs={{0,8},{4,12},{8,0},{12,4},{16,24},{20,28},{24,16},{28,20},{1,9},{5... | collective-permute-start | bytes 884744 | tf_op jit(solution)/shard_map/ppermute | solution.py:39
  348.5 27.1 %collective-permute-start.61 = (bf16[256,1024]{1,0:T(8,128)(2,1)S(1)}, bf16[256,1024]{1,0:T(8,128)(2,1)S(1)}, u32[]{:S(2)}, u32[]{:S(2)}) collective-permute-start(bf16[256,1024]{1,0:T(8,128)(2,1)S(1)} %fusion.31), channel_id=1, source_target_pairs={{0,4},{4,0},{8,12},{12,8},{16,20},{20,16},{24,28},{28,24},{1,5},{5... | collective-permute-start | bytes 1572872 | tf_op jit(solution)/shard_map/ppermute | solution.py:39
  363.9 27.4 %collective-permute-start.63 = (bf16[256,1024]{1,0:T(8,128)(2,1)S(1)}, bf16[256,1024]{1,0:T(8,128)(2,1)S(1)}, u32[]{:S(2)}, u32[]{:S(2)}) collective-permute-start(bf16[256,1024]{1,0:T(8,128)(2,1)S(1)} %fusion.27), channel_id=1, source_target_pairs={{0,1},{1,0},{2,3},{3,2},{4,5},{5,4},{6,7},{7,6},{8,9},{9,8},{10,11... | collective-permute-start | bytes 1572872 | tf_op jit(solution)/shard_map/ppermute | solution.py:39
  365.1 30.2 %collective-permute-start.55 = (bf16[256,1024]{1,0:T(8,128)(2,1)S(1)}, bf16[256,1024]{1,0:T(8,128)(2,1)S(1)}, u32[]{:S(2)}, u32[]{:S(2)}) collective-permute-start(bf16[256,1024]{1,0:T(8,128)(2,1)S(1)} %convolution_convert_fusion.5), channel_id=1, source_target_pairs={{0,4},{4,0},{8,12},{12,8},{16,20},{20,16},{24,28},{28,24},{1,5},{5... | collective-permute-start | bytes 1572872 | tf_op jit(solution)/shard_map/ppermute | solution.py:39
  372.8 29.8 %collective-permute-start.57 = (bf16[256,1024]{1,0:T(8,128)(2,1)S(1)}, bf16[256,1024]{1,0:T(8,128)(2,1)S(1)}, u32[]{:S(2)}, u32[]{:S(2)}) collective-permute-start(bf16[256,1024]{1,0:T(8,128)(2,1)S(1)} %fusion.30), channel_id=1, source_target_pairs={{0,1},{1,0},{2,3},{3,2},{4,5},{5,4},{6,7},{7,6},{8,9},{9,8},{10,11... | collective-permute-start | bytes 1572872 | tf_op jit(solution)/shard_map/ppermute | solution.py:39
  372.8 31.6 %collective-permute-start.104 = (bf16[128,1152]{1,0:T(8,128)(2,1)S(1)}, bf16[128,1152]{1,0:T(8,128)(2,1)S(1)}, u32[]{:S(2)}, u32[]{:S(2)}) collective-permute-start(bf16[128,1152]{1,0:T(8,128)(2,1)S(1)} %fusion.77), channel_id=1, source_target_pairs={{0,2},{1,3},{2,0},{3,1},{4,6},{5,7},{6,4},{7,5},{8,10},{9,11},{10,... | collective-permute-start | bytes 884744 | tf_op jit(solution)/shard_map/ppermute | solution.py:39
  375.6 49.0 %collective-permute-start.96 = (bf16[128,1152]{1,0:T(8,128)(2,1)S(1)}, bf16[128,1152]{1,0:T(8,128)(2,1)S(1)}, u32[]{:S(2)}, u32[]{:S(2)}) collective-permute-start(bf16[128,1152]{1,0:T(8,128)(2,1)S(1)} %fusion.75), channel_id=1, source_target_pairs={{0,2},{1,3},{2,0},{3,1},{4,6},{5,7},{6,4},{7,5},{8,10},{9,11},{10,... | collective-permute-start | bytes 884744 | tf_op jit(solution)/shard_map/ppermute | solution.py:39
  394.8 29.8 %collective-permute-start.64 = (bf16[4,64,1024]{2,1,0:T(8,128)(2,1)S(1)}, bf16[4,64,1024]{2,1,0:T(8,128)(2,1)S(1)}, u32[]{:S(2)}, u32[]{:S(2)}) collective-permute-start(bf16[4,64,1024]{2,1,0:T(8,128)(2,1)S(1)} %bitcast.247), channel_id=1, source_target_pairs={{0,2},{1,3},{2,0},{3,1},{4,6},{5,7},{6,4},{7,5},{8,10},{9,11},{10,... | collective-permute-start | bytes 1572872 | tf_op jit(solution)/shard_map/ppermute | solution.py:39
  395.3 30.3 %collective-permute-start.65 = (bf16[4,64,1024]{2,1,0:T(8,128)(2,1)S(1)}, bf16[4,64,1024]{2,1,0:T(8,128)(2,1)S(1)}, u32[]{:S(2)}, u32[]{:S(2)}) collective-permute-start(bf16[4,64,1024]{2,1,0:T(8,128)(2,1)S(1)} %bitcast.249), channel_id=1, source_target_pairs={{0,1},{1,0},{2,3},{3,2},{4,5},{5,4},{6,7},{7,6},{8,9},{9,8},{10,11... | collective-permute-start | bytes 1572872 | tf_op jit(solution)/shard_map/ppermute | solution.py:39
  447.2 36.4 %collective-permute-start.83 = (bf16[256,128]{1,0:T(8,128)(2,1)}, bf16[256,128]{1,0:T(8,128)(2,1)}, u32[]{:S(2)}, u32[]{:S(2)}) collective-permute-start(bf16[256,128]{1,0:T(8,128)(2,1)} %get-tuple-element.157), channel_id=1, source_target_pairs={{0,4},{4,0},{8,12},{12,8},{16,20},{20,16},{24,28},{28,24},{1,5},{5... | collective-permute-start | bytes 196616 | tf_op jit(solution)/shard_map/ppermute | solution.py:39
  447.2 36.4 %collective-permute-start.86 = (bf16[256,128]{1,0:T(8,128)(2,1)}, bf16[256,128]{1,0:T(8,128)(2,1)}, u32[]{:S(2)}, u32[]{:S(2)}) collective-permute-start(bf16[256,128]{1,0:T(8,128)(2,1)} %get-tuple-element.155), channel_id=1, source_target_pairs={{0,4},{4,0},{8,12},{12,8},{16,20},{20,16},{24,28},{28,24},{1,5},{5... | collective-permute-start | bytes 196616 | tf_op jit(solution)/shard_map/ppermute | solution.py:39
  447.7 49.4 %collective-permute-start.85 = (bf16[256,128]{1,0:T(8,128)(2,1)}, bf16[256,128]{1,0:T(8,128)(2,1)S(1)}, u32[]{:S(2)}, u32[]{:S(2)}) collective-permute-start(bf16[256,128]{1,0:T(8,128)(2,1)} %get-tuple-element.156), channel_id=1, source_target_pairs={{0,4},{4,0},{8,12},{12,8},{16,20},{20,16},{24,28},{28,24},{1,5},{5... | collective-permute-start | bytes 196616 | tf_op jit(solution)/shard_map/ppermute | solution.py:39
  447.7 75.7 %collective-permute-start.82 = (bf16[256,128]{1,0:T(8,128)(2,1)}, bf16[256,128]{1,0:T(8,128)(2,1)}, u32[]{:S(2)}, u32[]{:S(2)}) collective-permute-start(bf16[256,128]{1,0:T(8,128)(2,1)} %get-tuple-element.154), channel_id=1, source_target_pairs={{0,4},{4,0},{8,12},{12,8},{16,20},{20,16},{24,28},{28,24},{1,5},{5... | collective-permute-start | bytes 196616 | tf_op jit(solution)/shard_map/ppermute | solution.py:39
  494.3 24.6 %collective-permute-start.69 = (bf16[256,1024]{1,0:T(8,128)(2,1)S(1)}, bf16[256,1024]{1,0:T(8,128)(2,1)S(1)}, u32[]{:S(2)}, u32[]{:S(2)}) collective-permute-start(bf16[256,1024]{1,0:T(8,128)(2,1)S(1)} %get-tuple-element.139), channel_id=1, source_target_pairs={{0,2},{1,3},{2,0},{3,1},{4,6},{5,7},{6,4},{7,5},{8,10},{9,11},{10,... | collective-permute-start | bytes 1572872 | tf_op jit(solution)/shard_map/ppermute | solution.py:39
  500.1 27.8 %collective-permute-start.75 = (bf16[128,512]{1,0:T(8,128)(2,1)}, bf16[128,512]{1,0:T(8,128)(2,1)}, u32[]{:S(2)}, u32[]{:S(2)}) collective-permute-start(bf16[128,512]{1,0:T(8,128)(2,1)} %get-tuple-element.132), channel_id=1, source_target_pairs={{0,4},{4,0},{8,12},{12,8},{16,20},{20,16},{24,28},{28,24},{1,5},{5... | collective-permute-start | bytes 393224 | tf_op jit(solution)/shard_map/ppermute | solution.py:39
  (176 other events, 1770.6 us)

commit v2 on v1

--- a/solution.py
+++ b/solution.py
@@ -32,6 +32,10 @@
 def rotated(values, gain, cosine, sine):
     normed = norm_rows(values, gain)
     return normed * cosine + turn_half(normed) * sine
+
+
+def after(values, *others):
+    return lax.optimization_barrier((values, others))[0]
 
 
 def swap(values, axis, bit):
@@ -82,22 +86,21 @@
     return pieces
 
 
-def place(pieces, index, dim, count):
-    first = pieces[0]
-    shape = list(first.shape)
-    size = shape[dim]
-    shape[dim] = size * count
-    whole = jnp.zeros(shape, first.dtype)
-    for key, block in pieces.items():
-        whole = lax.dynamic_update_slice_in_dim(whole, block, (index ^ key) * size, dim)
-    return whole
-
-
-def cut(whole, index, dim, count, keys):
-    size = whole.shape[dim] // count
-    return {
-        key: lax.dynamic_slice_in_dim(whole, (index ^ key) * size, size, dim) for key in keys
-    }
+def widen(values, index, axis, bit):
+    got = swap(values, axis, bit)
+    upper = (index & bit) != 0
+    return jnp.concatenate(
+        [jnp.where(upper, got, values), jnp.where(upper, values, got)], axis=0
+    )
+
+
+def halve(values, index, axis, bit):
+    size = values.shape[0] // 2
+    mine = ((index & bit) != 0).astype(jnp.int32)
+    keep = lax.dynamic_slice_in_dim(values, mine * size, size, 0)
+    send = lax.dynamic_slice_in_dim(values, (1 - mine) * size, size, 0)
+    got = swap(send, axis, bit)
+    return (keep.astype(jnp.float32) + got.astype(jnp.float32)).astype(jnp.bfloat16)
 
 
 def on_device(
@@ -124,7 +127,6 @@
     dp_count = lax.axis_size("dp")
     tensor_at = lax.axis_index("tensor")
     group = lax.axis_index("dp")
-    first_core = (group & 1) == 0
     far = tensor_count // 2
     local_rows = units * unit
     group_rows = local_rows * tensor_count
@@ -132,84 +134,74 @@
     tensor_bits = bits_of(tensor_count)
     near_bits = tensor_bits[:-1]
     dp_bits = bits_of(dp_count)
-    plane_bits = dp_bits[1:]
-    plane_back = plane_bits[::-1]
     low = jnp.bfloat16
-
-    def rows_of_group(block):
-        pieces = spread({0: block.reshape(units, unit, width)}, "tensor", tensor_bits[::-1])
-        return place(pieces, tensor_at, 1, tensor_count).reshape(group_rows, width)
-
-    def sum_to_rows(make):
-        pieces = {key: make(key) for key in range(tensor_count - 1, -1, -1)}
-        return fold(pieces, "tensor", tensor_bits)[0]
-
-    def group_slice(whole, key):
-        cube = whole.reshape(units, unit * tensor_count, whole.shape[-1])
-        part = lax.dynamic_slice_in_dim(cube, (tensor_at ^ key) * unit, unit, 1)
-        return part.reshape(local_rows, whole.shape[-1])
-
-    def feed_spread(block):
-        pieces = spread({0: block}, "tensor", near_bits[::-1])
-        both = {2 * key: piece for key, piece in pieces.items()}
-        for key in sorted(both):
-            both[key | 1] = swap(both[key], "dp", 1)
-        return jnp.concatenate([both[key] for key in sorted(both)], axis=0)
-
-    def feed_fold(make):
-        pieces = {key: make(key) for key in range(2 * far - 1, -1, -1)}
-        pieces = fold(pieces, "dp", [1])
-        pieces = {key // 2: piece for key, piece in pieces.items()}
-        return fold(pieces, "tensor", near_bits)[0]
-
-    def feed_weight(shard, dim, order):
-        other = swap(shard, "tensor", far)
-        keep = jnp.where(first_core, shard, other)
-        got = swap(jnp.where(first_core, other, shard), "dp", 1)
-        pieces = spread({0: keep, 1: got}, "dp", order)
-        return place(pieces, group, dim, dp_count)
-
-    def feed_weight_grad(whole, dim, order):
-        pieces = cut(whole, group, dim, dp_count, range(dp_count))
-        pieces = fold(pieces, "dp", order)
-        got = swap(pieces[1].astype(low), "dp", 1).astype(jnp.float32)
-        mine = jnp.where(first_core, pieces[0], got)
-        away = jnp.where(first_core, got, pieces[0]).astype(low)
-        return mine + swap(away, "tensor", far).astype(jnp.float32)
-
-    def plane_weight(shard, dim, order):
-        return place(spread({0: shard}, "dp", order + [1]), group, dim, dp_count)
-
-    def plane_weight_grad(whole, dim, order):
-        pieces = cut(whole, group, dim, dp_count, range(dp_count))
-        return fold(pieces, "dp", [1] + order)[0]
-
-    local_x = tokens.reshape(local_rows, width).astype(jnp.float32)
-    attn_rows = rows_of_group(norm_rows(local_x, attention_gain).astype(low))
     query_cols = query_weight.shape[1]
     key_cols = key_weight.shape[1]
     heads = query_cols // head_dim
     value_heads = key_cols // head_dim
     repeat = heads // value_heads
     hidden_cols = gate_weight.shape[1]
-    half_hidden = hidden_cols // 2
-    project = plane_weight(
-        jnp.concatenate([query_weight, key_weight, value_weight], axis=1), 0, plane_bits
-    )
-    out_full = plane_weight(out_weight, 1, plane_back)
-    gate_full = feed_weight(gate_weight, 0, plane_bits)
-    up_full = feed_weight(up_weight, 0, plane_back)
-    down_full = jnp.concatenate(
-        [
-            feed_weight(down_weight[:half_hidden], 1, plane_bits),
-            feed_weight(down_weight[half_hidden:], 1, plane_back),
-        ],
-        axis=0,
-    )
+
+    def rows_of_group(block):
+        pieces = spread({0: block.reshape(units, 1, unit, width)}, "tensor", tensor_bits[::-1])
+        whole = jnp.concatenate([pieces[key] for key in range(tensor_count)], axis=1)
+        return whole.reshape(group_rows, width)
+
+    def group_slice(whole, key):
+        cols = whole.shape[-1]
+        part = whole.reshape(units, tensor_count, unit, cols)[:, key]
+        return part.reshape(local_rows, cols)
+
+    def row_blocks(block):
+        pieces = spread({0: block}, "tensor", tensor_bits[::-1])
+        near = jnp.concatenate([pieces[key] for key in range(far)], axis=0)
+        distant = jnp.concatenate([pieces[key] for key in range(far, tensor_count)], axis=0)
+        return near, distant
+
+    def block_of(near, distant, key):
+        half = near if key < far else distant
+        at = (key % far) * local_rows
+        return lax.slice_in_dim(half, at, at + local_rows, axis=0)
+
+    def sum_to_rows(make, between):
+        distant = {key - far: make(key) for key in range(2 * far - 1, far - 1, -1)}
+        distant = fold(distant, "tensor", near_bits)[0]
+        pieces = {key: make(key) for key in range(far - 1, -1, -1)}
+        send = after(distant.astype(low), *between())
+        pieces = {key: after(piece, send) for key, piece in pieces.items()}
+        got = swap(send, "tensor", far).astype(jnp.float32)
+        return fold(pieces, "tensor", near_bits)[0] + got, send
+
+    def whole_weight(shard):
+        return lax.all_gather(shard, "dp", axis=0, tiled=True)
+
+    def weight_grad(whole):
+        return lax.psum_scatter(whole.astype(low), "dp", scatter_dimension=0, tiled=True)
+
+    def in_turn(blocks):
+        picked = [
+            lax.dynamic_index_in_dim(blocks, tensor_at ^ key, 0) for key in range(tensor_count)
+        ]
+        return jnp.concatenate(picked, axis=0)
+
+    local_x = tokens.reshape(local_rows, width).astype(jnp.float32)
+    attn_rows = rows_of_group(norm_rows(local_x, attention_gain).astype(low))
+    attn_pack = jnp.concatenate([query_weight, key_weight, value_weight, out_weight.T], axis=1)
+    for bit in dp_bits:
+        attn_pack = widen(attn_pack, group, "dp", bit)
+    project = attn_pack[:, : query_cols + 2 * key_cols]
+    out_turned = attn_pack[:, query_cols + 2 * key_cols :]
+    feed_pack = whole_weight(jnp.concatenate([gate_weight, up_weight, down_weight.T], axis=1))
+    gate_full = feed_pack[:, :hidden_cols]
+    up_full = feed_pack[:, hidden_cols : 2 * hidden_cols]
+    down_full = feed_pack[:, 2 * hidden_cols :]
     local_back = cotangent.reshape(local_rows, width)
-    back_rows = feed_spread(local_back)
-
-    position = jnp.arange(group_rows, dtype=jnp.int32)
+    back_near, back_far = row_blocks(after(local_back, attn_rows))
+    back_rows = jnp.concatenate([back_near, back_far], axis=0)
+
+    row = jnp.arange(group_rows, dtype=jnp.int32)
+    relative = (row // unit) % tensor_count
+    position = row + ((relative ^ tensor_at) - relative) * unit
     start = offsets * BLOCK
     finish = start + lengths
     number = jnp.arange(lengths.shape[0], dtype=jnp.int32)
@@ -277,50 +269,66 @@
         .reshape(group_rows, heads * head_dim)
         .astype(jnp.bfloat16)
     )
-    attn_out = sum_to_rows(lambda key: dot(group_slice(mixed, key), out_full))
+    mixed = after(mixed, back_near, back_far)
+    attn_out, _ = sum_to_rows(
+        lambda key: dot_t(group_slice(mixed, key), out_turned), lambda: ()
+    )
     middle = local_x + attn_out
-    feed_rows = feed_spread(norm_rows(middle, feed_gain).astype(low))
-    gate = dot(feed_rows, gate_full)
-    up = dot(feed_rows, up_full)
-    grad_hidden = dot_t(back_rows, down_full)
-    sigmoid = jax.nn.sigmoid(gate)
-    silu = gate * sigmoid
-    hidden = (silu * up).astype(low)
-    grad_gate = (grad_hidden * up * sigmoid * (1.0 + gate * (1.0 - sigmoid))).astype(low)
-    grad_up = (grad_hidden * silu).astype(low)
-
-    def block_of(whole, key):
-        return lax.slice_in_dim(whole, key * local_rows, (key + 1) * local_rows, axis=0)
-
-    grad_feed_in = feed_fold(
-        lambda key: dot_t(block_of(grad_gate, key), gate_full)
-        + dot_t(block_of(grad_up, key), up_full)
-    )
-    feed_out = feed_fold(lambda key: dot(block_of(hidden, key), down_full))
-    output = (middle + feed_out).astype(low).reshape(shard_shape)
+    feed_near, feed_far = row_blocks(norm_rows(middle, feed_gain).astype(low))
+
+    def feed(rows, back):
+        gate = dot(rows, gate_full)
+        up = dot(rows, up_full)
+        grad_hidden = dot(back, down_full)
+        sigmoid = jax.nn.sigmoid(gate)
+        silu = gate * sigmoid
+        hidden = (silu * up).astype(low)
+        grad_gate = (grad_hidden * up * sigmoid * (1.0 + gate * (1.0 - sigmoid))).astype(low)
+        grad_up = (grad_hidden * silu).astype(low)
+        return hidden, grad_gate, grad_up
+
+    near_parts = feed(feed_near, back_near)
+    far_parts = feed(after(feed_far, near_parts), back_far)
+
+    def grad_feed_part(key):
+        return dot_t(block_of(near_parts[1], far_parts[1], key), gate_full) + dot_t(
+            block_of(near_parts[2], far_parts[2], key), up_full
+        )
+
+    grad_feed_in, _ = sum_to_rows(grad_feed_part, lambda: ())
+    hidden, grad_gate, grad_up = (
+        jnp.concatenate([one, two], axis=0) for one, two in zip(near_parts, far_parts)
+    )
+    feed_rows = jnp.concatenate([feed_near, feed_far], axis=0)
+    hidden, grad_gate, grad_up = after((hidden, grad_gate, grad_up), grad_feed_in)
+    grad_feed_pack = jnp.concatenate(
+        [
+            dot_tl(feed_rows, grad_gate).astype(low),
+            dot_tl(feed_rows, grad_up).astype(low),
+            dot_tl(back_rows, hidden).astype(low),
+        ],
+        axis=1,
+    )
+    grad_feed_w = weight_grad(grad_feed_pack).astype(jnp.float32)
     grad_middle_norm, grad_feed_gain = norm_pull(middle, feed_gain, grad_feed_in)
     grad_middle = local_back.astype(jnp.float32) + grad_middle_norm
     back_attn = rows_of_group(grad_middle.astype(low))
-    grad_gate_w = feed_weight_grad(dot_tl(feed_rows, grad_gate).astype(low), 0, plane_bits)
-    grad_up_w = feed_weight_grad(dot_tl(feed_rows, grad_up).astype(low), 0, plane_back)
-    grad_down = dot_tl(hidden, back_rows).astype(low)
-    grad_down_w = jnp.concatenate(
-        [
-            feed_weight_grad(grad_down[:half_hidden], 1, plane_bits),
-            feed_weight_grad(grad_down[half_hidden:], 1, plane_back),
-        ],
-        axis=0,
-    )
-    grad_out_w = plane_weight_grad(dot_tl(mixed, back_attn).astype(low), 1, plane_back)
+    feed_part = in_turn(dot_t(hidden, down_full).astype(low).reshape(tensor_count, local_rows, width))
+    back_attn, feed_part = after((back_attn, feed_part), grad_feed_pack)
+    feed_out = lax.psum_scatter(feed_part, "tensor", scatter_dimension=0, tiled=True).reshape(
+        local_rows, width
+    )
+    output = (middle + feed_out.astype(jnp.float32)).astype(low).reshape(shard_shape)
+    grad_out_turned = dot_tl(back_attn, mixed).astype(low)
     grad_mixed = (
-        dot_t(back_attn, out_full)
+        dot(back_attn, out_turned)
         .astype(low)
         .reshape(group_rows, value_heads, repeat, head_dim)
     )
     grad_keys = jnp.zeros((group_rows, value_heads, head_dim), jnp.float32)
     grad_values = jnp.zeros((group_rows, value_heads, head_dim), jnp.float32)
     query_parts = []
-    for index in range(block_count):
+    for index in range(block_count - 1, -1, -1):
         first = index * QROWS
         last = first + QROWS
         scores = block_scores(index)
@@ -350,6 +358,7 @@
             )
             * scale
         )
+    query_parts = query_parts[::-1]
     grad_queries = jnp.concatenate(query_parts, axis=0).reshape(group_rows, heads, head_dim)
 
     def query_side(values_in, gain_in):
@@ -367,23 +376,38 @@
         ],
         axis=1,
     ).astype(jnp.bfloat16)
-    grad_project_w = plane_weight_grad(dot_tl(attn_rows, grad_project).astype(low), 0, plane_bits)
-    gain_parts = []
+    later = {}
 
     def grad_rows_part(key):
         part = dot_t(group_slice(grad_project, key), project)
-        rows = group_slice(attn_rows, key).astype(jnp.float32)
-        gain_parts.append(jnp.sum(part * rows, axis=0))
+        if key == 2 * far - 1:
+            later["project"] = after(grad_project, part)
         return part
 
-    grad_attn_in = sum_to_rows(grad_rows_part)
-    grad_attention_gain = sum(gain_parts) / attention_gain
+    def tail_between():
+        full = dot_tl(attn_rows, later["project"])
+        grad_attention_gain = jnp.sum(full * project.astype(jnp.float32), axis=1) / attention_gain
+        pack = jnp.concatenate([full.astype(low), grad_out_turned], axis=1)
+        gains = jnp.concatenate(
+            [grad_attention_gain, grad_feed_gain, grad_query_gain, grad_key_gain]
+        )
+        for bit in near_bits:
+            gains = gains + swap(gains, "tensor", bit)
+        later["gains"] = gains
+        later["sums"] = halve(pack, group, "dp", dp_bits[-1])
+        return gains, grad_feed_w
+
+    grad_attn_in, attn_sent = sum_to_rows(grad_rows_part, tail_between)
+    gains = after(later["gains"], attn_sent)
+    gains = gains + swap(gains, "tensor", far)
+    for bit in dp_bits[::-1]:
+        gains = gains + swap(gains, "dp", bit)
+    attn_grad = later["sums"]
+    for bit in dp_bits[-2::-1]:
+        attn_grad = halve(attn_grad, group, "dp", bit)
+    grad_attn_in, attn_grad, gains = lax.optimization_barrier((grad_attn_in, attn_grad, gains))
     grad_x_norm, _ = norm_pull(local_x, attention_gain, grad_attn_in)
     grad_tokens = (grad_middle + grad_x_norm).astype(low).reshape(shard_shape)
-    gains = jnp.concatenate([grad_attention_gain, grad_feed_gain, grad_query_gain, grad_key_gain])
-    for axis, bits in (("tensor", tensor_bits), ("dp", dp_bits)):
-        for bit in bits:
-            gains = gains + swap(gains, axis, bit)
     sizes = (width, width, head_dim, head_dim)
     gain_outs = []
     at = 0
@@ -394,13 +418,13 @@
         output,
         grad_tokens,
         *gain_outs,
-        grad_project_w[:, :query_cols],
-        grad_project_w[:, query_cols : query_cols + key_cols],
-        grad_project_w[:, query_cols + key_cols :],
-        grad_out_w,
-        grad_gate_w,
-        grad_up_w,
-        grad_down_w,
+        attn_grad[:, :query_cols].astype(jnp.float32),
+        attn_grad[:, query_cols : query_cols + key_cols].astype(jnp.float32),
+        attn_grad[:, query_cols + key_cols : query_cols + 2 * key_cols].astype(jnp.float32),
+        attn_grad[:, query_cols + 2 * key_cols :].astype(jnp.float32).T,
+        grad_feed_w[:, :hidden_cols],
+        grad_feed_w[:, hidden_cols : 2 * hidden_cols],
+        grad_feed_w[:, 2 * hidden_cols :].T,
     )
 
 

time: 549 us -> 426 us (0.78)
  starting transfers between devices: 101 us -> 37.5 us
  waiting for transfers between devices: 250 us -> 203 us
  matrix products: 93.9 us -> 74.6 us
  local copies, waits for them, and re-layouts: 55.8 us -> 41 us
  between operations: 3.15 us -> 16.1 us
  other arithmetic: 40.1 us -> 49 us
    ppermute x121 -> x32, starting transfers between devices: 101 us -> 37.2 us  [swap(): lax.ppermute(values, axis, [(index, index ^ bit) for index in range(count)])]
    ppermute x121 -> x32, waiting for transfers between devices: 250 us -> 203 us  [swap(): lax.ppermute(values, axis, [(index, index ^ bit) for index in range(count)])]
    dot_general x11 -> x8, matrix products: 36.5 us -> 16.1 us  [dot(): return jnp.dot(left, right, preferred_element_type=jnp.float32)]
    concatenate x1 -> x17, other arithmetic: 0.85 us -> 16.5 us  [the longest x2 3.39 us: rows_of_group(): jnp.concatenate([pieces[key] for key in range(tensor_count)], axis=1)]
    dynamic_update_slice x51 -> x0, local copies, waits for them, and re-layouts: 15.2 us -> none  [place(): lax.dynamic_update_slice_in_dim(whole, block, (index ^ key) * size, dim)]
    dynamic_slice x13 -> x3, local copies, waits for them, and re-layouts: 12 us -> 0.26 us  [the longest x1 0.2 us: in_turn(): lax.dynamic_index_in_dim(blocks, tensor_at ^ key, 0)]
    concatenate x4 -> x6, local copies, waits for them, and re-layouts: 3.37 us -> 12.9 us  [on_device(): jnp.concatenate([grad_query_pre.reshape(group_rows, query_cols), grad_key...]
    dot_general x14 -> x17, matrix products: 29.2 us -> 19.9 us  [dot_t(): lax.dot_general(left, right, (((1,), (1,)), ((), ())), preferred_element_...]
  transfers between devices with their start and end apart: 121 -> 35, of which waited for: 52 -> 21; matrix products, arithmetic and copies ran while one was open for 24% -> 30% of each run, Pallas kernels for 0% -> 0%
where the time goes in v2:
time: 426 us; the launch traced here: 422 us
  waiting for transfers between devices  203 us (48%)
  matrix products  74.6 us (18%)
  other arithmetic  49 us (12%)
  local copies, waits for them, and re-layouts  41 us (10%)
  starting transfers between devices  37.5 us (9%)
  between operations  16.1 us (4%)
    ppermute x32, waiting for transfers between devices, swap(): lax.ppermute(values, axis, [(index, index ^ bit) for index in range(count)])  203 us
    ppermute x32, starting transfers between devices, swap(): lax.ppermute(values, axis, [(index, index ^ bit) for index in range(count)])  37.2 us
    unnamed x214, local copies, waits for them, and re-layouts  20 us
    dot_general x17, matrix products, dot_t(): lax.dot_general(left, right, (((1,), (1,)), ((), ())), preferred_element_...  19.9 us
    dot_general x8, matrix products, dot(): return jnp.dot(left, right, preferred_element_type=jnp.float32)  16.1 us
    dot_general x5, matrix products, dot_tl(): lax.dot_general(left, right, (((0,), (0,)), ((), ())), preferred_element_...  13.7 us
    concatenate x6, local copies, waits for them, and re-layouts, on_device(): jnp.concatenate([grad_query_pre.reshape(group_rows, query_cols), grad_key...  12.9 us
  transfers between devices with their start and end apart: 35, of which 21 were waited for; matrix products, arithmetic and copies ran while one was open for 30% of the time, Pallas kernels for 0%

profile of v2, /device:TPU:0, one launch (start us, length us, event | category | flops | bytes accessed | tf_op | source)
XLA Modules:
  0.0 421.5 jit_solution(11039761368617041367)
XLA Ops:
  9.8 4.1 collective-permute-start.1
  23.3 14.1 %collective-permute-done.1 = bf16[4,1,64,1024]{3,2,1,0:T(8,128)(2,1)} collective-permute-done((bf16[4,1,64,1024]{3,2,1,0:T(8,128)(2,1)S(1)}, bf16[4,1,64,1024]{3,2,1,0:T(8,128)(2,1)}, u32[]{:S(2)}, u32[]{:S(2)}) %collective-permute-start.1) | collective-permute-done | bytes 524320 | tf_op jit(solution)/shard_map/ppermute | solution.py:43
  41.7 8.9 %collective-permute-done.2 = bf16[4,1,64,1024]{3,2,1,0:T(8,128)(2,1)} collective-permute-done((bf16[4,1,64,1024]{3,2,1,0:T(8,128)(2,1)}, bf16[4,1,64,1024]{3,2,1,0:T(8,128)(2,1)}, u32[]{:S(2)}, u32[]{:S(2)}) %collective-permute-start.2) | collective-permute-done | bytes 524320 | tf_op jit(solution)/shard_map/ppermute | solution.py:43
  53.7 3.5 collective-permute-start.7
  57.2 10.3 %collective-permute-done.5 = bf16[512,768]{0,1:T(8,128)(2,1)S(1)} collective-permute-done((bf16[512,768]{0,1:T(8,128)(2,1)S(1)}, bf16[512,768]{0,1:T(8,128)(2,1)S(1)}, u32[]{:S(2)}, u32[]{:S(2)}) %collective-permute-start.5) | collective-permute-done | bytes 786464 | tf_op jit(solution)/shard_map/ppermute | solution.py:43
  83.8 6.9 %collective-permute-done.8 = bf16[256,1024]{1,0:T(8,128)(2,1)S(1)} collective-permute-done((bf16[256,1024]{1,0:T(8,128)(2,1)S(1)}, bf16[256,1024]{1,0:T(8,128)(2,1)S(1)}, u32[]{:S(2)}, u32[]{:S(2)}) %collective-permute-start.8) | collective-permute-done | bytes 524320 | tf_op jit(solution)/shard_map/ppermute | solution.py:43
  99.2 10.8 %collective-permute-done.9 = bf16[256,1024]{1,0:T(8,128)(2,1)S(1)} collective-permute-done((bf16[256,1024]{1,0:T(8,128)(2,1)S(1)}, bf16[256,1024]{1,0:T(8,128)(2,1)S(1)}, u32[]{:S(2)}, u32[]{:S(2)}) %collective-permute-start.9) | collective-permute-done | bytes 524320 | tf_op jit(solution)/shard_map/ppermute | solution.py:43
  112.8 18.4 %collective-permute-done.11 = bf16[256,1024]{1,0:T(8,128)(2,1)S(1)} collective-permute-done((bf16[256,1024]{1,0:T(8,128)(2,1)S(1)}, bf16[256,1024]{1,0:T(8,128)(2,1)S(1)}, u32[]{:S(2)}, u32[]{:S(2)}) %collective-permute-start.11) | collective-permute-done | bytes 524320 | tf_op jit(solution)/shard_map/ppermute | solution.py:43
  135.7 21.3 %collective-permute-done.13 = bf16[256,1024]{1,0:T(8,128)(2,1)} collective-permute-done((bf16[256,1024]{1,0:T(8,128)(2,1)S(1)}, bf16[256,1024]{1,0:T(8,128)(2,1)}, u32[]{:S(2)}, u32[]{:S(2)}) %collective-permute-start.13) | collective-permute-done | bytes 524320 | tf_op jit(solution)/shard_map/ppermute | solution.py:43
  162.1 9.9 %collective-permute-done.14 = bf16[256,1024]{1,0:T(8,128)(2,1)} collective-permute-done((bf16[256,1024]{1,0:T(8,128)(2,1)}, bf16[256,1024]{1,0:T(8,128)(2,1)}, u32[]{:S(2)}, u32[]{:S(2)}) %collective-permute-start.14) | collective-permute-done | bytes 524320 | tf_op jit(solution)/shard_map/ppermute | solution.py:43
  174.4 8.0 %collective-permute-done.12 = bf16[256,1024]{1,0:T(8,128)(2,1)} collective-permute-done((bf16[256,1024]{1,0:T(8,128)(2,1)S(1)}, bf16[256,1024]{1,0:T(8,128)(2,1)}, u32[]{:S(2)}, u32[]{:S(2)}) %collective-permute-start.12) | collective-permute-done | bytes 524320 | tf_op jit(solution)/shard_map/ppermute | solution.py:43
  182.4 3.7 fusion.82
  186.6 2.7 fusion.90
  202.4 9.8 %collective-permute-done.15 = bf16[256,1024]{1,0:T(8,128)(2,1)S(1)} collective-permute-done((bf16[256,1024]{1,0:T(8,128)(2,1)S(1)}, bf16[256,1024]{1,0:T(8,128)(2,1)S(1)}, u32[]{:S(2)}, u32[]{:S(2)}) %collective-permute-start.15) | collective-permute-done | bytes 524320 | tf_op jit(solution)/shard_map/ppermute | solution.py:43
  216.5 20.8 %collective-permute-done.17 = bf16[256,1024]{1,0:T(8,128)(2,1)S(1)} collective-permute-done((bf16[256,1024]{1,0:T(8,128)(2,1)S(1)}, bf16[256,1024]{1,0:T(8,128)(2,1)S(1)}, u32[]{:S(2)}, u32[]{:S(2)}) %collective-permute-start.17) | collective-permute-done | bytes 524320 | tf_op jit(solution)/shard_map/ppermute | solution.py:43
  241.7 3.2 convolution_convert_fusion
  244.9 4.3 %convolution_convert_fusion.1 = bf16[1024,1152]{1,0:T(8,128)(2,1)S(1)} fusion(bf16[1024,1152]{1,0:T(8,128)(2,1)S(1)} %pad_maximum_fusion.3, bf16[256,1024]{1,0:T(8,128)(2,1)} %collective-permute-done.14, bf16[256,1024]{1,0:T(8,128)(2,1)} %collective-permute-done.13, bf16[256,1024]{1,0:T(8,128)(2,1)} %collective-permute-done.12, ...), kind=kOutput, calls=%fused_computation.25 | convolution fusion | flops 2425487360 | bytes 6815744 | tf_op jit(solution)/shard_map/dot_general | solution.py:66
  249.2 4.3 %convolution_convert_fusion.2 = bf16[1024,1152]{1,0:T(8,128)(2,1)S(1)} fusion(bf16[1024,1152]{1,0:T(8,128)(2,1)S(1)} %pad_maximum_fusion.2, bf16[256,1024]{1,0:T(8,128)(2,1)} %collective-permute-done.14, bf16[256,1024]{1,0:T(8,128)(2,1)} %collective-permute-done.13, bf16[256,1024]{1,0:T(8,128)(2,1)} %collective-permute-done.12, ...), kind=kOutput, calls=%fused_computation.26 | convolution fusion | flops 2425487360 | bytes 6815744 | tf_op jit(solution)/shard_map/dot_general | solution.py:66
  253.5 3.3 pad_maximum_fusion
  257.1 6.4 %collective-permute-done.19 = bf16[4,1,64,1024]{3,2,1,0:T(8,128)(2,1)} collective-permute-done((bf16[4,1,64,1024]{3,2,1,0:T(8,128)(2,1)}, bf16[4,1,64,1024]{3,2,1,0:T(8,128)(2,1)}, u32[]{:S(2)}, u32[]{:S(2)}) %collective-permute-start.19) | collective-permute-done | bytes 524320 | tf_op jit(solution)/shard_map/ppermute | solution.py:43
  263.5 6.1 %convolution_convert_fusion.3 = bf16[1024,1024]{1,0:T(8,128)(2,1)S(1)} fusion(bf16[1024,1152]{1,0:T(8,128)(2,1)} %copy-done.26, bf16[1024,3456]{0,1:T(8,128)(2,1)} %all-gather.2.cloned.1.call-done), kind=kOutput, calls=%fused_computation.60 | convolution fusion | flops 2416967680 | bytes 6815744 | tf_op jit(solution)/shard_map/dot_general | solution.py:60
  271.5 6.0 %collective-permute-done.20 = bf16[4,1,64,1024]{3,2,1,0:T(8,128)(2,1)} collective-permute-done((bf16[4,1,64,1024]{3,2,1,0:T(8,128)(2,1)}, bf16[4,1,64,1024]{3,2,1,0:T(8,128)(2,1)}, u32[]{:S(2)}, u32[]{:S(2)}) %collective-permute-start.20) | collective-permute-done | bytes 524320 | tf_op jit(solution)/shard_map/ppermute | solution.py:43
  280.8 5.4 %fusion.5 = f32[2,64,1024,1]{2,1,3,0:T(8,128)S(1)} fusion(bf16[512,2,2,64]{0,3,2,1:T(8,128)(2,1)S(1)} %bitcast.245, f32[2,2,512,1024]{2,3,1,0:T(8,128)} %copy-done, f32[2,2,512]{2,1,0:T(2,128)S(1)} %copy-done.65), kind=kOutput, calls=%fused_computation.12 | convolution fusion | flops 272629760 | bytes 9183232 | tf_op jit(solution)/shard_map/kgqp,qkgd->pkd/dot_general | solution.py:339
  292.0 5.5 %fusion = (f32[2,2,512]{2,1,0:T(2,128)S(1)}, f32[2,1024,512,2]{2,1,3,0:T(8,128)S(1)}) fusion(f32[2,2,512,1024]{2,3,1,0:T(8,128)} %copy-done, f32[2,2,512]{2,1,0:T(2,128)} %log_add_fusion, bf16[1024,2,64,1]{0,2,3,1:T(8,128)(2,1)} %bitcast.259, bf16[512,2,2,64]{0,3,2,1:T(8,128)(2,1)} %bitcast.246), kind=kOutput, calls=%fused_computation.2 | convolution fusion | flops 274724864 | bytes 17317888 | tf_op jit(solution)/shard_map/qkgd,pkd->kgqp/dot_general | solution.py:341
  297.5 5.0 %fusion.2 = bf16[2,2,512,1024]{2,3,1,0:T(8,128)(2,1)S(1)} fusion(f32[2,1024,512,2]{2,1,3,0:T(8,128)S(1)} %get-tuple-element.247, f32[2,2,512,1024]{2,3,1,0:T(8,128)} %copy-done, f32[2,2,512]{2,1,0:T(2,128)S(1)} %get-tuple-element.246, f32[2,2,512]{2,1,0:T(2,128)S(1)} %copy-done.66), kind=kLoop, calls=%fused_computation.4 | loop fusion | flops 8388608 | bytes 20987904 | tf_op jit(solution)/shard_map/convert_element_type | solution.py:345
  317.9 3.1 fusion.38
  324.3 2.6 reshape.496
  338.4 16.0 %collective-permute-done.25 = bf16[512,768]{0,1:T(8,128)(2,1)} collective-permute-done((bf16[512,768]{0,1:T(8,128)(2,1)}, bf16[512,768]{0,1:T(8,128)(2,1)}, u32[]{:S(2)}, u32[]{:S(2)}) %collective-permute-start.25) | collective-permute-done | bytes 786464 | tf_op jit(solution)/shard_map/ppermute | solution.py:43
  360.7 5.2 %collective-permute-done.26 = bf16[256,768]{0,1:T(8,128)(2,1)S(1)} collective-permute-done((bf16[256,768]{0,1:T(8,128)(2,1)S(1)}, bf16[256,768]{0,1:T(8,128)(2,1)S(1)}, u32[]{:S(2)}, u32[]{:S(2)}) %collective-permute-start.26) | collective-permute-done | bytes 393248 | tf_op jit(solution)/shard_map/ppermute | solution.py:43
  369.5 4.7 %collective-permute-done.28 = f32[2176]{0:T(1024)S(1)} collective-permute-done((f32[2176]{0:T(1024)S(1)}, f32[2176]{0:T(1024)S(1)}, u32[]{:S(2)}, u32[]{:S(2)}) %collective-permute-start.28) | collective-permute-done | bytes 8736 | tf_op jit(solution)/shard_map/ppermute | solution.py:43
  382.8 21.7 %collective-permute-done.24 = bf16[256,1024]{1,0:T(8,128)(2,1)} collective-permute-done((bf16[256,1024]{1,0:T(8,128)(2,1)S(1)}, bf16[256,1024]{1,0:T(8,128)(2,1)}, u32[]{:S(2)}, u32[]{:S(2)}) %collective-permute-start.24) | collective-permute-done | bytes 524320 | tf_op jit(solution)/shard_map/ppermute | solution.py:43
  411.7 2.8 fusion.71
  (411 shorter events, 146.7 us)
Async XLA Ops:
  7.2 175.2 %all-gather.2.cloned.1.call-start = ((), (), s32[]{:S(2)}) async-start(), calls=%async_computation.2 | async-start | bytes 7962624 | tf_op jit(solution)/shard_map/all_gather | solution.py:176
  9.8 27.5 %collective-permute-start.1 = (bf16[4,1,64,1024]{3,2,1,0:T(8,128)(2,1)S(1)}, bf16[4,1,64,1024]{3,2,1,0:T(8,128)(2,1)}, u32[]{:S(2)}, u32[]{:S(2)}) collective-permute-start(bf16[4,1,64,1024]{3,2,1,0:T(8,128)(2,1)S(1)} %fusion.66), channel_id=1, source_target_pairs={{0,2},{1,3},{2,0},{3,1},{4,6},{5,7},{6,4},{7,5},{8,10},{9,11},{10,... | collective-permute-start | bytes 1572872 | tf_op jit(solution)/shard_map/ppermute | solution.py:43
  13.9 27.8 %collective-permute-start = (bf16[4,1,64,1024]{3,2,1,0:T(8,128)(2,1)S(1)}, bf16[4,1,64,1024]{3,2,1,0:T(8,128)(2,1)}, u32[]{:S(2)}, u32[]{:S(2)}) collective-permute-start(bf16[4,1,64,1024]{3,2,1,0:T(8,128)(2,1)S(1)} %fusion.66), channel_id=1, source_target_pairs={{0,1},{1,0},{2,3},{3,2},{4,5},{5,4},{6,7},{7,6},{8,9},{9,8},{10,11... | collective-permute-start | bytes 1572872 | tf_op jit(solution)/shard_map/ppermute | solution.py:43
  20.7 345.4 %reduce-scatter.5.cloned.1.call-start = ((), (), s32[]{:S(2)}) async-start(), calls=%async_computation.4 | async-start | bytes 7962624 | tf_op jit(solution)/shard_map/reduce_scatter | solution.py:179
  21.7 16.2 %collective-permute-start.4 = (bf16[256,768]{0,1:T(8,128)(2,1)S(1)}, bf16[256,768]{0,1:T(8,128)(2,1)S(1)}, u32[]{:S(2)}, u32[]{:S(2)}) collective-permute-start(bf16[256,768]{0,1:T(8,128)(2,1)S(1)} %pad_maximum_fusion.19), channel_id=1, source_target_pairs={{0,8},{4,12},{8,0},{12,4},{16,24},{20,28},{24,16},{28,20},{1,9},{5... | collective-permute-start | bytes 1179656 | tf_op jit(solution)/shard_map/ppermute | solution.py:43
  37.3 13.4 %collective-permute-start.2 = (bf16[4,1,64,1024]{3,2,1,0:T(8,128)(2,1)}, bf16[4,1,64,1024]{3,2,1,0:T(8,128)(2,1)}, u32[]{:S(2)}, u32[]{:S(2)}) collective-permute-start(bf16[4,1,64,1024]{3,2,1,0:T(8,128)(2,1)} %collective-permute-done.1), channel_id=1, source_target_pairs={{0,1},{1,0},{2,3},{3,2},{4,5},{5,4},{6,7},{7,6},{8,9},{9,8},{10,11... | collective-permute-start | bytes 1572872 | tf_op jit(solution)/shard_map/ppermute | solution.py:43
  38.1 29.4 %collective-permute-start.5 = (bf16[512,768]{0,1:T(8,128)(2,1)S(1)}, bf16[512,768]{0,1:T(8,128)(2,1)S(1)}, u32[]{:S(2)}, u32[]{:S(2)}) collective-permute-start(bf16[512,768]{0,1:T(8,128)(2,1)S(1)} %pad_maximum_fusion.14), channel_id=1, source_target_pairs={{0,16},{4,20},{8,24},{12,28},{16,0},{20,4},{24,8},{28,12},{1,17},{... | collective-permute-start | bytes 2359304 | tf_op jit(solution)/shard_map/ppermute | solution.py:43
  52.3 30.6 %collective-permute-start.6 = (bf16[256,1024]{1,0:T(8,128)(2,1)S(1)}, bf16[256,1024]{1,0:T(8,128)(2,1)S(1)}, u32[]{:S(2)}, u32[]{:S(2)}) collective-permute-start(bf16[256,1024]{1,0:T(8,128)(2,1)S(1)} %bitcast.235), channel_id=1, source_target_pairs={{0,1},{1,0},{2,3},{3,2},{4,5},{5,4},{6,7},{7,6},{8,9},{9,8},{10,11... | collective-permute-start | bytes 1572872 | tf_op jit(solution)/shard_map/ppermute | solution.py:43
  53.7 26.0 %collective-permute-start.7 = (bf16[256,1024]{1,0:T(8,128)(2,1)S(1)}, bf16[256,1024]{1,0:T(8,128)(2,1)S(1)}, u32[]{:S(2)}, u32[]{:S(2)}) collective-permute-start(bf16[256,1024]{1,0:T(8,128)(2,1)S(1)} %bitcast.236), channel_id=1, source_target_pairs={{0,2},{1,3},{2,0},{3,1},{4,6},{5,7},{6,4},{7,5},{8,10},{9,11},{10,... | collective-permute-start | bytes 1572872 | tf_op jit(solution)/shard_map/ppermute | solution.py:43
  79.7 11.0 %collective-permute-start.8 = (bf16[256,1024]{1,0:T(8,128)(2,1)S(1)}, bf16[256,1024]{1,0:T(8,128)(2,1)S(1)}, u32[]{:S(2)}, u32[]{:S(2)}) collective-permute-start(bf16[256,1024]{1,0:T(8,128)(2,1)S(1)} %collective-permute-done.7), channel_id=1, source_target_pairs={{0,1},{1,0},{2,3},{3,2},{4,5},{5,4},{6,7},{7,6},{8,9},{9,8},{10,11... | collective-permute-start | bytes 1572872 | tf_op jit(solution)/shard_map/ppermute | solution.py:43
  97.1 12.9 %collective-permute-start.9 = (bf16[256,1024]{1,0:T(8,128)(2,1)S(1)}, bf16[256,1024]{1,0:T(8,128)(2,1)S(1)}, u32[]{:S(2)}, u32[]{:S(2)}) collective-permute-start(bf16[256,1024]{1,0:T(8,128)(2,1)S(1)} %convolution_convert_fusion.4), channel_id=1, source_target_pairs={{0,1},{1,0},{2,3},{3,2},{4,5},{5,4},{6,7},{7,6},{8,9},{9,8},{10,11... | collective-permute-start | bytes 1572872 | tf_op jit(solution)/shard_map/ppermute | solution.py:43
  110.3 20.9 %collective-permute-start.11 = (bf16[256,1024]{1,0:T(8,128)(2,1)S(1)}, bf16[256,1024]{1,0:T(8,128)(2,1)S(1)}, u32[]{:S(2)}, u32[]{:S(2)}) collective-permute-start(bf16[256,1024]{1,0:T(8,128)(2,1)S(1)} %fusion.33), channel_id=1, source_target_pairs={{0,2},{1,3},{2,0},{3,1},{4,6},{5,7},{6,4},{7,5},{8,10},{9,11},{10,... | collective-permute-start | bytes 1572872 | tf_op jit(solution)/shard_map/ppermute | solution.py:43
  110.5 20.7 %collective-permute-start.10 = (bf16[256,1024]{1,0:T(8,128)(2,1)S(1)}, bf16[256,1024]{1,0:T(8,128)(2,1)S(1)}, u32[]{:S(2)}, u32[]{:S(2)}) collective-permute-start(bf16[256,1024]{1,0:T(8,128)(2,1)S(1)} %fusion.143), channel_id=1, source_target_pairs={{0,1},{1,0},{2,3},{3,2},{4,5},{5,4},{6,7},{7,6},{8,9},{9,8},{10,11... | collective-permute-start | bytes 1572872 | tf_op jit(solution)/shard_map/ppermute | solution.py:43
  133.5 23.4 %collective-permute-start.13 = (bf16[256,1024]{1,0:T(8,128)(2,1)S(1)}, bf16[256,1024]{1,0:T(8,128)(2,1)}, u32[]{:S(2)}, u32[]{:S(2)}) collective-permute-start(bf16[256,1024]{1,0:T(8,128)(2,1)S(1)} %multiply_convert_fusion.6), channel_id=1, source_target_pairs={{0,2},{1,3},{2,0},{3,1},{4,6},{5,7},{6,4},{7,5},{8,10},{9,11},{10,... | collective-permute-start | bytes 1572872 | tf_op jit(solution)/shard_map/ppermute | solution.py:43
  157.0 15.1 %collective-permute-start.14 = (bf16[256,1024]{1,0:T(8,128)(2,1)}, bf16[256,1024]{1,0:T(8,128)(2,1)}, u32[]{:S(2)}, u32[]{:S(2)}) collective-permute-start(bf16[256,1024]{1,0:T(8,128)(2,1)} %collective-permute-done.13), channel_id=1, source_target_pairs={{0,1},{1,0},{2,3},{3,2},{4,5},{5,4},{6,7},{7,6},{8,9},{9,8},{10,11... | collective-permute-start | bytes 1572872 | tf_op jit(solution)/shard_map/ppermute | solution.py:43
  158.9 23.4 %collective-permute-start.12 = (bf16[256,1024]{1,0:T(8,128)(2,1)S(1)}, bf16[256,1024]{1,0:T(8,128)(2,1)}, u32[]{:S(2)}, u32[]{:S(2)}) collective-permute-start(bf16[256,1024]{1,0:T(8,128)(2,1)S(1)} %copy-done.51), channel_id=1, source_target_pairs={{0,1},{1,0},{2,3},{3,2},{4,5},{5,4},{6,7},{7,6},{8,9},{9,8},{10,11... | collective-permute-start | bytes 1572872 | tf_op jit(solution)/shard_map/ppermute | solution.py:43
  199.1 13.1 %collective-permute-start.15 = (bf16[256,1024]{1,0:T(8,128)(2,1)S(1)}, bf16[256,1024]{1,0:T(8,128)(2,1)S(1)}, u32[]{:S(2)}, u32[]{:S(2)}) collective-permute-start(bf16[256,1024]{1,0:T(8,128)(2,1)S(1)} %fusion.34), channel_id=1, source_target_pairs={{0,1},{1,0},{2,3},{3,2},{4,5},{5,4},{6,7},{7,6},{8,9},{9,8},{10,11... | collective-permute-start | bytes 1572872 | tf_op jit(solution)/shard_map/ppermute | solution.py:43
  213.0 24.3 %collective-permute-start.17 = (bf16[256,1024]{1,0:T(8,128)(2,1)S(1)}, bf16[256,1024]{1,0:T(8,128)(2,1)S(1)}, u32[]{:S(2)}, u32[]{:S(2)}) collective-permute-start(bf16[256,1024]{1,0:T(8,128)(2,1)S(1)} %add_convert_fusion.1), channel_id=1, source_target_pairs={{0,2},{1,3},{2,0},{3,1},{4,6},{5,7},{6,4},{7,5},{8,10},{9,11},{10,... | collective-permute-start | bytes 1572872 | tf_op jit(solution)/shard_map/ppermute | solution.py:43
  213.3 24.0 %collective-permute-start.16 = (bf16[256,1024]{1,0:T(8,128)(2,1)S(1)}, bf16[256,1024]{1,0:T(8,128)(2,1)S(1)}, u32[]{:S(2)}, u32[]{:S(2)}) collective-permute-start(bf16[256,1024]{1,0:T(8,128)(2,1)S(1)} %convolution_add_fusion), channel_id=1, source_target_pairs={{0,1},{1,0},{2,3},{3,2},{4,5},{5,4},{6,7},{7,6},{8,9},{9,8},{10,11... | collective-permute-start | bytes 1572872 | tf_op jit(solution)/shard_map/ppermute | solution.py:43
  239.6 23.8 %collective-permute-start.19 = (bf16[4,1,64,1024]{3,2,1,0:T(8,128)(2,1)}, bf16[4,1,64,1024]{3,2,1,0:T(8,128)(2,1)}, u32[]{:S(2)}, u32[]{:S(2)}) collective-permute-start(bf16[4,1,64,1024]{3,2,1,0:T(8,128)(2,1)} %bitcast.31), channel_id=1, source_target_pairs={{0,2},{1,3},{2,0},{3,1},{4,6},{5,7},{6,4},{7,5},{8,10},{9,11},{10,... | collective-permute-start | bytes 1572872 | tf_op jit(solution)/shard_map/ppermute | solution.py:43
  240.6 30.9 %collective-permute-start.18 = (bf16[4,1,64,1024]{3,2,1,0:T(8,128)(2,1)}, bf16[4,1,64,1024]{3,2,1,0:T(8,128)(2,1)}, u32[]{:S(2)}, u32[]{:S(2)}) collective-permute-start(bf16[4,1,64,1024]{3,2,1,0:T(8,128)(2,1)} %bitcast.31), channel_id=1, source_target_pairs={{0,1},{1,0},{2,3},{3,2},{4,5},{5,4},{6,7},{7,6},{8,9},{9,8},{10,11... | collective-permute-start | bytes 1572872 | tf_op jit(solution)/shard_map/ppermute | solution.py:43
  256.8 154.9 %reduce-scatter.3.cloned.1.call-start = ((), (), s32[]{:S(2)}) async-start(), calls=%async_computation.3 | async-start | bytes 2621440 | tf_op jit(solution)/shard_map/reduce_scatter | solution.py:318
  263.5 14.1 %collective-permute-start.20 = (bf16[4,1,64,1024]{3,2,1,0:T(8,128)(2,1)}, bf16[4,1,64,1024]{3,2,1,0:T(8,128)(2,1)}, u32[]{:S(2)}, u32[]{:S(2)}) collective-permute-start(bf16[4,1,64,1024]{3,2,1,0:T(8,128)(2,1)} %collective-permute-done.19), channel_id=1, source_target_pairs={{0,1},{1,0},{2,3},{3,2},{4,5},{5,4},{6,7},{7,6},{8,9},{9,8},{10,11... | collective-permute-start | bytes 1572872 | tf_op jit(solution)/shard_map/ppermute | solution.py:43
  334.9 19.5 %collective-permute-start.25 = (bf16[512,768]{0,1:T(8,128)(2,1)}, bf16[512,768]{0,1:T(8,128)(2,1)}, u32[]{:S(2)}, u32[]{:S(2)}) collective-permute-start(bf16[512,768]{0,1:T(8,128)(2,1)} %fusion.94), channel_id=1, source_target_pairs={{0,16},{4,20},{8,24},{12,28},{16,0},{20,4},{24,8},{28,12},{1,17},{... | collective-permute-start | bytes 2359304 | tf_op jit(solution)/shard_map/ppermute | solution.py:43
  336.3 22.9 %collective-permute-start.21 = (bf16[256,1024]{1,0:T(8,128)(2,1)}, bf16[256,1024]{1,0:T(8,128)(2,1)}, u32[]{:S(2)}, u32[]{:S(2)}) collective-permute-start(bf16[256,1024]{1,0:T(8,128)(2,1)} %fusion.145), channel_id=1, source_target_pairs={{0,1},{1,0},{2,3},{3,2},{4,5},{5,4},{6,7},{7,6},{8,9},{9,8},{10,11... | collective-permute-start | bytes 1572872 | tf_op jit(solution)/shard_map/ppermute | solution.py:43
  336.7 22.5 %collective-permute-start.22 = (f32[2176]{0:T(1024)S(1)}, f32[2176]{0:T(1024)S(1)}, u32[]{:S(2)}, u32[]{:S(2)}) collective-permute-start(f32[2176]{0:T(1024)S(1)} %concatenate.132), channel_id=1, source_target_pairs={{0,1},{1,0},{2,3},{3,2},{4,5},{5,4},{6,7},{7,6},{8,9},{9,8},{10,11... | collective-permute-start | bytes 26120 | tf_op jit(solution)/shard_map/ppermute | solution.py:43
  355.9 10.0 %collective-permute-start.26 = (bf16[256,768]{0,1:T(8,128)(2,1)S(1)}, bf16[256,768]{0,1:T(8,128)(2,1)S(1)}, u32[]{:S(2)}, u32[]{:S(2)}) collective-permute-start(bf16[256,768]{0,1:T(8,128)(2,1)S(1)} %constant_dynamic-slice_fusion), channel_id=1, source_target_pairs={{0,8},{4,12},{8,0},{12,4},{16,24},{20,28},{24,16},{28,20},{1,9},{5... | collective-permute-start | bytes 1179656 | tf_op jit(solution)/shard_map/ppermute | solution.py:43
  366.0 8.1 %collective-permute-start.27 = (bf16[128,768]{0,1:T(8,128)(2,1)S(1)}, bf16[128,768]{0,1:T(8,128)(2,1)S(1)}, u32[]{:S(2)}, u32[]{:S(2)}) collective-permute-start(bf16[128,768]{0,1:T(8,128)(2,1)S(1)} %constant_dynamic-slice_fusion.5), channel_id=1, source_target_pairs={{0,4},{4,0},{8,12},{12,8},{16,20},{20,16},{24,28},{28,24},{1,5},{5... | collective-permute-start | bytes 589832 | tf_op jit(solution)/shard_map/ppermute | solution.py:43
  367.5 6.6 %collective-permute-start.28 = (f32[2176]{0:T(1024)S(1)}, f32[2176]{0:T(1024)S(1)}, u32[]{:S(2)}, u32[]{:S(2)}) collective-permute-start(f32[2176]{0:T(1024)S(1)} %add.322), channel_id=1, source_target_pairs={{0,2},{1,3},{2,0},{3,1},{4,6},{5,7},{6,4},{7,5},{8,10},{9,11},{10,... | collective-permute-start | bytes 26120 | tf_op jit(solution)/shard_map/ppermute | solution.py:43
  374.1 3.7 collective-permute-start.29
  374.2 30.3 %collective-permute-start.24 = (bf16[256,1024]{1,0:T(8,128)(2,1)S(1)}, bf16[256,1024]{1,0:T(8,128)(2,1)}, u32[]{:S(2)}, u32[]{:S(2)}) collective-permute-start(bf16[256,1024]{1,0:T(8,128)(2,1)S(1)} %fusion.32), channel_id=1, source_target_pairs={{0,2},{1,3},{2,0},{3,1},{4,6},{5,7},{6,4},{7,5},{8,10},{9,11},{10,... | collective-permute-start | bytes 1572872 | tf_op jit(solution)/shard_map/ppermute | solution.py:43
  374.7 30.9 %collective-permute-start.23 = (bf16[256,1024]{1,0:T(8,128)(2,1)S(1)}, bf16[256,1024]{1,0:T(8,128)(2,1)}, u32[]{:S(2)}, u32[]{:S(2)}) collective-permute-start(bf16[256,1024]{1,0:T(8,128)(2,1)S(1)} %fusion.146), channel_id=1, source_target_pairs={{0,1},{1,0},{2,3},{3,2},{4,5},{5,4},{6,7},{7,6},{8,9},{9,8},{10,11... | collective-permute-start | bytes 1572872 | tf_op jit(solution)/shard_map/ppermute | solution.py:43
  (104 other events, 773.0 us)
Sparse Core Ops, SparseCore 0:
  20.8 58.7 all-gather.1
  256.9 64.8 reduce-scatter.4
  338.5 50.5 reduce-scatter.2

commit v3 on v2

--- a/solution.py
+++ b/solution.py
@@ -76,22 +76,22 @@
     return pieces
 
 
-def fold(pieces, axis, bits):
+def fold(pieces, axis, bits, arrived=None):
     pieces = dict(pieces)
     for bit in bits:
         for key in sorted(pieces, reverse=True):
             if key & bit:
                 got = swap(pieces.pop(key).astype(jnp.bfloat16), axis, bit)
+                if arrived is not None:
+                    arrived.append(got)
                 pieces[key ^ bit] = pieces[key ^ bit] + got.astype(jnp.float32)
     return pieces
 
 
-def widen(values, index, axis, bit):
+def widen(values, index, axis, bit, at):
     got = swap(values, axis, bit)
     upper = (index & bit) != 0
-    return jnp.concatenate(
-        [jnp.where(upper, got, values), jnp.where(upper, values, got)], axis=0
-    )
+    return jnp.stack([jnp.where(upper, got, values), jnp.where(upper, values, got)], axis=at)
 
 
 def halve(values, index, axis, bit):
@@ -170,25 +170,23 @@
         send = after(distant.astype(low), *between())
         pieces = {key: after(piece, send) for key, piece in pieces.items()}
         got = swap(send, "tensor", far).astype(jnp.float32)
-        return fold(pieces, "tensor", near_bits)[0] + got, send
+        arrived = []
+        near = fold(pieces, "tensor", near_bits, arrived)[0]
+        return near + got, arrived
 
     def whole_weight(shard):
         return lax.all_gather(shard, "dp", axis=0, tiled=True)
 
     def weight_grad(whole):
         return lax.psum_scatter(whole.astype(low), "dp", scatter_dimension=0, tiled=True)
-
-    def in_turn(blocks):
-        picked = [
-            lax.dynamic_index_in_dim(blocks, tensor_at ^ key, 0) for key in range(tensor_count)
-        ]
-        return jnp.concatenate(picked, axis=0)
 
     local_x = tokens.reshape(local_rows, width).astype(jnp.float32)
     attn_rows = rows_of_group(norm_rows(local_x, attention_gain).astype(low))
     attn_pack = jnp.concatenate([query_weight, key_weight, value_weight, out_weight.T], axis=1)
-    for bit in dp_bits:
-        attn_pack = widen(attn_pack, group, "dp", bit)
+    attn_cols = attn_pack.shape[1]
+    for bit in dp_bits[1:]:
+        attn_pack = widen(attn_pack, group, "dp", bit, 0)
+    attn_pack = widen(attn_pack, group, "dp", 1, attn_pack.ndim - 2).reshape(width, attn_cols)
     project = attn_pack[:, : query_cols + 2 * key_cols]
     out_turned = attn_pack[:, query_cols + 2 * key_cols :]
     feed_pack = whole_weight(jnp.concatenate([gate_weight, up_weight, down_weight.T], axis=1))
@@ -273,6 +271,7 @@
     attn_out, _ = sum_to_rows(
         lambda key: dot_t(group_slice(mixed, key), out_turned), lambda: ()
     )
+    attn_out = after(attn_out, feed_pack)
     middle = local_x + attn_out
     feed_near, feed_far = row_blocks(norm_rows(middle, feed_gain).astype(low))
 
@@ -313,12 +312,7 @@
     grad_middle_norm, grad_feed_gain = norm_pull(middle, feed_gain, grad_feed_in)
     grad_middle = local_back.astype(jnp.float32) + grad_middle_norm
     back_attn = rows_of_group(grad_middle.astype(low))
-    feed_part = in_turn(dot_t(hidden, down_full).astype(low).reshape(tensor_count, local_rows, width))
-    back_attn, feed_part = after((back_attn, feed_part), grad_feed_pack)
-    feed_out = lax.psum_scatter(feed_part, "tensor", scatter_dimension=0, tiled=True).reshape(
-        local_rows, width
-    )
-    output = (middle + feed_out.astype(jnp.float32)).astype(low).reshape(shard_shape)
+    back_attn = after(back_attn, grad_feed_pack)
     grad_out_turned = dot_tl(back_attn, mixed).astype(low)
     grad_mixed = (
         dot(back_attn, out_turned)
@@ -343,6 +337,8 @@
         )
         inner = jnp.sum(attend * grad_attend, axis=-1, keepdims=True)
         grad_scores = (attend * (grad_attend - inner)).astype(jnp.bfloat16)
+        if index == block_count - 1:
+            first_block = grad_scores
         query_parts.append(
             jnp.einsum(
                 "kgqp,pkd->qkgd", grad_scores, keys[:last], preferred_element_type=jnp.float32
@@ -359,6 +355,13 @@
             * scale
         )
     query_parts = query_parts[::-1]
+    feed_out, _ = sum_to_rows(
+        lambda key: dot_t(
+            lax.slice_in_dim(hidden, key * local_rows, (key + 1) * local_rows, axis=0), down_full
+        ),
+        lambda: (first_block,),
+    )
+    output = (middle + feed_out).astype(low).reshape(shard_shape)
     grad_queries = jnp.concatenate(query_parts, axis=0).reshape(group_rows, heads, head_dim)
 
     def query_side(values_in, gain_in):
@@ -376,6 +379,7 @@
         ],
         axis=1,
     ).astype(jnp.bfloat16)
+    grad_project = after(grad_project, output)
     later = {}
 
     def grad_rows_part(key):
@@ -391,21 +395,18 @@
         gains = jnp.concatenate(
             [grad_attention_gain, grad_feed_gain, grad_query_gain, grad_key_gain]
         )
-        for bit in near_bits:
-            gains = gains + swap(gains, "tensor", bit)
         later["gains"] = gains
         later["sums"] = halve(pack, group, "dp", dp_bits[-1])
-        return gains, grad_feed_w
-
-    grad_attn_in, attn_sent = sum_to_rows(grad_rows_part, tail_between)
-    gains = after(later["gains"], attn_sent)
-    gains = gains + swap(gains, "tensor", far)
+        return (grad_feed_w,)
+
+    grad_attn_in, arrived = sum_to_rows(grad_rows_part, tail_between)
+    gains, attn_grad = after((later["gains"], later["sums"]), arrived)
+    for bit in tensor_bits:
+        gains = gains + swap(gains, "tensor", bit)
     for bit in dp_bits[::-1]:
         gains = gains + swap(gains, "dp", bit)
-    attn_grad = later["sums"]
     for bit in dp_bits[-2::-1]:
         attn_grad = halve(attn_grad, group, "dp", bit)
-    grad_attn_in, attn_grad, gains = lax.optimization_barrier((grad_attn_in, attn_grad, gains))
     grad_x_norm, _ = norm_pull(local_x, attention_gain, grad_attn_in)
     grad_tokens = (grad_middle + grad_x_norm).astype(low).reshape(shard_shape)
     sizes = (width, width, head_dim, head_dim)

time: 426 us -> 394 us (0.925)
  waiting for transfers between devices: 203 us -> 156 us
  starting transfers between devices: 37.5 us -> 51.3 us
    ppermute x32 -> x35, waiting for transfers between devices: 203 us -> 156 us  [swap(): lax.ppermute(values, axis, [(index, index ^ bit) for index in range(count)])]
    ppermute x32 -> x35, starting transfers between devices: 37.2 us -> 51.2 us  [swap(): lax.ppermute(values, axis, [(index, index ^ bit) for index in range(count)])]
    concatenate x6 -> x0, local copies, waits for them, and re-layouts: 12.9 us -> none  [on_device(): jnp.concatenate([grad_query_pre.reshape(group_rows, query_cols), grad_key...]
    dot_general x17 -> x20, matrix products: 19.9 us -> 28.9 us  [dot_t(): lax.dot_general(left, right, (((1,), (1,)), ((), ())), preferred_element_...]
    unnamed x214 -> x196, local copies, waits for them, and re-layouts: 20 us -> 18.6 us
  transfers between devices with their start and end apart: 35 -> 37, of which waited for: 21 -> 25; matrix products, arithmetic and copies ran while one was open for 30% -> 35% of each run, Pallas kernels for 0% -> 0%
where the time goes in v3:
time: 394 us; the launch traced here: 387 us
  waiting for transfers between devices  156 us (40%)
  matrix products  77.3 us (20%)
  starting transfers between devices  51.3 us (13%)
  other arithmetic  47.7 us (12%)
  local copies, waits for them, and re-layouts  39.4 us (10%)
  between operations  16 us (4%)
    ppermute x35, waiting for transfers between devices, swap(): lax.ppermute(values, axis, [(index, index ^ bit) for index in range(count)])  156 us
    ppermute x35, starting transfers between devices, swap(): lax.ppermute(values, axis, [(index, index ^ bit) for index in range(count)])  51.2 us
    dot_general x20, matrix products, dot_t(): lax.dot_general(left, right, (((1,), (1,)), ((), ())), preferred_element_...  28.9 us
    dot_general x8, matrix products, dot(): return jnp.dot(left, right, preferred_element_type=jnp.float32)  19.4 us
    unnamed x196, local copies, waits for them, and re-layouts  18.6 us
    dot_general x5, matrix products, dot_tl(): lax.dot_general(left, right, (((0,), (0,)), ((), ())), preferred_element_...  14.4 us
  transfers between devices with their start and end apart: 37, of which 25 were waited for; matrix products, arithmetic and copies ran while one was open for 35% of the time, Pallas kernels for 0%

profile of v3, /device:TPU:0, one launch (start us, length us, event | category | flops | bytes accessed | tf_op | source)
XLA Modules:
  0.0 387.4 jit_solution(9474472576005600061)
XLA Ops:
  9.8 4.1 %collective-permute-start.1 = (bf16[4,1,64,1024]{3,2,1,0:T(8,128)(2,1)S(1)}, bf16[4,1,64,1024]{3,2,1,0:T(8,128)(2,1)}, u32[]{:S(2)}, u32[]{:S(2)}) collective-permute-start(bf16[4,1,64,1024]{3,2,1,0:T(8,128)(2,1)S(1)} %fusion.57), channel_id=1, source_target_pairs={{0,2},{1,3},{2,0},{3,1},{4,6},{5,7},{6,4},{7,5},{8,10},{9,11},{10,... | collective-permute-start | bytes 1572872 | tf_op jit(solution)/shard_map/ppermute | solution.py:43
  27.1 10.3 %collective-permute-done.1 = bf16[4,1,64,1024]{3,2,1,0:T(8,128)(2,1)} collective-permute-done((bf16[4,1,64,1024]{3,2,1,0:T(8,128)(2,1)S(1)}, bf16[4,1,64,1024]{3,2,1,0:T(8,128)(2,1)}, u32[]{:S(2)}, u32[]{:S(2)}) %collective-permute-start.1) | collective-permute-done | bytes 524320 | tf_op jit(solution)/shard_map/ppermute | solution.py:43
  37.8 4.5 %collective-permute-done.4 = bf16[2,128,768]{1,2,0:T(8,128)(2,1)S(1)} collective-permute-done((bf16[2,128,768]{1,2,0:T(8,128)(2,1)S(1)}, bf16[2,128,768]{1,2,0:T(8,128)(2,1)S(1)}, u32[]{:S(2)}, u32[]{:S(2)}) %collective-permute-start.4) | collective-permute-done | bytes 393248 | tf_op jit(solution)/shard_map/ppermute | solution.py:43
  45.0 5.7 %collective-permute-done.2 = bf16[4,1,64,1024]{3,2,1,0:T(8,128)(2,1)} collective-permute-done((bf16[4,1,64,1024]{3,2,1,0:T(8,128)(2,1)}, bf16[4,1,64,1024]{3,2,1,0:T(8,128)(2,1)}, u32[]{:S(2)}, u32[]{:S(2)}) %collective-permute-start.2) | collective-permute-done | bytes 524320 | tf_op jit(solution)/shard_map/ppermute | solution.py:43
  63.5 4.0 %reshape.461 = bf16[1024,768]{0,1:T(8,128)(2,1)} reshape(bf16[2,2,2,128,768]{3,2,1,0,4:T(2,128)(2,1)} %copy.98) | data formatting | bytes 3145728 | tf_op jit(solution)/shard_map/reshape | solution.py:189
  85.7 8.2 %collective-permute-done.8 = bf16[256,1024]{1,0:T(8,128)(2,1)S(1)} collective-permute-done((bf16[256,1024]{1,0:T(8,128)(2,1)}, bf16[256,1024]{1,0:T(8,128)(2,1)S(1)}, u32[]{:S(2)}, u32[]{:S(2)}) %collective-permute-start.8) | collective-permute-done | bytes 524320 | tf_op jit(solution)/shard_map/ppermute | solution.py:43
  98.6 10.6 %collective-permute-done.9 = bf16[256,1024]{1,0:T(8,128)(2,1)S(1)} collective-permute-done((bf16[256,1024]{1,0:T(8,128)(2,1)S(1)}, bf16[256,1024]{1,0:T(8,128)(2,1)S(1)}, u32[]{:S(2)}, u32[]{:S(2)}) %collective-permute-start.9) | collective-permute-done | bytes 524320 | tf_op jit(solution)/shard_map/ppermute | solution.py:43
  110.6 4.1 %collective-permute-start.11 = (bf16[256,1024]{1,0:T(8,128)(2,1)S(1)}, bf16[256,1024]{1,0:T(8,128)(2,1)S(1)}, u32[]{:S(2)}, u32[]{:S(2)}) collective-permute-start(bf16[256,1024]{1,0:T(8,128)(2,1)S(1)} %add_convert_fusion.5), channel_id=1, source_target_pairs={{0,2},{1,3},{2,0},{3,1},{4,6},{5,7},{6,4},{7,5},{8,10},{9,11},{10,... | collective-permute-start | bytes 1572872 | tf_op jit(solution)/shard_map/ppermute | solution.py:43
  115.0 16.5 %collective-permute-done.10 = bf16[256,1024]{1,0:T(8,128)(2,1)S(1)} collective-permute-done((bf16[256,1024]{1,0:T(8,128)(2,1)S(1)}, bf16[256,1024]{1,0:T(8,128)(2,1)S(1)}, u32[]{:S(2)}, u32[]{:S(2)}) %collective-permute-start.10) | collective-permute-done | bytes 524320 | tf_op jit(solution)/shard_map/ppermute | solution.py:43
  135.9 5.4 %collective-permute-start.12 = (bf16[256,1024]{1,0:T(8,128)(2,1)}, bf16[256,1024]{1,0:T(8,128)(2,1)}, u32[]{:S(2)}, u32[]{:S(2)}) collective-permute-start(bf16[256,1024]{1,0:T(8,128)(2,1)} %multiply_convert_fusion.6), channel_id=1, source_target_pairs={{0,1},{1,0},{2,3},{3,2},{4,5},{5,4},{6,7},{7,6},{8,9},{9,8},{10,11... | collective-permute-start | bytes 1572872 | tf_op jit(solution)/shard_map/ppermute | solution.py:43
  148.5 9.1 %collective-permute-done.12 = bf16[256,1024]{1,0:T(8,128)(2,1)} collective-permute-done((bf16[256,1024]{1,0:T(8,128)(2,1)}, bf16[256,1024]{1,0:T(8,128)(2,1)}, u32[]{:S(2)}, u32[]{:S(2)}) %collective-permute-start.12) | collective-permute-done | bytes 524320 | tf_op jit(solution)/shard_map/ppermute | solution.py:43
  157.6 4.0 %fusion.82 = f32[512,1152]{1,0:T(8,128)S(1)} fusion(bf16[1024,3456]{0,1:T(8,128)(2,1)} %all-gather.2.cloned.1.call-done, bf16[256,1024]{1,0:T(8,128)(2,1)} %collective-permute-done.12, bf16[256,1024]{1,0:T(8,128)(2,1)} %multiply_convert_fusion.6), kind=kOutput, calls=%fused_computation.151 | convolution fusion | flops 1210056704 | bytes 5767168 | tf_op jit(solution)/shard_map/dot_general | solution.py:56
  164.4 5.0 %collective-permute-done.13 = bf16[256,1024]{1,0:T(8,128)(2,1)S(1)} collective-permute-done((bf16[256,1024]{1,0:T(8,128)(2,1)}, bf16[256,1024]{1,0:T(8,128)(2,1)S(1)}, u32[]{:S(2)}, u32[]{:S(2)}) %collective-permute-start.13) | collective-permute-done | bytes 524320 | tf_op jit(solution)/shard_map/ppermute | solution.py:43
  175.1 5.5 %collective-permute-done.14 = bf16[256,1024]{1,0:T(8,128)(2,1)S(1)} collective-permute-done((bf16[256,1024]{1,0:T(8,128)(2,1)S(1)}, bf16[256,1024]{1,0:T(8,128)(2,1)S(1)}, u32[]{:S(2)}, u32[]{:S(2)}) %collective-permute-start.14) | collective-permute-done | bytes 524320 | tf_op jit(solution)/shard_map/ppermute | solution.py:43
  189.1 9.0 %collective-permute-done.15 = bf16[256,1024]{1,0:T(8,128)(2,1)S(1)} collective-permute-done((bf16[256,1024]{1,0:T(8,128)(2,1)S(1)}, bf16[256,1024]{1,0:T(8,128)(2,1)S(1)}, u32[]{:S(2)}, u32[]{:S(2)}) %collective-permute-start.15) | collective-permute-done | bytes 524320 | tf_op jit(solution)/shard_map/ppermute | solution.py:43
  202.7 15.7 %collective-permute-done.16 = bf16[256,1024]{1,0:T(8,128)(2,1)S(1)} collective-permute-done((bf16[256,1024]{1,0:T(8,128)(2,1)S(1)}, bf16[256,1024]{1,0:T(8,128)(2,1)S(1)}, u32[]{:S(2)}, u32[]{:S(2)}) %collective-permute-start.16) | collective-permute-done | bytes 524320 | tf_op jit(solution)/shard_map/ppermute | solution.py:43
  227.6 4.1 %convolution_convert_fusion = bf16[1024,1152]{1,0:T(8,128)(2,1)S(1)} fusion(bf16[1024,1152]{1,0:T(8,128)(2,1)S(1)} %pad_maximum_fusion.1, bf16[256,1024]{1,0:T(8,128)(2,1)S(1)} %copy-done.40, bf16[256,1024]{1,0:T(8,128)(2,1)} %collective-permute-done.7, bf16[256,1024]{1,0:T(8,128)(2,1)} %collective-permute-done.6, bf16[256,1024]{1,0:T(8,128)(2,1)S(1)} %bitcast.234), kind=kOutput, calls=%fused_computation.24 | convolution fusion | flops 2425487360 | bytes 6815744 | tf_op jit(solution)/shard_map/dot_general | solution.py:66
  231.7 4.1 %convolution_convert_fusion.2 = bf16[1024,1152]{1,0:T(8,128)(2,1)S(1)} fusion(bf16[1024,1152]{1,0:T(8,128)(2,1)S(1)} %pad_maximum_fusion.2, bf16[256,1024]{1,0:T(8,128)(2,1)S(1)} %collective-permute-done.14, bf16[256,1024]{1,0:T(8,128)(2,1)S(1)} %collective-permute-done.13, bf16[256,1024]{1,0:T(8,128)(2,1)} %collective-permute-done.12, ...), kind=kOutput, calls=%fused_computation.26 | convolution fusion | flops 2425487360 | bytes 6815744 | tf_op jit(solution)/shard_map/dot_general | solution.py:66
  235.9 4.1 %convolution_convert_fusion.1 = bf16[1024,1152]{1,0:T(8,128)(2,1)S(1)} fusion(bf16[1024,1152]{1,0:T(8,128)(2,1)S(1)} %pad_maximum_fusion.3, bf16[256,1024]{1,0:T(8,128)(2,1)S(1)} %collective-permute-done.14, bf16[256,1024]{1,0:T(8,128)(2,1)S(1)} %collective-permute-done.13, bf16[256,1024]{1,0:T(8,128)(2,1)} %collective-permute-done.12, ...), kind=kOutput, calls=%fused_computation.25 | convolution fusion | flops 2425487360 | bytes 6815744 | tf_op jit(solution)/shard_map/dot_general | solution.py:66
  240.0 3.5 pad_maximum_fusion
  243.6 3.9 fusion.68
  249.1 3.4 fusion.63
  252.5 8.9 %collective-permute-done.18 = bf16[256,1024]{1,0:T(8,128)(2,1)} collective-permute-done((bf16[256,1024]{1,0:T(8,128)(2,1)}, bf16[256,1024]{1,0:T(8,128)(2,1)}, u32[]{:S(2)}, u32[]{:S(2)}) %collective-permute-start.18) | collective-permute-done | bytes 524320 | tf_op jit(solution)/shard_map/ppermute | solution.py:43
  261.4 3.6 add_convert_fusion.3
  265.0 6.0 %collective-permute-done.21 = bf16[4,1,64,1024]{3,2,1,0:T(8,128)(2,1)S(1)} collective-permute-done((bf16[4,1,64,1024]{3,2,1,0:T(8,128)(2,1)}, bf16[4,1,64,1024]{3,2,1,0:T(8,128)(2,1)S(1)}, u32[]{:S(2)}, u32[]{:S(2)}) %collective-permute-start.21) | collective-permute-done | bytes 524320 | tf_op jit(solution)/shard_map/ppermute | solution.py:43
  278.5 3.6 fusion.2
  296.5 10.2 %collective-permute-done.22 = bf16[256,1024]{1,0:T(8,128)(2,1)S(1)} collective-permute-done((bf16[256,1024]{1,0:T(8,128)(2,1)}, bf16[256,1024]{1,0:T(8,128)(2,1)S(1)}, u32[]{:S(2)}, u32[]{:S(2)}) %collective-permute-start.22) | collective-permute-done | bytes 524320 | tf_op jit(solution)/shard_map/ppermute | solution.py:43
  323.0 5.1 %collective-permute-done.24 = bf16[256,1024]{1,0:T(8,128)(2,1)} collective-permute-done((bf16[256,1024]{1,0:T(8,128)(2,1)}, bf16[256,1024]{1,0:T(8,128)(2,1)}, u32[]{:S(2)}, u32[]{:S(2)}) %collective-permute-start.24) | collective-permute-done | bytes 524320 | tf_op jit(solution)/shard_map/ppermute | solution.py:43
  332.1 4.9 %collective-permute-done.27 = bf16[512,768]{0,1:T(8,128)(2,1)} collective-permute-done((bf16[512,768]{0,1:T(8,128)(2,1)}, bf16[512,768]{0,1:T(8,128)(2,1)}, u32[]{:S(2)}, u32[]{:S(2)}) %collective-permute-start.27) | collective-permute-done | bytes 786464 | tf_op jit(solution)/shard_map/ppermute | solution.py:43
  343.0 6.1 %collective-permute-done.25 = bf16[256,1024]{1,0:T(8,128)(2,1)S(1)} collective-permute-done((bf16[256,1024]{1,0:T(8,128)(2,1)}, bf16[256,1024]{1,0:T(8,128)(2,1)S(1)}, u32[]{:S(2)}, u32[]{:S(2)}) %collective-permute-start.25) | collective-permute-done | bytes 524320 | tf_op jit(solution)/shard_map/ppermute | solution.py:43
  354.2 3.8 collective-permute-start.29
  360.5 4.3 %collective-permute-done.29 = f32[2176]{0:T(1024)S(1)} collective-permute-done((f32[2176]{0:T(1024)S(1)}, f32[2176]{0:T(1024)S(1)}, u32[]{:S(2)}, u32[]{:S(2)}) %collective-permute-start.29) | collective-permute-done | bytes 8736 | tf_op jit(solution)/shard_map/ppermute | solution.py:43
  (395 shorter events, 170.4 us)
Async XLA Ops:
  7.2 125.6 %all-gather.2.cloned.1.call-start = ((), (), s32[]{:S(2)}) async-start(), calls=%async_computation.1 | async-start | bytes 7962624 | tf_op jit(solution)/shard_map/all_gather | solution.py:178
  9.8 27.5 %collective-permute-start.1 = (bf16[4,1,64,1024]{3,2,1,0:T(8,128)(2,1)S(1)}, bf16[4,1,64,1024]{3,2,1,0:T(8,128)(2,1)}, u32[]{:S(2)}, u32[]{:S(2)}) collective-permute-start(bf16[4,1,64,1024]{3,2,1,0:T(8,128)(2,1)S(1)} %fusion.57), channel_id=1, source_target_pairs={{0,2},{1,3},{2,0},{3,1},{4,6},{5,7},{6,4},{7,5},{8,10},{9,11},{10,... | collective-permute-start | bytes 1572872 | tf_op jit(solution)/shard_map/ppermute | solution.py:43
  13.9 31.1 %collective-permute-start = (bf16[4,1,64,1024]{3,2,1,0:T(8,128)(2,1)S(1)}, bf16[4,1,64,1024]{3,2,1,0:T(8,128)(2,1)}, u32[]{:S(2)}, u32[]{:S(2)}) collective-permute-start(bf16[4,1,64,1024]{3,2,1,0:T(8,128)(2,1)S(1)} %fusion.57), channel_id=1, source_target_pairs={{0,1},{1,0},{2,3},{3,2},{4,5},{5,4},{6,7},{7,6},{8,9},{9,8},{10,11... | collective-permute-start | bytes 1572872 | tf_op jit(solution)/shard_map/ppermute | solution.py:43
  19.1 6.1 %collective-permute-start.3 = (bf16[128,768]{0,1:T(8,128)(2,1)S(1)}, bf16[128,768]{0,1:T(8,128)(2,1)S(1)}, u32[]{:S(2)}, u32[]{:S(2)}) collective-permute-start(bf16[128,768]{0,1:T(8,128)(2,1)S(1)} %pad_maximum_fusion.22), channel_id=1, source_target_pairs={{0,8},{4,12},{8,0},{12,4},{16,24},{20,28},{24,16},{28,20},{1,9},{5... | collective-permute-start | bytes 589832 | tf_op jit(solution)/shard_map/ppermute | solution.py:43
  22.2 308.2 %reduce-scatter.2.cloned.1.call-start = ((), (), s32[]{:S(2)}) async-start(), calls=%async_computation.2 | async-start | bytes 7962624 | tf_op jit(solution)/shard_map/reduce_scatter | solution.py:181
  25.4 16.9 %collective-permute-start.4 = (bf16[2,128,768]{1,2,0:T(8,128)(2,1)S(1)}, bf16[2,128,768]{1,2,0:T(8,128)(2,1)S(1)}, u32[]{:S(2)}, u32[]{:S(2)}) collective-permute-start(bf16[2,128,768]{1,2,0:T(8,128)(2,1)S(1)} %pad_maximum_fusion.17), channel_id=1, source_target_pairs={{0,16},{4,20},{8,24},{12,28},{16,0},{20,4},{24,8},{28,12},{1,17},{... | collective-permute-start | bytes 1179656 | tf_op jit(solution)/shard_map/ppermute | solution.py:43
  37.3 13.4 %collective-permute-start.2 = (bf16[4,1,64,1024]{3,2,1,0:T(8,128)(2,1)}, bf16[4,1,64,1024]{3,2,1,0:T(8,128)(2,1)}, u32[]{:S(2)}, u32[]{:S(2)}) collective-permute-start(bf16[4,1,64,1024]{3,2,1,0:T(8,128)(2,1)} %collective-permute-done.1), channel_id=1, source_target_pairs={{0,1},{1,0},{2,3},{3,2},{4,5},{5,4},{6,7},{7,6},{8,9},{9,8},{10,11... | collective-permute-start | bytes 1572872 | tf_op jit(solution)/shard_map/ppermute | solution.py:43
  42.4 16.9 %collective-permute-start.5 = (bf16[2,2,128,768]{2,3,1,0:T(8,128)(2,1)S(1)}, bf16[2,2,128,768]{2,3,1,0:T(8,128)(2,1)}, u32[]{:S(2)}, u32[]{:S(2)}) collective-permute-start(bf16[2,2,128,768]{2,3,1,0:T(8,128)(2,1)S(1)} %pad_maximum_fusion.13), channel_id=1, source_target_pairs={{0,4},{4,0},{8,12},{12,8},{16,20},{20,16},{24,28},{28,24},{1,5},{5... | collective-permute-start | bytes 2359304 | tf_op jit(solution)/shard_map/ppermute | solution.py:43
  53.7 27.5 %collective-permute-start.7 = (bf16[256,1024]{1,0:T(8,128)(2,1)S(1)}, bf16[256,1024]{1,0:T(8,128)(2,1)}, u32[]{:S(2)}, u32[]{:S(2)}) collective-permute-start(bf16[256,1024]{1,0:T(8,128)(2,1)S(1)} %bitcast.231), channel_id=1, source_target_pairs={{0,2},{1,3},{2,0},{3,1},{4,6},{5,7},{6,4},{7,5},{8,10},{9,11},{10,... | collective-permute-start | bytes 1572872 | tf_op jit(solution)/shard_map/ppermute | solution.py:43
  56.8 27.8 %collective-permute-start.6 = (bf16[256,1024]{1,0:T(8,128)(2,1)S(1)}, bf16[256,1024]{1,0:T(8,128)(2,1)}, u32[]{:S(2)}, u32[]{:S(2)}) collective-permute-start(bf16[256,1024]{1,0:T(8,128)(2,1)S(1)} %bitcast.232), channel_id=1, source_target_pairs={{0,1},{1,0},{2,3},{3,2},{4,5},{5,4},{6,7},{7,6},{8,9},{9,8},{10,11... | collective-permute-start | bytes 1572872 | tf_op jit(solution)/shard_map/ppermute | solution.py:43
  81.2 12.7 %collective-permute-start.8 = (bf16[256,1024]{1,0:T(8,128)(2,1)}, bf16[256,1024]{1,0:T(8,128)(2,1)S(1)}, u32[]{:S(2)}, u32[]{:S(2)}) collective-permute-start(bf16[256,1024]{1,0:T(8,128)(2,1)} %collective-permute-done.7), channel_id=1, source_target_pairs={{0,1},{1,0},{2,3},{3,2},{4,5},{5,4},{6,7},{7,6},{8,9},{9,8},{10,11... | collective-permute-start | bytes 1572872 | tf_op jit(solution)/shard_map/ppermute | solution.py:43
  97.4 11.8 %collective-permute-start.9 = (bf16[256,1024]{1,0:T(8,128)(2,1)S(1)}, bf16[256,1024]{1,0:T(8,128)(2,1)S(1)}, u32[]{:S(2)}, u32[]{:S(2)}) collective-permute-start(bf16[256,1024]{1,0:T(8,128)(2,1)S(1)} %convolution_convert_fusion.4), channel_id=1, source_target_pairs={{0,1},{1,0},{2,3},{3,2},{4,5},{5,4},{6,7},{7,6},{8,9},{9,8},{10,11... | collective-permute-start | bytes 1572872 | tf_op jit(solution)/shard_map/ppermute | solution.py:43
  109.5 22.0 %collective-permute-start.10 = (bf16[256,1024]{1,0:T(8,128)(2,1)S(1)}, bf16[256,1024]{1,0:T(8,128)(2,1)S(1)}, u32[]{:S(2)}, u32[]{:S(2)}) collective-permute-start(bf16[256,1024]{1,0:T(8,128)(2,1)S(1)} %fusion.128), channel_id=1, source_target_pairs={{0,1},{1,0},{2,3},{3,2},{4,5},{5,4},{6,7},{7,6},{8,9},{9,8},{10,11... | collective-permute-start | bytes 1572872 | tf_op jit(solution)/shard_map/ppermute | solution.py:43
  110.6 20.9 %collective-permute-start.11 = (bf16[256,1024]{1,0:T(8,128)(2,1)S(1)}, bf16[256,1024]{1,0:T(8,128)(2,1)S(1)}, u32[]{:S(2)}, u32[]{:S(2)}) collective-permute-start(bf16[256,1024]{1,0:T(8,128)(2,1)S(1)} %add_convert_fusion.5), channel_id=1, source_target_pairs={{0,2},{1,3},{2,0},{3,1},{4,6},{5,7},{6,4},{7,5},{8,10},{9,11},{10,... | collective-permute-start | bytes 1572872 | tf_op jit(solution)/shard_map/ppermute | solution.py:43
  135.9 21.7 %collective-permute-start.12 = (bf16[256,1024]{1,0:T(8,128)(2,1)}, bf16[256,1024]{1,0:T(8,128)(2,1)}, u32[]{:S(2)}, u32[]{:S(2)}) collective-permute-start(bf16[256,1024]{1,0:T(8,128)(2,1)} %multiply_convert_fusion.6), channel_id=1, source_target_pairs={{0,1},{1,0},{2,3},{3,2},{4,5},{5,4},{6,7},{7,6},{8,9},{9,8},{10,11... | collective-permute-start | bytes 1572872 | tf_op jit(solution)/shard_map/ppermute | solution.py:43
  145.8 23.6 %collective-permute-start.13 = (bf16[256,1024]{1,0:T(8,128)(2,1)}, bf16[256,1024]{1,0:T(8,128)(2,1)S(1)}, u32[]{:S(2)}, u32[]{:S(2)}) collective-permute-start(bf16[256,1024]{1,0:T(8,128)(2,1)} %multiply_convert_fusion.6), channel_id=1, source_target_pairs={{0,2},{1,3},{2,0},{3,1},{4,6},{5,7},{6,4},{7,5},{8,10},{9,11},{10,... | collective-permute-start | bytes 1572872 | tf_op jit(solution)/shard_map/ppermute | solution.py:43
  169.4 11.2 %collective-permute-start.14 = (bf16[256,1024]{1,0:T(8,128)(2,1)S(1)}, bf16[256,1024]{1,0:T(8,128)(2,1)S(1)}, u32[]{:S(2)}, u32[]{:S(2)}) collective-permute-start(bf16[256,1024]{1,0:T(8,128)(2,1)S(1)} %collective-permute-done.13), channel_id=1, source_target_pairs={{0,1},{1,0},{2,3},{3,2},{4,5},{5,4},{6,7},{7,6},{8,9},{9,8},{10,11... | collective-permute-start | bytes 1572872 | tf_op jit(solution)/shard_map/ppermute | solution.py:43
  187.8 10.3 %collective-permute-start.15 = (bf16[256,1024]{1,0:T(8,128)(2,1)S(1)}, bf16[256,1024]{1,0:T(8,128)(2,1)S(1)}, u32[]{:S(2)}, u32[]{:S(2)}) collective-permute-start(bf16[256,1024]{1,0:T(8,128)(2,1)S(1)} %fusion.27), channel_id=1, source_target_pairs={{0,1},{1,0},{2,3},{3,2},{4,5},{5,4},{6,7},{7,6},{8,9},{9,8},{10,11... | collective-permute-start | bytes 1572872 | tf_op jit(solution)/shard_map/ppermute | solution.py:43
  199.0 21.6 %collective-permute-start.17 = (bf16[256,1024]{1,0:T(8,128)(2,1)S(1)}, bf16[256,1024]{1,0:T(8,128)(2,1)S(1)}, u32[]{:S(2)}, u32[]{:S(2)}) collective-permute-start(bf16[256,1024]{1,0:T(8,128)(2,1)S(1)} %add_convert_fusion.4), channel_id=1, source_target_pairs={{0,2},{1,3},{2,0},{3,1},{4,6},{5,7},{6,4},{7,5},{8,10},{9,11},{10,... | collective-permute-start | bytes 1572872 | tf_op jit(solution)/shard_map/ppermute | solution.py:43
  200.5 17.9 %collective-permute-start.16 = (bf16[256,1024]{1,0:T(8,128)(2,1)S(1)}, bf16[256,1024]{1,0:T(8,128)(2,1)S(1)}, u32[]{:S(2)}, u32[]{:S(2)}) collective-permute-start(bf16[256,1024]{1,0:T(8,128)(2,1)S(1)} %convolution_add_fusion), channel_id=1, source_target_pairs={{0,1},{1,0},{2,3},{3,2},{4,5},{5,4},{6,7},{7,6},{8,9},{9,8},{10,11... | collective-permute-start | bytes 1572872 | tf_op jit(solution)/shard_map/ppermute | solution.py:43
  222.8 25.7 %collective-permute-start.20 = (bf16[4,1,64,1024]{3,2,1,0:T(8,128)(2,1)}, bf16[4,1,64,1024]{3,2,1,0:T(8,128)(2,1)}, u32[]{:S(2)}, u32[]{:S(2)}) collective-permute-start(bf16[4,1,64,1024]{3,2,1,0:T(8,128)(2,1)} %bitcast.39), channel_id=1, source_target_pairs={{0,2},{1,3},{2,0},{3,1},{4,6},{5,7},{6,4},{7,5},{8,10},{9,11},{10,... | collective-permute-start | bytes 1572872 | tf_op jit(solution)/shard_map/ppermute | solution.py:43
  223.9 41.1 %collective-permute-start.19 = (bf16[4,1,64,1024]{3,2,1,0:T(8,128)(2,1)}, bf16[4,1,64,1024]{3,2,1,0:T(8,128)(2,1)}, u32[]{:S(2)}, u32[]{:S(2)}) collective-permute-start(bf16[4,1,64,1024]{3,2,1,0:T(8,128)(2,1)} %bitcast.39), channel_id=1, source_target_pairs={{0,1},{1,0},{2,3},{3,2},{4,5},{5,4},{6,7},{7,6},{8,9},{9,8},{10,11... | collective-permute-start | bytes 1572872 | tf_op jit(solution)/shard_map/ppermute | solution.py:43
  227.3 34.2 %collective-permute-start.18 = (bf16[256,1024]{1,0:T(8,128)(2,1)}, bf16[256,1024]{1,0:T(8,128)(2,1)}, u32[]{:S(2)}, u32[]{:S(2)}) collective-permute-start(bf16[256,1024]{1,0:T(8,128)(2,1)} %convolution_convert_fusion.3), channel_id=1, source_target_pairs={{0,1},{1,0},{2,3},{3,2},{4,5},{5,4},{6,7},{7,6},{8,9},{9,8},{10,11... | collective-permute-start | bytes 1572872 | tf_op jit(solution)/shard_map/ppermute | solution.py:43
  248.6 22.5 %collective-permute-start.21 = (bf16[4,1,64,1024]{3,2,1,0:T(8,128)(2,1)}, bf16[4,1,64,1024]{3,2,1,0:T(8,128)(2,1)S(1)}, u32[]{:S(2)}, u32[]{:S(2)}) collective-permute-start(bf16[4,1,64,1024]{3,2,1,0:T(8,128)(2,1)} %collective-permute-done.20), channel_id=1, source_target_pairs={{0,1},{1,0},{2,3},{3,2},{4,5},{5,4},{6,7},{7,6},{8,9},{9,8},{10,11... | collective-permute-start | bytes 1572872 | tf_op jit(solution)/shard_map/ppermute | solution.py:43
  282.1 24.6 %collective-permute-start.23 = (bf16[256,1024]{1,0:T(8,128)(2,1)}, bf16[256,1024]{1,0:T(8,128)(2,1)S(1)}, u32[]{:S(2)}, u32[]{:S(2)}) collective-permute-start(bf16[256,1024]{1,0:T(8,128)(2,1)} %add_convert_fusion.3), channel_id=1, source_target_pairs={{0,2},{1,3},{2,0},{3,1},{4,6},{5,7},{6,4},{7,5},{8,10},{9,11},{10,... | collective-permute-start | bytes 1572872 | tf_op jit(solution)/shard_map/ppermute | solution.py:43
  282.6 24.1 %collective-permute-start.22 = (bf16[256,1024]{1,0:T(8,128)(2,1)}, bf16[256,1024]{1,0:T(8,128)(2,1)S(1)}, u32[]{:S(2)}, u32[]{:S(2)}) collective-permute-start(bf16[256,1024]{1,0:T(8,128)(2,1)} %fusion.63), channel_id=1, source_target_pairs={{0,1},{1,0},{2,3},{3,2},{4,5},{5,4},{6,7},{7,6},{8,9},{9,8},{10,11... | collective-permute-start | bytes 1572872 | tf_op jit(solution)/shard_map/ppermute | solution.py:43
  314.1 14.0 %collective-permute-start.24 = (bf16[256,1024]{1,0:T(8,128)(2,1)}, bf16[256,1024]{1,0:T(8,128)(2,1)}, u32[]{:S(2)}, u32[]{:S(2)}) collective-permute-start(bf16[256,1024]{1,0:T(8,128)(2,1)} %fusion.117), channel_id=1, source_target_pairs={{0,1},{1,0},{2,3},{3,2},{4,5},{5,4},{6,7},{7,6},{8,9},{9,8},{10,11... | collective-permute-start | bytes 1572872 | tf_op jit(solution)/shard_map/ppermute | solution.py:43
  317.8 19.3 %collective-permute-start.27 = (bf16[512,768]{0,1:T(8,128)(2,1)}, bf16[512,768]{0,1:T(8,128)(2,1)}, u32[]{:S(2)}, u32[]{:S(2)}) collective-permute-start(bf16[512,768]{0,1:T(8,128)(2,1)} %fusion.98), channel_id=1, source_target_pairs={{0,16},{4,20},{8,24},{12,28},{16,0},{20,4},{24,8},{28,12},{1,17},{... | collective-permute-start | bytes 2359304 | tf_op jit(solution)/shard_map/ppermute | solution.py:43
  331.8 17.2 %collective-permute-start.25 = (bf16[256,1024]{1,0:T(8,128)(2,1)}, bf16[256,1024]{1,0:T(8,128)(2,1)S(1)}, u32[]{:S(2)}, u32[]{:S(2)}) collective-permute-start(bf16[256,1024]{1,0:T(8,128)(2,1)} %fusion.115), channel_id=1, source_target_pairs={{0,1},{1,0},{2,3},{3,2},{4,5},{5,4},{6,7},{7,6},{8,9},{9,8},{10,11... | collective-permute-start | bytes 1572872 | tf_op jit(solution)/shard_map/ppermute | solution.py:43
  339.4 26.9 %collective-permute-start.26 = (bf16[256,1024]{1,0:T(8,128)(2,1)}, bf16[256,1024]{1,0:T(8,128)(2,1)}, u32[]{:S(2)}, u32[]{:S(2)}) collective-permute-start(bf16[256,1024]{1,0:T(8,128)(2,1)} %add_convert_fusion.1), channel_id=1, source_target_pairs={{0,2},{1,3},{2,0},{3,1},{4,6},{5,7},{6,4},{7,5},{8,10},{9,11},{10,... | collective-permute-start | bytes 1572872 | tf_op jit(solution)/shard_map/ppermute | solution.py:43
  354.2 10.6 %collective-permute-start.29 = (f32[2176]{0:T(1024)S(1)}, f32[2176]{0:T(1024)S(1)}, u32[]{:S(2)}, u32[]{:S(2)}) collective-permute-start(f32[2176]{0:T(1024)S(1)} %add.320), channel_id=1, source_target_pairs={{0,2},{1,3},{2,0},{3,1},{4,6},{5,7},{6,4},{7,5},{8,10},{9,11},{10,... | collective-permute-start | bytes 26120 | tf_op jit(solution)/shard_map/ppermute | solution.py:43
  359.0 16.4 %collective-permute-start.33 = (bf16[256,768]{0,1:T(8,128)(2,1)S(1)}, bf16[256,768]{0,1:T(8,128)(2,1)S(1)}, u32[]{:S(2)}, u32[]{:S(2)}) collective-permute-start(bf16[256,768]{0,1:T(8,128)(2,1)S(1)} %constant_dynamic-slice_fusion), channel_id=1, source_target_pairs={{0,8},{4,12},{8,0},{12,4},{16,24},{20,28},{24,16},{28,20},{1,9},{5... | collective-permute-start | bytes 1179656 | tf_op jit(solution)/shard_map/ppermute | solution.py:43
  (97 other events, 814.7 us)
Sparse Core Ops, SparseCore 0:
  22.3 50.1 all-gather.1
  243.7 65.0 reduce-scatter.1

commit v4 on v3

--- a/solution.py
+++ b/solution.py
@@ -172,7 +172,7 @@
         got = swap(send, "tensor", far).astype(jnp.float32)
         arrived = []
         near = fold(pieces, "tensor", near_bits, arrived)[0]
-        return near + got, arrived
+        return near + got, arrived, send
 
     def whole_weight(shard):
         return lax.all_gather(shard, "dp", axis=0, tiled=True)
@@ -268,7 +268,7 @@
         .astype(jnp.bfloat16)
     )
     mixed = after(mixed, back_near, back_far)
-    attn_out, _ = sum_to_rows(
+    attn_out, _, _ = sum_to_rows(
         lambda key: dot_t(group_slice(mixed, key), out_turned), lambda: ()
     )
     attn_out = after(attn_out, feed_pack)
@@ -294,7 +294,7 @@
             block_of(near_parts[2], far_parts[2], key), up_full
         )
 
-    grad_feed_in, _ = sum_to_rows(grad_feed_part, lambda: ())
+    grad_feed_in, _, _ = sum_to_rows(grad_feed_part, lambda: ())
     hidden, grad_gate, grad_up = (
         jnp.concatenate([one, two], axis=0) for one, two in zip(near_parts, far_parts)
     )
@@ -355,7 +355,7 @@
             * scale
         )
     query_parts = query_parts[::-1]
-    feed_out, _ = sum_to_rows(
+    feed_out, feed_arrived, feed_sent = sum_to_rows(
         lambda key: dot_t(
             lax.slice_in_dim(hidden, key * local_rows, (key + 1) * local_rows, axis=0), down_full
         ),
@@ -379,7 +379,7 @@
         ],
         axis=1,
     ).astype(jnp.bfloat16)
-    grad_project = after(grad_project, output)
+    grad_project = after(grad_project, feed_arrived)
     later = {}
 
     def grad_rows_part(key):
@@ -397,9 +397,9 @@
         )
         later["gains"] = gains
         later["sums"] = halve(pack, group, "dp", dp_bits[-1])
-        return (grad_feed_w,)
-
-    grad_attn_in, arrived = sum_to_rows(grad_rows_part, tail_between)
+        return grad_feed_w, output
+
+    grad_attn_in, arrived, _ = sum_to_rows(grad_rows_part, tail_between)
     gains, attn_grad = after((later["gains"], later["sums"]), arrived)
     for bit in tensor_bits:
         gains = gains + swap(gains, "tensor", bit)

time: 394 us -> 389 us (0.987)
  waiting for transfers between devices: 156 us -> 151 us
    ppermute x35, waiting for transfers between devices: 156 us -> 151 us  [swap(): lax.ppermute(values, axis, [(index, index ^ bit) for index in range(count)])]
    unnamed x196 -> x198, local copies, waits for them, and re-layouts: 18.6 us -> 17.7 us
  transfers between devices with their start and end apart: 37 -> 37, of which waited for: 25 -> 25; matrix products, arithmetic and copies ran while one was open for 35% -> 36% of each run, Pallas kernels for 0% -> 0%
where the time goes in v4:
time: 389 us; the launch traced here: 382 us
  waiting for transfers between devices  151 us (39%)
  matrix products  76.3 us (20%)
  starting transfers between devices  51.5 us (13%)
  other arithmetic  48.9 us (13%)
  local copies, waits for them, and re-layouts  38.3 us (10%)
  between operations  16 us (4%)
    ppermute x35, waiting for transfers between devices, swap(): lax.ppermute(values, axis, [(index, index ^ bit) for index in range(count)])  151 us
    ppermute x35, starting transfers between devices, swap(): lax.ppermute(values, axis, [(index, index ^ bit) for index in range(count)])  51.4 us
    dot_general x20, matrix products, dot_t(): lax.dot_general(left, right, (((1,), (1,)), ((), ())), preferred_element_...  27.9 us
    dot_general x8, matrix products, dot(): return jnp.dot(left, right, preferred_element_type=jnp.float32)  19.4 us
    unnamed x198, local copies, waits for them, and re-layouts  17.7 us
    dot_general x5, matrix products, dot_tl(): lax.dot_general(left, right, (((0,), (0,)), ((), ())), preferred_element_...  14.4 us
  transfers between devices with their start and end apart: 37, of which 25 were waited for; matrix products, arithmetic and copies ran while one was open for 36% of the time, Pallas kernels for 0%

profile of v4, /device:TPU:0, one launch (start us, length us, event | category | flops | bytes accessed | tf_op | source)
XLA Modules:
  0.0 382.5 jit_solution(14115965782010776917)
XLA Ops:
  9.8 4.1 %collective-permute-start.1 = (bf16[4,1,64,1024]{3,2,1,0:T(8,128)(2,1)S(1)}, bf16[4,1,64,1024]{3,2,1,0:T(8,128)(2,1)}, u32[]{:S(2)}, u32[]{:S(2)}) collective-permute-start(bf16[4,1,64,1024]{3,2,1,0:T(8,128)(2,1)S(1)} %fusion.57), channel_id=1, source_target_pairs={{0,2},{1,3},{2,0},{3,1},{4,6},{5,7},{6,4},{7,5},{8,10},{9,11},{10,... | collective-permute-start | bytes 1572872 | tf_op jit(solution)/shard_map/ppermute | solution.py:43
  27.1 10.3 %collective-permute-done.1 = bf16[4,1,64,1024]{3,2,1,0:T(8,128)(2,1)} collective-permute-done((bf16[4,1,64,1024]{3,2,1,0:T(8,128)(2,1)S(1)}, bf16[4,1,64,1024]{3,2,1,0:T(8,128)(2,1)}, u32[]{:S(2)}, u32[]{:S(2)}) %collective-permute-start.1) | collective-permute-done | bytes 524320 | tf_op jit(solution)/shard_map/ppermute | solution.py:43
  37.8 4.5 %collective-permute-done.4 = bf16[2,128,768]{1,2,0:T(8,128)(2,1)S(1)} collective-permute-done((bf16[2,128,768]{1,2,0:T(8,128)(2,1)S(1)}, bf16[2,128,768]{1,2,0:T(8,128)(2,1)S(1)}, u32[]{:S(2)}, u32[]{:S(2)}) %collective-permute-start.4) | collective-permute-done | bytes 393248 | tf_op jit(solution)/shard_map/ppermute | solution.py:43
  45.0 5.7 %collective-permute-done.2 = bf16[4,1,64,1024]{3,2,1,0:T(8,128)(2,1)} collective-permute-done((bf16[4,1,64,1024]{3,2,1,0:T(8,128)(2,1)}, bf16[4,1,64,1024]{3,2,1,0:T(8,128)(2,1)}, u32[]{:S(2)}, u32[]{:S(2)}) %collective-permute-start.2) | collective-permute-done | bytes 524320 | tf_op jit(solution)/shard_map/ppermute | solution.py:43
  53.7 3.0 collective-permute-start.7
  63.5 4.0 %reshape.461 = bf16[1024,768]{0,1:T(8,128)(2,1)} reshape(bf16[2,2,2,128,768]{3,2,1,0,4:T(2,128)(2,1)} %copy.98) | data formatting | bytes 3145728 | tf_op jit(solution)/shard_map/reshape | solution.py:189
  67.5 3.1 fusion.169
  85.7 8.2 %collective-permute-done.8 = bf16[256,1024]{1,0:T(8,128)(2,1)S(1)} collective-permute-done((bf16[256,1024]{1,0:T(8,128)(2,1)}, bf16[256,1024]{1,0:T(8,128)(2,1)S(1)}, u32[]{:S(2)}, u32[]{:S(2)}) %collective-permute-start.8) | collective-permute-done | bytes 524320 | tf_op jit(solution)/shard_map/ppermute | solution.py:43
  98.6 10.6 %collective-permute-done.9 = bf16[256,1024]{1,0:T(8,128)(2,1)S(1)} collective-permute-done((bf16[256,1024]{1,0:T(8,128)(2,1)S(1)}, bf16[256,1024]{1,0:T(8,128)(2,1)S(1)}, u32[]{:S(2)}, u32[]{:S(2)}) %collective-permute-start.9) | collective-permute-done | bytes 524320 | tf_op jit(solution)/shard_map/ppermute | solution.py:43
  110.6 4.1 %collective-permute-start.11 = (bf16[256,1024]{1,0:T(8,128)(2,1)S(1)}, bf16[256,1024]{1,0:T(8,128)(2,1)S(1)}, u32[]{:S(2)}, u32[]{:S(2)}) collective-permute-start(bf16[256,1024]{1,0:T(8,128)(2,1)S(1)} %add_convert_fusion.5), channel_id=1, source_target_pairs={{0,2},{1,3},{2,0},{3,1},{4,6},{5,7},{6,4},{7,5},{8,10},{9,11},{10,... | collective-permute-start | bytes 1572872 | tf_op jit(solution)/shard_map/ppermute | solution.py:43
  115.0 16.5 %collective-permute-done.10 = bf16[256,1024]{1,0:T(8,128)(2,1)S(1)} collective-permute-done((bf16[256,1024]{1,0:T(8,128)(2,1)S(1)}, bf16[256,1024]{1,0:T(8,128)(2,1)S(1)}, u32[]{:S(2)}, u32[]{:S(2)}) %collective-permute-start.10) | collective-permute-done | bytes 524320 | tf_op jit(solution)/shard_map/ppermute | solution.py:43
  135.9 5.3 %collective-permute-start.12 = (bf16[256,1024]{1,0:T(8,128)(2,1)}, bf16[256,1024]{1,0:T(8,128)(2,1)}, u32[]{:S(2)}, u32[]{:S(2)}) collective-permute-start(bf16[256,1024]{1,0:T(8,128)(2,1)} %multiply_convert_fusion.6), channel_id=1, source_target_pairs={{0,1},{1,0},{2,3},{3,2},{4,5},{5,4},{6,7},{7,6},{8,9},{9,8},{10,11... | collective-permute-start | bytes 1572872 | tf_op jit(solution)/shard_map/ppermute | solution.py:43
  148.5 9.1 %collective-permute-done.12 = bf16[256,1024]{1,0:T(8,128)(2,1)} collective-permute-done((bf16[256,1024]{1,0:T(8,128)(2,1)}, bf16[256,1024]{1,0:T(8,128)(2,1)}, u32[]{:S(2)}, u32[]{:S(2)}) %collective-permute-start.12) | collective-permute-done | bytes 524320 | tf_op jit(solution)/shard_map/ppermute | solution.py:43
  157.6 4.0 %fusion.82 = f32[512,1152]{1,0:T(8,128)S(1)} fusion(bf16[1024,3456]{0,1:T(8,128)(2,1)} %all-gather.2.cloned.1.call-done, bf16[256,1024]{1,0:T(8,128)(2,1)} %collective-permute-done.12, bf16[256,1024]{1,0:T(8,128)(2,1)} %multiply_convert_fusion.6), kind=kOutput, calls=%fused_computation.151 | convolution fusion | flops 1210056704 | bytes 5767168 | tf_op jit(solution)/shard_map/dot_general | solution.py:56
  164.4 5.0 %collective-permute-done.13 = bf16[256,1024]{1,0:T(8,128)(2,1)S(1)} collective-permute-done((bf16[256,1024]{1,0:T(8,128)(2,1)}, bf16[256,1024]{1,0:T(8,128)(2,1)S(1)}, u32[]{:S(2)}, u32[]{:S(2)}) %collective-permute-start.13) | collective-permute-done | bytes 524320 | tf_op jit(solution)/shard_map/ppermute | solution.py:43
  175.1 5.5 %collective-permute-done.14 = bf16[256,1024]{1,0:T(8,128)(2,1)S(1)} collective-permute-done((bf16[256,1024]{1,0:T(8,128)(2,1)S(1)}, bf16[256,1024]{1,0:T(8,128)(2,1)S(1)}, u32[]{:S(2)}, u32[]{:S(2)}) %collective-permute-start.14) | collective-permute-done | bytes 524320 | tf_op jit(solution)/shard_map/ppermute | solution.py:43
  189.1 9.0 %collective-permute-done.15 = bf16[256,1024]{1,0:T(8,128)(2,1)S(1)} collective-permute-done((bf16[256,1024]{1,0:T(8,128)(2,1)S(1)}, bf16[256,1024]{1,0:T(8,128)(2,1)S(1)}, u32[]{:S(2)}, u32[]{:S(2)}) %collective-permute-start.15) | collective-permute-done | bytes 524320 | tf_op jit(solution)/shard_map/ppermute | solution.py:43
  202.7 15.7 %collective-permute-done.16 = bf16[256,1024]{1,0:T(8,128)(2,1)S(1)} collective-permute-done((bf16[256,1024]{1,0:T(8,128)(2,1)S(1)}, bf16[256,1024]{1,0:T(8,128)(2,1)S(1)}, u32[]{:S(2)}, u32[]{:S(2)}) %collective-permute-start.16) | collective-permute-done | bytes 524320 | tf_op jit(solution)/shard_map/ppermute | solution.py:43
  227.6 4.1 %convolution_convert_fusion = bf16[1024,1152]{1,0:T(8,128)(2,1)S(1)} fusion(bf16[1024,1152]{1,0:T(8,128)(2,1)S(1)} %pad_maximum_fusion.1, bf16[256,1024]{1,0:T(8,128)(2,1)S(1)} %copy-done.40, bf16[256,1024]{1,0:T(8,128)(2,1)} %collective-permute-done.7, bf16[256,1024]{1,0:T(8,128)(2,1)} %collective-permute-done.6, bf16[256,1024]{1,0:T(8,128)(2,1)S(1)} %bitcast.234), kind=kOutput, calls=%fused_computation.24 | convolution fusion | flops 2425487360 | bytes 6815744 | tf_op jit(solution)/shard_map/dot_general | solution.py:66
  231.7 4.1 %convolution_convert_fusion.2 = bf16[1024,1152]{1,0:T(8,128)(2,1)S(1)} fusion(bf16[1024,1152]{1,0:T(8,128)(2,1)S(1)} %pad_maximum_fusion.2, bf16[256,1024]{1,0:T(8,128)(2,1)S(1)} %collective-permute-done.14, bf16[256,1024]{1,0:T(8,128)(2,1)S(1)} %collective-permute-done.13, bf16[256,1024]{1,0:T(8,128)(2,1)} %collective-permute-done.12, ...), kind=kOutput, calls=%fused_computation.26 | convolution fusion | flops 2425487360 | bytes 6815744 | tf_op jit(solution)/shard_map/dot_general | solution.py:66
  235.9 4.1 %convolution_convert_fusion.1 = bf16[1024,1152]{1,0:T(8,128)(2,1)S(1)} fusion(bf16[1024,1152]{1,0:T(8,128)(2,1)S(1)} %pad_maximum_fusion.3, bf16[256,1024]{1,0:T(8,128)(2,1)S(1)} %collective-permute-done.14, bf16[256,1024]{1,0:T(8,128)(2,1)S(1)} %collective-permute-done.13, bf16[256,1024]{1,0:T(8,128)(2,1)} %collective-permute-done.12, ...), kind=kOutput, calls=%fused_computation.25 | convolution fusion | flops 2425487360 | bytes 6815744 | tf_op jit(solution)/shard_map/dot_general | solution.py:66
  240.0 3.5 pad_maximum_fusion
  243.6 3.9 %fusion.68 = f32[256,1024]{1,0:T(8,128)} fusion(bf16[1024,3456]{0,1:T(8,128)(2,1)} %all-gather.2.cloned.1.call-done, bf16[1024,1152]{1,0:T(8,128)(2,1)} %copy-done.20), kind=kOutput, calls=%fused_computation.139 | convolution fusion | flops 603979776 | bytes 3997696 | tf_op jit(solution)/shard_map/dot_general | solution.py:60
  249.2 3.4 fusion.63
  252.5 8.9 %collective-permute-done.18 = bf16[256,1024]{1,0:T(8,128)(2,1)} collective-permute-done((bf16[256,1024]{1,0:T(8,128)(2,1)}, bf16[256,1024]{1,0:T(8,128)(2,1)}, u32[]{:S(2)}, u32[]{:S(2)}) %collective-permute-start.18) | collective-permute-done | bytes 524320 | tf_op jit(solution)/shard_map/ppermute | solution.py:43
  261.5 3.6 add_convert_fusion.3
  265.0 6.0 %collective-permute-done.21 = bf16[4,1,64,1024]{3,2,1,0:T(8,128)(2,1)S(1)} collective-permute-done((bf16[4,1,64,1024]{3,2,1,0:T(8,128)(2,1)}, bf16[4,1,64,1024]{3,2,1,0:T(8,128)(2,1)S(1)}, u32[]{:S(2)}, u32[]{:S(2)}) %collective-permute-start.21) | collective-permute-done | bytes 524320 | tf_op jit(solution)/shard_map/ppermute | solution.py:43
  278.5 3.6 fusion.2
  296.5 10.3 %collective-permute-done.22 = bf16[256,1024]{1,0:T(8,128)(2,1)} collective-permute-done((bf16[256,1024]{1,0:T(8,128)(2,1)}, bf16[256,1024]{1,0:T(8,128)(2,1)}, u32[]{:S(2)}, u32[]{:S(2)}) %collective-permute-start.22) | collective-permute-done | bytes 524320 | tf_op jit(solution)/shard_map/ppermute | solution.py:43
  329.4 4.8 %collective-permute-done.27 = bf16[512,768]{0,1:T(8,128)(2,1)} collective-permute-done((bf16[512,768]{0,1:T(8,128)(2,1)}, bf16[512,768]{0,1:T(8,128)(2,1)}, u32[]{:S(2)}, u32[]{:S(2)}) %collective-permute-start.27) | collective-permute-done | bytes 786464 | tf_op jit(solution)/shard_map/ppermute | solution.py:43
  338.0 4.2 %collective-permute-done.25 = bf16[256,1024]{1,0:T(8,128)(2,1)S(1)} collective-permute-done((bf16[256,1024]{1,0:T(8,128)(2,1)}, bf16[256,1024]{1,0:T(8,128)(2,1)S(1)}, u32[]{:S(2)}, u32[]{:S(2)}) %collective-permute-start.25) | collective-permute-done | bytes 524320 | tf_op jit(solution)/shard_map/ppermute | solution.py:43
  354.8 5.1 %collective-permute-done.29 = f32[2176]{0:T(1024)S(1)} collective-permute-done((f32[2176]{0:T(1024)S(1)}, f32[2176]{0:T(1024)S(1)}, u32[]{:S(2)}, u32[]{:S(2)}) %collective-permute-start.29) | collective-permute-done | bytes 8736 | tf_op jit(solution)/shard_map/ppermute | solution.py:43
  (397 shorter events, 169.1 us)
Async XLA Ops:
  7.2 125.6 %all-gather.2.cloned.1.call-start = ((), (), s32[]{:S(2)}) async-start(), calls=%async_computation.1 | async-start | bytes 7962624 | tf_op jit(solution)/shard_map/all_gather | solution.py:178
  9.8 27.5 %collective-permute-start.1 = (bf16[4,1,64,1024]{3,2,1,0:T(8,128)(2,1)S(1)}, bf16[4,1,64,1024]{3,2,1,0:T(8,128)(2,1)}, u32[]{:S(2)}, u32[]{:S(2)}) collective-permute-start(bf16[4,1,64,1024]{3,2,1,0:T(8,128)(2,1)S(1)} %fusion.57), channel_id=1, source_target_pairs={{0,2},{1,3},{2,0},{3,1},{4,6},{5,7},{6,4},{7,5},{8,10},{9,11},{10,... | collective-permute-start | bytes 1572872 | tf_op jit(solution)/shard_map/ppermute | solution.py:43
  13.9 31.1 %collective-permute-start = (bf16[4,1,64,1024]{3,2,1,0:T(8,128)(2,1)S(1)}, bf16[4,1,64,1024]{3,2,1,0:T(8,128)(2,1)}, u32[]{:S(2)}, u32[]{:S(2)}) collective-permute-start(bf16[4,1,64,1024]{3,2,1,0:T(8,128)(2,1)S(1)} %fusion.57), channel_id=1, source_target_pairs={{0,1},{1,0},{2,3},{3,2},{4,5},{5,4},{6,7},{7,6},{8,9},{9,8},{10,11... | collective-permute-start | bytes 1572872 | tf_op jit(solution)/shard_map/ppermute | solution.py:43
  22.2 304.0 %reduce-scatter.2.cloned.1.call-start = ((), (), s32[]{:S(2)}) async-start(), calls=%async_computation.2 | async-start | bytes 7962624 | tf_op jit(solution)/shard_map/reduce_scatter | solution.py:181
  25.4 16.9 %collective-permute-start.4 = (bf16[2,128,768]{1,2,0:T(8,128)(2,1)S(1)}, bf16[2,128,768]{1,2,0:T(8,128)(2,1)S(1)}, u32[]{:S(2)}, u32[]{:S(2)}) collective-permute-start(bf16[2,128,768]{1,2,0:T(8,128)(2,1)S(1)} %pad_maximum_fusion.17), channel_id=1, source_target_pairs={{0,16},{4,20},{8,24},{12,28},{16,0},{20,4},{24,8},{28,12},{1,17},{... | collective-permute-start | bytes 1179656 | tf_op jit(solution)/shard_map/ppermute | solution.py:43
  37.3 13.4 %collective-permute-start.2 = (bf16[4,1,64,1024]{3,2,1,0:T(8,128)(2,1)}, bf16[4,1,64,1024]{3,2,1,0:T(8,128)(2,1)}, u32[]{:S(2)}, u32[]{:S(2)}) collective-permute-start(bf16[4,1,64,1024]{3,2,1,0:T(8,128)(2,1)} %collective-permute-done.1), channel_id=1, source_target_pairs={{0,1},{1,0},{2,3},{3,2},{4,5},{5,4},{6,7},{7,6},{8,9},{9,8},{10,11... | collective-permute-start | bytes 1572872 | tf_op jit(solution)/shard_map/ppermute | solution.py:43
  42.4 16.9 %collective-permute-start.5 = (bf16[2,2,128,768]{2,3,1,0:T(8,128)(2,1)S(1)}, bf16[2,2,128,768]{2,3,1,0:T(8,128)(2,1)}, u32[]{:S(2)}, u32[]{:S(2)}) collective-permute-start(bf16[2,2,128,768]{2,3,1,0:T(8,128)(2,1)S(1)} %pad_maximum_fusion.13), channel_id=1, source_target_pairs={{0,4},{4,0},{8,12},{12,8},{16,20},{20,16},{24,28},{28,24},{1,5},{5... | collective-permute-start | bytes 2359304 | tf_op jit(solution)/shard_map/ppermute | solution.py:43
  53.7 27.5 %collective-permute-start.7 = (bf16[256,1024]{1,0:T(8,128)(2,1)S(1)}, bf16[256,1024]{1,0:T(8,128)(2,1)}, u32[]{:S(2)}, u32[]{:S(2)}) collective-permute-start(bf16[256,1024]{1,0:T(8,128)(2,1)S(1)} %bitcast.231), channel_id=1, source_target_pairs={{0,2},{1,3},{2,0},{3,1},{4,6},{5,7},{6,4},{7,5},{8,10},{9,11},{10,... | collective-permute-start | bytes 1572872 | tf_op jit(solution)/shard_map/ppermute | solution.py:43
  56.7 27.8 %collective-permute-start.6 = (bf16[256,1024]{1,0:T(8,128)(2,1)S(1)}, bf16[256,1024]{1,0:T(8,128)(2,1)}, u32[]{:S(2)}, u32[]{:S(2)}) collective-permute-start(bf16[256,1024]{1,0:T(8,128)(2,1)S(1)} %bitcast.232), channel_id=1, source_target_pairs={{0,1},{1,0},{2,3},{3,2},{4,5},{5,4},{6,7},{7,6},{8,9},{9,8},{10,11... | collective-permute-start | bytes 1572872 | tf_op jit(solution)/shard_map/ppermute | solution.py:43
  81.2 12.7 %collective-permute-start.8 = (bf16[256,1024]{1,0:T(8,128)(2,1)}, bf16[256,1024]{1,0:T(8,128)(2,1)S(1)}, u32[]{:S(2)}, u32[]{:S(2)}) collective-permute-start(bf16[256,1024]{1,0:T(8,128)(2,1)} %collective-permute-done.7), channel_id=1, source_target_pairs={{0,1},{1,0},{2,3},{3,2},{4,5},{5,4},{6,7},{7,6},{8,9},{9,8},{10,11... | collective-permute-start | bytes 1572872 | tf_op jit(solution)/shard_map/ppermute | solution.py:43
  97.4 11.8 %collective-permute-start.9 = (bf16[256,1024]{1,0:T(8,128)(2,1)S(1)}, bf16[256,1024]{1,0:T(8,128)(2,1)S(1)}, u32[]{:S(2)}, u32[]{:S(2)}) collective-permute-start(bf16[256,1024]{1,0:T(8,128)(2,1)S(1)} %convolution_convert_fusion.4), channel_id=1, source_target_pairs={{0,1},{1,0},{2,3},{3,2},{4,5},{5,4},{6,7},{7,6},{8,9},{9,8},{10,11... | collective-permute-start | bytes 1572872 | tf_op jit(solution)/shard_map/ppermute | solution.py:43
  109.5 22.0 %collective-permute-start.10 = (bf16[256,1024]{1,0:T(8,128)(2,1)S(1)}, bf16[256,1024]{1,0:T(8,128)(2,1)S(1)}, u32[]{:S(2)}, u32[]{:S(2)}) collective-permute-start(bf16[256,1024]{1,0:T(8,128)(2,1)S(1)} %fusion.128), channel_id=1, source_target_pairs={{0,1},{1,0},{2,3},{3,2},{4,5},{5,4},{6,7},{7,6},{8,9},{9,8},{10,11... | collective-permute-start | bytes 1572872 | tf_op jit(solution)/shard_map/ppermute | solution.py:43
  110.6 20.9 %collective-permute-start.11 = (bf16[256,1024]{1,0:T(8,128)(2,1)S(1)}, bf16[256,1024]{1,0:T(8,128)(2,1)S(1)}, u32[]{:S(2)}, u32[]{:S(2)}) collective-permute-start(bf16[256,1024]{1,0:T(8,128)(2,1)S(1)} %add_convert_fusion.5), channel_id=1, source_target_pairs={{0,2},{1,3},{2,0},{3,1},{4,6},{5,7},{6,4},{7,5},{8,10},{9,11},{10,... | collective-permute-start | bytes 1572872 | tf_op jit(solution)/shard_map/ppermute | solution.py:43
  135.9 21.6 %collective-permute-start.12 = (bf16[256,1024]{1,0:T(8,128)(2,1)}, bf16[256,1024]{1,0:T(8,128)(2,1)}, u32[]{:S(2)}, u32[]{:S(2)}) collective-permute-start(bf16[256,1024]{1,0:T(8,128)(2,1)} %multiply_convert_fusion.6), channel_id=1, source_target_pairs={{0,1},{1,0},{2,3},{3,2},{4,5},{5,4},{6,7},{7,6},{8,9},{9,8},{10,11... | collective-permute-start | bytes 1572872 | tf_op jit(solution)/shard_map/ppermute | solution.py:43
  145.8 23.6 %collective-permute-start.13 = (bf16[256,1024]{1,0:T(8,128)(2,1)}, bf16[256,1024]{1,0:T(8,128)(2,1)S(1)}, u32[]{:S(2)}, u32[]{:S(2)}) collective-permute-start(bf16[256,1024]{1,0:T(8,128)(2,1)} %multiply_convert_fusion.6), channel_id=1, source_target_pairs={{0,2},{1,3},{2,0},{3,1},{4,6},{5,7},{6,4},{7,5},{8,10},{9,11},{10,... | collective-permute-start | bytes 1572872 | tf_op jit(solution)/shard_map/ppermute | solution.py:43
  169.4 11.2 %collective-permute-start.14 = (bf16[256,1024]{1,0:T(8,128)(2,1)S(1)}, bf16[256,1024]{1,0:T(8,128)(2,1)S(1)}, u32[]{:S(2)}, u32[]{:S(2)}) collective-permute-start(bf16[256,1024]{1,0:T(8,128)(2,1)S(1)} %collective-permute-done.13), channel_id=1, source_target_pairs={{0,1},{1,0},{2,3},{3,2},{4,5},{5,4},{6,7},{7,6},{8,9},{9,8},{10,11... | collective-permute-start | bytes 1572872 | tf_op jit(solution)/shard_map/ppermute | solution.py:43
  187.8 10.3 %collective-permute-start.15 = (bf16[256,1024]{1,0:T(8,128)(2,1)S(1)}, bf16[256,1024]{1,0:T(8,128)(2,1)S(1)}, u32[]{:S(2)}, u32[]{:S(2)}) collective-permute-start(bf16[256,1024]{1,0:T(8,128)(2,1)S(1)} %fusion.27), channel_id=1, source_target_pairs={{0,1},{1,0},{2,3},{3,2},{4,5},{5,4},{6,7},{7,6},{8,9},{9,8},{10,11... | collective-permute-start | bytes 1572872 | tf_op jit(solution)/shard_map/ppermute | solution.py:43
  199.0 21.6 %collective-permute-start.17 = (bf16[256,1024]{1,0:T(8,128)(2,1)S(1)}, bf16[256,1024]{1,0:T(8,128)(2,1)S(1)}, u32[]{:S(2)}, u32[]{:S(2)}) collective-permute-start(bf16[256,1024]{1,0:T(8,128)(2,1)S(1)} %add_convert_fusion.4), channel_id=1, source_target_pairs={{0,2},{1,3},{2,0},{3,1},{4,6},{5,7},{6,4},{7,5},{8,10},{9,11},{10,... | collective-permute-start | bytes 1572872 | tf_op jit(solution)/shard_map/ppermute | solution.py:43
  200.5 17.9 %collective-permute-start.16 = (bf16[256,1024]{1,0:T(8,128)(2,1)S(1)}, bf16[256,1024]{1,0:T(8,128)(2,1)S(1)}, u32[]{:S(2)}, u32[]{:S(2)}) collective-permute-start(bf16[256,1024]{1,0:T(8,128)(2,1)S(1)} %convolution_add_fusion), channel_id=1, source_target_pairs={{0,1},{1,0},{2,3},{3,2},{4,5},{5,4},{6,7},{7,6},{8,9},{9,8},{10,11... | collective-permute-start | bytes 1572872 | tf_op jit(solution)/shard_map/ppermute | solution.py:43
  222.9 25.7 %collective-permute-start.20 = (bf16[4,1,64,1024]{3,2,1,0:T(8,128)(2,1)}, bf16[4,1,64,1024]{3,2,1,0:T(8,128)(2,1)}, u32[]{:S(2)}, u32[]{:S(2)}) collective-permute-start(bf16[4,1,64,1024]{3,2,1,0:T(8,128)(2,1)} %bitcast.39), channel_id=1, source_target_pairs={{0,2},{1,3},{2,0},{3,1},{4,6},{5,7},{6,4},{7,5},{8,10},{9,11},{10,... | collective-permute-start | bytes 1572872 | tf_op jit(solution)/shard_map/ppermute | solution.py:43
  223.9 41.1 %collective-permute-start.19 = (bf16[4,1,64,1024]{3,2,1,0:T(8,128)(2,1)}, bf16[4,1,64,1024]{3,2,1,0:T(8,128)(2,1)}, u32[]{:S(2)}, u32[]{:S(2)}) collective-permute-start(bf16[4,1,64,1024]{3,2,1,0:T(8,128)(2,1)} %bitcast.39), channel_id=1, source_target_pairs={{0,1},{1,0},{2,3},{3,2},{4,5},{5,4},{6,7},{7,6},{8,9},{9,8},{10,11... | collective-permute-start | bytes 1572872 | tf_op jit(solution)/shard_map/ppermute | solution.py:43
  227.3 34.2 %collective-permute-start.18 = (bf16[256,1024]{1,0:T(8,128)(2,1)}, bf16[256,1024]{1,0:T(8,128)(2,1)}, u32[]{:S(2)}, u32[]{:S(2)}) collective-permute-start(bf16[256,1024]{1,0:T(8,128)(2,1)} %convolution_convert_fusion.3), channel_id=1, source_target_pairs={{0,1},{1,0},{2,3},{3,2},{4,5},{5,4},{6,7},{7,6},{8,9},{9,8},{10,11... | collective-permute-start | bytes 1572872 | tf_op jit(solution)/shard_map/ppermute | solution.py:43
  248.6 22.5 %collective-permute-start.21 = (bf16[4,1,64,1024]{3,2,1,0:T(8,128)(2,1)}, bf16[4,1,64,1024]{3,2,1,0:T(8,128)(2,1)S(1)}, u32[]{:S(2)}, u32[]{:S(2)}) collective-permute-start(bf16[4,1,64,1024]{3,2,1,0:T(8,128)(2,1)} %collective-permute-done.20), channel_id=1, source_target_pairs={{0,1},{1,0},{2,3},{3,2},{4,5},{5,4},{6,7},{7,6},{8,9},{9,8},{10,11... | collective-permute-start | bytes 1572872 | tf_op jit(solution)/shard_map/ppermute | solution.py:43
  282.1 38.7 %collective-permute-start.23 = (bf16[256,1024]{1,0:T(8,128)(2,1)}, bf16[256,1024]{1,0:T(8,128)(2,1)}, u32[]{:S(2)}, u32[]{:S(2)}) collective-permute-start(bf16[256,1024]{1,0:T(8,128)(2,1)} %add_convert_fusion.3), channel_id=1, source_target_pairs={{0,2},{1,3},{2,0},{3,1},{4,6},{5,7},{6,4},{7,5},{8,10},{9,11},{10,... | collective-permute-start | bytes 1572872 | tf_op jit(solution)/shard_map/ppermute | solution.py:43
  282.6 24.2 %collective-permute-start.22 = (bf16[256,1024]{1,0:T(8,128)(2,1)}, bf16[256,1024]{1,0:T(8,128)(2,1)}, u32[]{:S(2)}, u32[]{:S(2)}) collective-permute-start(bf16[256,1024]{1,0:T(8,128)(2,1)} %fusion.63), channel_id=1, source_target_pairs={{0,1},{1,0},{2,3},{3,2},{4,5},{5,4},{6,7},{7,6},{8,9},{9,8},{10,11... | collective-permute-start | bytes 1572872 | tf_op jit(solution)/shard_map/ppermute | solution.py:43
  312.9 11.0 %collective-permute-start.24 = (bf16[256,1024]{1,0:T(8,128)(2,1)}, bf16[256,1024]{1,0:T(8,128)(2,1)}, u32[]{:S(2)}, u32[]{:S(2)}) collective-permute-start(bf16[256,1024]{1,0:T(8,128)(2,1)} %fusion.117), channel_id=1, source_target_pairs={{0,1},{1,0},{2,3},{3,2},{4,5},{5,4},{6,7},{7,6},{8,9},{9,8},{10,11... | collective-permute-start | bytes 1572872 | tf_op jit(solution)/shard_map/ppermute | solution.py:43
  316.6 17.7 %collective-permute-start.27 = (bf16[512,768]{0,1:T(8,128)(2,1)}, bf16[512,768]{0,1:T(8,128)(2,1)}, u32[]{:S(2)}, u32[]{:S(2)}) collective-permute-start(bf16[512,768]{0,1:T(8,128)(2,1)} %fusion.98), channel_id=1, source_target_pairs={{0,16},{4,20},{8,24},{12,28},{16,0},{20,4},{24,8},{28,12},{1,17},{... | collective-permute-start | bytes 2359304 | tf_op jit(solution)/shard_map/ppermute | solution.py:43
  327.6 14.5 %collective-permute-start.25 = (bf16[256,1024]{1,0:T(8,128)(2,1)}, bf16[256,1024]{1,0:T(8,128)(2,1)S(1)}, u32[]{:S(2)}, u32[]{:S(2)}) collective-permute-start(bf16[256,1024]{1,0:T(8,128)(2,1)} %fusion.115), channel_id=1, source_target_pairs={{0,1},{1,0},{2,3},{3,2},{4,5},{5,4},{6,7},{7,6},{8,9},{9,8},{10,11... | collective-permute-start | bytes 1572872 | tf_op jit(solution)/shard_map/ppermute | solution.py:43
  336.6 24.7 %collective-permute-start.26 = (bf16[256,1024]{1,0:T(8,128)(2,1)}, bf16[256,1024]{1,0:T(8,128)(2,1)}, u32[]{:S(2)}, u32[]{:S(2)}) collective-permute-start(bf16[256,1024]{1,0:T(8,128)(2,1)} %add_convert_fusion.1), channel_id=1, source_target_pairs={{0,2},{1,3},{2,0},{3,1},{4,6},{5,7},{6,4},{7,5},{8,10},{9,11},{10,... | collective-permute-start | bytes 1572872 | tf_op jit(solution)/shard_map/ppermute | solution.py:43
  342.1 7.8 %collective-permute-start.28 = (f32[2176]{0:T(1024)S(1)}, f32[2176]{0:T(1024)S(1)}, u32[]{:S(2)}, u32[]{:S(2)}) collective-permute-start(f32[2176]{0:T(1024)S(1)} %concatenate.102), channel_id=1, source_target_pairs={{0,1},{1,0},{2,3},{3,2},{4,5},{5,4},{6,7},{7,6},{8,9},{9,8},{10,11... | collective-permute-start | bytes 26120 | tf_op jit(solution)/shard_map/ppermute | solution.py:43
  350.0 9.9 %collective-permute-start.29 = (f32[2176]{0:T(1024)S(1)}, f32[2176]{0:T(1024)S(1)}, u32[]{:S(2)}, u32[]{:S(2)}) collective-permute-start(f32[2176]{0:T(1024)S(1)} %add.320), channel_id=1, source_target_pairs={{0,2},{1,3},{2,0},{3,1},{4,6},{5,7},{6,4},{7,5},{8,10},{9,11},{10,... | collective-permute-start | bytes 26120 | tf_op jit(solution)/shard_map/ppermute | solution.py:43
  353.2 17.2 %collective-permute-start.33 = (bf16[256,768]{0,1:T(8,128)(2,1)S(1)}, bf16[256,768]{0,1:T(8,128)(2,1)S(1)}, u32[]{:S(2)}, u32[]{:S(2)}) collective-permute-start(bf16[256,768]{0,1:T(8,128)(2,1)S(1)} %constant_dynamic-slice_fusion), channel_id=1, source_target_pairs={{0,8},{4,12},{8,0},{12,4},{16,24},{20,28},{24,16},{28,20},{1,9},{5... | collective-permute-start | bytes 1179656 | tf_op jit(solution)/shard_map/ppermute | solution.py:43
  (98 other events, 814.0 us)
Sparse Core Ops, SparseCore 0:
  22.3 50.1 all-gather.1
  243.7 64.9 reduce-scatter.1

commit v5 on v4

--- a/solution.py
+++ b/solution.py
@@ -184,9 +184,10 @@
     attn_rows = rows_of_group(norm_rows(local_x, attention_gain).astype(low))
     attn_pack = jnp.concatenate([query_weight, key_weight, value_weight, out_weight.T], axis=1)
     attn_cols = attn_pack.shape[1]
-    for bit in dp_bits[1:]:
+    for bit in dp_bits[1:-1]:
         attn_pack = widen(attn_pack, group, "dp", bit, 0)
-    attn_pack = widen(attn_pack, group, "dp", 1, attn_pack.ndim - 2).reshape(width, attn_cols)
+    attn_pack = widen(attn_pack, group, "dp", 1, attn_pack.ndim - 2)
+    attn_pack = widen(attn_pack, group, "dp", dp_bits[-1], 0).reshape(width, attn_cols)
     project = attn_pack[:, : query_cols + 2 * key_cols]
     out_turned = attn_pack[:, query_cols + 2 * key_cols :]
     feed_pack = whole_weight(jnp.concatenate([gate_weight, up_weight, down_weight.T], axis=1))

time: 389 us -> 385 us (0.990)
  starting transfers between devices: 51.5 us -> 43.6 us
  waiting for transfers between devices: 151 us -> 155 us
    ppermute x35, starting transfers between devices: 51.4 us -> 43.5 us  [swap(): lax.ppermute(values, axis, [(index, index ^ bit) for index in range(count)])]
    ppermute x35, waiting for transfers between devices: 151 us -> 155 us  [swap(): lax.ppermute(values, axis, [(index, index ^ bit) for index in range(count)])]
  transfers between devices with their start and end apart: 37 -> 37, of which waited for: 25 -> 24; matrix products, arithmetic and copies ran while one was open for 36% -> 36% of each run, Pallas kernels for 0% -> 0%
where the time goes in v5:
time: 385 us; the launch traced here: 379 us
  waiting for transfers between devices  155 us (40%)
  matrix products  76.8 us (20%)
  other arithmetic  48.8 us (13%)
  starting transfers between devices  43.6 us (11%)
  local copies, waits for them, and re-layouts  38.1 us (10%)
  between operations  16.1 us (4%)
    ppermute x35, waiting for transfers between devices, swap(): lax.ppermute(values, axis, [(index, index ^ bit) for index in range(count)])  155 us
    ppermute x35, starting transfers between devices, swap(): lax.ppermute(values, axis, [(index, index ^ bit) for index in range(count)])  43.5 us
    dot_general x20, matrix products, dot_t(): lax.dot_general(left, right, (((1,), (1,)), ((), ())), preferred_element_...  27.9 us
    dot_general x8, matrix products, dot(): return jnp.dot(left, right, preferred_element_type=jnp.float32)  19.8 us
    unnamed x198, local copies, waits for them, and re-layouts  17.4 us
    dot_general x5, matrix products, dot_tl(): lax.dot_general(left, right, (((0,), (0,)), ((), ())), preferred_element_...  14.4 us
  transfers between devices with their start and end apart: 37, of which 24 were waited for; matrix products, arithmetic and copies ran while one was open for 36% of the time, Pallas kernels for 0%

profile of v5, /device:TPU:0, one launch (start us, length us, event | category | flops | bytes accessed | tf_op | source)
XLA Modules:
  0.0 378.8 jit_solution(7182698276563582227)
XLA Ops:
  9.8 4.1 %collective-permute-start.1 = (bf16[4,1,64,1024]{3,2,1,0:T(8,128)(2,1)S(1)}, bf16[4,1,64,1024]{3,2,1,0:T(8,128)(2,1)}, u32[]{:S(2)}, u32[]{:S(2)}) collective-permute-start(bf16[4,1,64,1024]{3,2,1,0:T(8,128)(2,1)S(1)} %fusion.57), channel_id=1, source_target_pairs={{0,2},{1,3},{2,0},{3,1},{4,6},{5,7},{6,4},{7,5},{8,10},{9,11},{10,... | collective-permute-start | bytes 1572872 | tf_op jit(solution)/shard_map/ppermute | solution.py:43
  25.6 11.8 %collective-permute-done.1 = bf16[4,1,64,1024]{3,2,1,0:T(8,128)(2,1)} collective-permute-done((bf16[4,1,64,1024]{3,2,1,0:T(8,128)(2,1)S(1)}, bf16[4,1,64,1024]{3,2,1,0:T(8,128)(2,1)}, u32[]{:S(2)}, u32[]{:S(2)}) %collective-permute-start.1) | collective-permute-done | bytes 524320 | tf_op jit(solution)/shard_map/ppermute | solution.py:43
  42.1 8.6 %collective-permute-done.2 = bf16[4,1,64,1024]{3,2,1,0:T(8,128)(2,1)} collective-permute-done((bf16[4,1,64,1024]{3,2,1,0:T(8,128)(2,1)}, bf16[4,1,64,1024]{3,2,1,0:T(8,128)(2,1)}, u32[]{:S(2)}, u32[]{:S(2)}) %collective-permute-start.2) | collective-permute-done | bytes 524320 | tf_op jit(solution)/shard_map/ppermute | solution.py:43
  50.7 2.9 pad_maximum_fusion.4
  53.6 3.0 collective-permute-start.7
  59.3 9.1 %collective-permute-done.5 = bf16[2,2,128,768]{2,3,0,1:T(8,128)(2,1)} collective-permute-done((bf16[2,2,128,768]{2,3,0,1:T(8,128)(2,1)S(1)}, bf16[2,2,128,768]{2,3,0,1:T(8,128)(2,1)}, u32[]{:S(2)}, u32[]{:S(2)}) %collective-permute-start.5) | collective-permute-done | bytes 786464 | tf_op jit(solution)/shard_map/ppermute | solution.py:43
  72.5 4.0 %reshape.461 = bf16[1024,768]{0,1:T(8,128)(2,1)} reshape(bf16[2,2,2,128,768]{3,2,1,0,4:T(2,128)(2,1)} %copy.98) | data formatting | bytes 3145728 | tf_op jit(solution)/shard_map/reshape | solution.py:190
  76.5 3.6 fusion.169
  95.7 5.0 %collective-permute-done.8 = bf16[256,1024]{1,0:T(8,128)(2,1)S(1)} collective-permute-done((bf16[256,1024]{1,0:T(8,128)(2,1)}, bf16[256,1024]{1,0:T(8,128)(2,1)S(1)}, u32[]{:S(2)}, u32[]{:S(2)}) %collective-permute-start.8) | collective-permute-done | bytes 524320 | tf_op jit(solution)/shard_map/ppermute | solution.py:43
  105.0 17.2 %collective-permute-done.9 = bf16[256,1024]{1,0:T(8,128)(2,1)S(1)} collective-permute-done((bf16[256,1024]{1,0:T(8,128)(2,1)S(1)}, bf16[256,1024]{1,0:T(8,128)(2,1)S(1)}, u32[]{:S(2)}, u32[]{:S(2)}) %collective-permute-start.9) | collective-permute-done | bytes 524320 | tf_op jit(solution)/shard_map/ppermute | solution.py:43
  125.5 11.6 %collective-permute-done.10 = bf16[256,1024]{1,0:T(8,128)(2,1)S(1)} collective-permute-done((bf16[256,1024]{1,0:T(8,128)(2,1)S(1)}, bf16[256,1024]{1,0:T(8,128)(2,1)S(1)}, u32[]{:S(2)}, u32[]{:S(2)}) %collective-permute-start.10) | collective-permute-done | bytes 524320 | tf_op jit(solution)/shard_map/ppermute | solution.py:43
  137.1 3.3 collective-permute-done.11
  150.0 9.5 %collective-permute-done.12 = bf16[256,1024]{1,0:T(8,128)(2,1)} collective-permute-done((bf16[256,1024]{1,0:T(8,128)(2,1)}, bf16[256,1024]{1,0:T(8,128)(2,1)}, u32[]{:S(2)}, u32[]{:S(2)}) %collective-permute-start.12) | collective-permute-done | bytes 524320 | tf_op jit(solution)/shard_map/ppermute | solution.py:43
  159.5 4.0 %fusion.82 = f32[512,1152]{1,0:T(8,128)S(1)} fusion(bf16[1024,3456]{0,1:T(8,128)(2,1)} %all-gather.2.cloned.1.call-done, bf16[256,1024]{1,0:T(8,128)(2,1)} %collective-permute-done.12, bf16[256,1024]{1,0:T(8,128)(2,1)} %multiply_convert_fusion.6), kind=kOutput, calls=%fused_computation.151 | convolution fusion | flops 1210056704 | bytes 5767168 | tf_op jit(solution)/shard_map/dot_general | solution.py:56
  172.8 5.5 %collective-permute-done.14 = bf16[256,1024]{1,0:T(8,128)(2,1)S(1)} collective-permute-done((bf16[256,1024]{1,0:T(8,128)(2,1)S(1)}, bf16[256,1024]{1,0:T(8,128)(2,1)S(1)}, u32[]{:S(2)}, u32[]{:S(2)}) %collective-permute-start.14) | collective-permute-done | bytes 524320 | tf_op jit(solution)/shard_map/ppermute | solution.py:43
  186.8 9.1 %collective-permute-done.15 = bf16[256,1024]{1,0:T(8,128)(2,1)S(1)} collective-permute-done((bf16[256,1024]{1,0:T(8,128)(2,1)S(1)}, bf16[256,1024]{1,0:T(8,128)(2,1)S(1)}, u32[]{:S(2)}, u32[]{:S(2)}) %collective-permute-start.15) | collective-permute-done | bytes 524320 | tf_op jit(solution)/shard_map/ppermute | solution.py:43
  200.9 17.4 %collective-permute-done.16 = bf16[256,1024]{1,0:T(8,128)(2,1)S(1)} collective-permute-done((bf16[256,1024]{1,0:T(8,128)(2,1)S(1)}, bf16[256,1024]{1,0:T(8,128)(2,1)S(1)}, u32[]{:S(2)}, u32[]{:S(2)}) %collective-permute-start.16) | collective-permute-done | bytes 524320 | tf_op jit(solution)/shard_map/ppermute | solution.py:43
  225.5 4.1 %convolution_convert_fusion = bf16[1024,1152]{1,0:T(8,128)(2,1)S(1)} fusion(bf16[1024,1152]{1,0:T(8,128)(2,1)S(1)} %pad_maximum_fusion.1, bf16[256,1024]{1,0:T(8,128)(2,1)S(1)} %copy-done.40, bf16[256,1024]{1,0:T(8,128)(2,1)} %collective-permute-done.7, bf16[256,1024]{1,0:T(8,128)(2,1)} %collective-permute-done.6, bf16[256,1024]{1,0:T(8,128)(2,1)S(1)} %bitcast.234), kind=kOutput, calls=%fused_computation.24 | convolution fusion | flops 2425487360 | bytes 6815744 | tf_op jit(solution)/shard_map/dot_general | solution.py:66
  229.6 4.1 %convolution_convert_fusion.2 = bf16[1024,1152]{1,0:T(8,128)(2,1)S(1)} fusion(bf16[1024,1152]{1,0:T(8,128)(2,1)S(1)} %pad_maximum_fusion.2, bf16[256,1024]{1,0:T(8,128)(2,1)S(1)} %collective-permute-done.14, bf16[256,1024]{1,0:T(8,128)(2,1)S(1)} %collective-permute-done.13, bf16[256,1024]{1,0:T(8,128)(2,1)} %collective-permute-done.12, ...), kind=kOutput, calls=%fused_computation.26 | convolution fusion | flops 2425487360 | bytes 6815744 | tf_op jit(solution)/shard_map/dot_general | solution.py:66
  233.8 4.1 %convolution_convert_fusion.1 = bf16[1024,1152]{1,0:T(8,128)(2,1)S(1)} fusion(bf16[1024,1152]{1,0:T(8,128)(2,1)S(1)} %pad_maximum_fusion.3, bf16[256,1024]{1,0:T(8,128)(2,1)S(1)} %collective-permute-done.14, bf16[256,1024]{1,0:T(8,128)(2,1)S(1)} %collective-permute-done.13, bf16[256,1024]{1,0:T(8,128)(2,1)} %collective-permute-done.12, ...), kind=kOutput, calls=%fused_computation.25 | convolution fusion | flops 2425487360 | bytes 6815744 | tf_op jit(solution)/shard_map/dot_general | solution.py:66
  237.9 3.5 pad_maximum_fusion
  241.5 3.9 %fusion.68 = f32[256,1024]{1,0:T(8,128)} fusion(bf16[1024,3456]{0,1:T(8,128)(2,1)} %all-gather.2.cloned.1.call-done, bf16[1024,1152]{1,0:T(8,128)(2,1)} %copy-done.20), kind=kOutput, calls=%fused_computation.139 | convolution fusion | flops 603979776 | bytes 3997696 | tf_op jit(solution)/shard_map/dot_general | solution.py:60
  247.0 3.4 fusion.63
  250.4 8.9 %collective-permute-done.18 = bf16[256,1024]{1,0:T(8,128)(2,1)} collective-permute-done((bf16[256,1024]{1,0:T(8,128)(2,1)}, bf16[256,1024]{1,0:T(8,128)(2,1)}, u32[]{:S(2)}, u32[]{:S(2)}) %collective-permute-start.18) | collective-permute-done | bytes 524320 | tf_op jit(solution)/shard_map/ppermute | solution.py:43
  259.3 3.6 add_convert_fusion.3
  262.9 5.6 %collective-permute-done.21 = bf16[4,1,64,1024]{3,2,1,0:T(8,128)(2,1)S(1)} collective-permute-done((bf16[4,1,64,1024]{3,2,1,0:T(8,128)(2,1)}, bf16[4,1,64,1024]{3,2,1,0:T(8,128)(2,1)S(1)}, u32[]{:S(2)}, u32[]{:S(2)}) %collective-permute-start.21) | collective-permute-done | bytes 524320 | tf_op jit(solution)/shard_map/ppermute | solution.py:43
  275.9 3.6 fusion.2
  294.0 9.6 %collective-permute-done.22 = bf16[256,1024]{1,0:T(8,128)(2,1)} collective-permute-done((bf16[256,1024]{1,0:T(8,128)(2,1)}, bf16[256,1024]{1,0:T(8,128)(2,1)}, u32[]{:S(2)}, u32[]{:S(2)}) %collective-permute-start.22) | collective-permute-done | bytes 524320 | tf_op jit(solution)/shard_map/ppermute | solution.py:43
  325.9 4.8 %collective-permute-done.27 = bf16[512,768]{0,1:T(8,128)(2,1)} collective-permute-done((bf16[512,768]{0,1:T(8,128)(2,1)}, bf16[512,768]{0,1:T(8,128)(2,1)}, u32[]{:S(2)}, u32[]{:S(2)}) %collective-permute-start.27) | collective-permute-done | bytes 786464 | tf_op jit(solution)/shard_map/ppermute | solution.py:43
  334.1 3.3 collective-permute-done.25
  341.5 3.3 collective-permute-done.28
  350.3 5.3 %collective-permute-done.29 = f32[2176]{0:T(1024)S(1)} collective-permute-done((f32[2176]{0:T(1024)S(1)}, f32[2176]{0:T(1024)S(1)}, u32[]{:S(2)}, u32[]{:S(2)}) %collective-permute-start.29) | collective-permute-done | bytes 8736 | tf_op jit(solution)/shard_map/ppermute | solution.py:43
  (397 shorter events, 162.0 us)
Async XLA Ops:
  7.2 134.5 %all-gather.2.cloned.1.call-start = ((), (), s32[]{:S(2)}) async-start(), calls=%async_computation.1 | async-start | bytes 7962624 | tf_op jit(solution)/shard_map/all_gather | solution.py:178
  9.8 27.5 %collective-permute-start.1 = (bf16[4,1,64,1024]{3,2,1,0:T(8,128)(2,1)S(1)}, bf16[4,1,64,1024]{3,2,1,0:T(8,128)(2,1)}, u32[]{:S(2)}, u32[]{:S(2)}) collective-permute-start(bf16[4,1,64,1024]{3,2,1,0:T(8,128)(2,1)S(1)} %fusion.57), channel_id=1, source_target_pairs={{0,2},{1,3},{2,0},{3,1},{4,6},{5,7},{6,4},{7,5},{8,10},{9,11},{10,... | collective-permute-start | bytes 1572872 | tf_op jit(solution)/shard_map/ppermute | solution.py:43
  13.9 28.1 %collective-permute-start = (bf16[4,1,64,1024]{3,2,1,0:T(8,128)(2,1)S(1)}, bf16[4,1,64,1024]{3,2,1,0:T(8,128)(2,1)}, u32[]{:S(2)}, u32[]{:S(2)}) collective-permute-start(bf16[4,1,64,1024]{3,2,1,0:T(8,128)(2,1)S(1)} %fusion.57), channel_id=1, source_target_pairs={{0,1},{1,0},{2,3},{3,2},{4,5},{5,4},{6,7},{7,6},{8,9},{9,8},{10,11... | collective-permute-start | bytes 1572872 | tf_op jit(solution)/shard_map/ppermute | solution.py:43
  22.2 300.5 %reduce-scatter.2.cloned.1.call-start = ((), (), s32[]{:S(2)}) async-start(), calls=%async_computation.2 | async-start | bytes 7962624 | tf_op jit(solution)/shard_map/reduce_scatter | solution.py:181
  25.4 12.4 %collective-permute-start.4 = (bf16[2,128,768]{1,2,0:T(8,128)(2,1)S(1)}, bf16[2,128,768]{1,2,0:T(8,128)(2,1)S(1)}, u32[]{:S(2)}, u32[]{:S(2)}) collective-permute-start(bf16[2,128,768]{1,2,0:T(8,128)(2,1)S(1)} %pad_maximum_fusion.17), channel_id=1, source_target_pairs={{0,4},{4,0},{8,12},{12,8},{16,20},{20,16},{24,28},{28,24},{1,5},{5... | collective-permute-start | bytes 1179656 | tf_op jit(solution)/shard_map/ppermute | solution.py:43
  37.3 13.4 %collective-permute-start.2 = (bf16[4,1,64,1024]{3,2,1,0:T(8,128)(2,1)}, bf16[4,1,64,1024]{3,2,1,0:T(8,128)(2,1)}, u32[]{:S(2)}, u32[]{:S(2)}) collective-permute-start(bf16[4,1,64,1024]{3,2,1,0:T(8,128)(2,1)} %collective-permute-done.1), channel_id=1, source_target_pairs={{0,1},{1,0},{2,3},{3,2},{4,5},{5,4},{6,7},{7,6},{8,9},{9,8},{10,11... | collective-permute-start | bytes 1572872 | tf_op jit(solution)/shard_map/ppermute | solution.py:43
  38.0 30.4 %collective-permute-start.5 = (bf16[2,2,128,768]{2,3,0,1:T(8,128)(2,1)S(1)}, bf16[2,2,128,768]{2,3,0,1:T(8,128)(2,1)}, u32[]{:S(2)}, u32[]{:S(2)}) collective-permute-start(bf16[2,2,128,768]{2,3,0,1:T(8,128)(2,1)S(1)} %pad_maximum_fusion.13), channel_id=1, source_target_pairs={{0,16},{4,20},{8,24},{12,28},{16,0},{20,4},{24,8},{28,12},{1,17},{... | collective-permute-start | bytes 2359304 | tf_op jit(solution)/shard_map/ppermute | solution.py:43
  53.6 37.0 %collective-permute-start.7 = (bf16[256,1024]{1,0:T(8,128)(2,1)S(1)}, bf16[256,1024]{1,0:T(8,128)(2,1)}, u32[]{:S(2)}, u32[]{:S(2)}) collective-permute-start(bf16[256,1024]{1,0:T(8,128)(2,1)S(1)} %bitcast.231), channel_id=1, source_target_pairs={{0,2},{1,3},{2,0},{3,1},{4,6},{5,7},{6,4},{7,5},{8,10},{9,11},{10,... | collective-permute-start | bytes 1572872 | tf_op jit(solution)/shard_map/ppermute | solution.py:43
  56.7 37.8 %collective-permute-start.6 = (bf16[256,1024]{1,0:T(8,128)(2,1)S(1)}, bf16[256,1024]{1,0:T(8,128)(2,1)}, u32[]{:S(2)}, u32[]{:S(2)}) collective-permute-start(bf16[256,1024]{1,0:T(8,128)(2,1)S(1)} %bitcast.232), channel_id=1, source_target_pairs={{0,1},{1,0},{2,3},{3,2},{4,5},{5,4},{6,7},{7,6},{8,9},{9,8},{10,11... | collective-permute-start | bytes 1572872 | tf_op jit(solution)/shard_map/ppermute | solution.py:43
  90.7 10.0 %collective-permute-start.8 = (bf16[256,1024]{1,0:T(8,128)(2,1)}, bf16[256,1024]{1,0:T(8,128)(2,1)S(1)}, u32[]{:S(2)}, u32[]{:S(2)}) collective-permute-start(bf16[256,1024]{1,0:T(8,128)(2,1)} %collective-permute-done.7), channel_id=1, source_target_pairs={{0,1},{1,0},{2,3},{3,2},{4,5},{5,4},{6,7},{7,6},{8,9},{9,8},{10,11... | collective-permute-start | bytes 1572872 | tf_op jit(solution)/shard_map/ppermute | solution.py:43
  104.2 18.0 %collective-permute-start.9 = (bf16[256,1024]{1,0:T(8,128)(2,1)S(1)}, bf16[256,1024]{1,0:T(8,128)(2,1)S(1)}, u32[]{:S(2)}, u32[]{:S(2)}) collective-permute-start(bf16[256,1024]{1,0:T(8,128)(2,1)S(1)} %convolution_convert_fusion.4), channel_id=1, source_target_pairs={{0,1},{1,0},{2,3},{3,2},{4,5},{5,4},{6,7},{7,6},{8,9},{9,8},{10,11... | collective-permute-start | bytes 1572872 | tf_op jit(solution)/shard_map/ppermute | solution.py:43
  122.5 14.6 %collective-permute-start.10 = (bf16[256,1024]{1,0:T(8,128)(2,1)S(1)}, bf16[256,1024]{1,0:T(8,128)(2,1)S(1)}, u32[]{:S(2)}, u32[]{:S(2)}) collective-permute-start(bf16[256,1024]{1,0:T(8,128)(2,1)S(1)} %fusion.128), channel_id=1, source_target_pairs={{0,1},{1,0},{2,3},{3,2},{4,5},{5,4},{6,7},{7,6},{8,9},{9,8},{10,11... | collective-permute-start | bytes 1572872 | tf_op jit(solution)/shard_map/ppermute | solution.py:43
  122.6 17.8 %collective-permute-start.11 = (bf16[256,1024]{1,0:T(8,128)(2,1)S(1)}, bf16[256,1024]{1,0:T(8,128)(2,1)S(1)}, u32[]{:S(2)}, u32[]{:S(2)}) collective-permute-start(bf16[256,1024]{1,0:T(8,128)(2,1)S(1)} %add_convert_fusion.5), channel_id=1, source_target_pairs={{0,2},{1,3},{2,0},{3,1},{4,6},{5,7},{6,4},{7,5},{8,10},{9,11},{10,... | collective-permute-start | bytes 1572872 | tf_op jit(solution)/shard_map/ppermute | solution.py:43
  144.8 14.7 %collective-permute-start.12 = (bf16[256,1024]{1,0:T(8,128)(2,1)}, bf16[256,1024]{1,0:T(8,128)(2,1)}, u32[]{:S(2)}, u32[]{:S(2)}) collective-permute-start(bf16[256,1024]{1,0:T(8,128)(2,1)} %multiply_convert_fusion.6), channel_id=1, source_target_pairs={{0,1},{1,0},{2,3},{3,2},{4,5},{5,4},{6,7},{7,6},{8,9},{9,8},{10,11... | collective-permute-start | bytes 1572872 | tf_op jit(solution)/shard_map/ppermute | solution.py:43
  149.4 17.7 %collective-permute-start.13 = (bf16[256,1024]{1,0:T(8,128)(2,1)}, bf16[256,1024]{1,0:T(8,128)(2,1)S(1)}, u32[]{:S(2)}, u32[]{:S(2)}) collective-permute-start(bf16[256,1024]{1,0:T(8,128)(2,1)} %multiply_convert_fusion.6), channel_id=1, source_target_pairs={{0,2},{1,3},{2,0},{3,1},{4,6},{5,7},{6,4},{7,5},{8,10},{9,11},{10,... | collective-permute-start | bytes 1572872 | tf_op jit(solution)/shard_map/ppermute | solution.py:43
  167.2 11.1 %collective-permute-start.14 = (bf16[256,1024]{1,0:T(8,128)(2,1)S(1)}, bf16[256,1024]{1,0:T(8,128)(2,1)S(1)}, u32[]{:S(2)}, u32[]{:S(2)}) collective-permute-start(bf16[256,1024]{1,0:T(8,128)(2,1)S(1)} %collective-permute-done.13), channel_id=1, source_target_pairs={{0,1},{1,0},{2,3},{3,2},{4,5},{5,4},{6,7},{7,6},{8,9},{9,8},{10,11... | collective-permute-start | bytes 1572872 | tf_op jit(solution)/shard_map/ppermute | solution.py:43
  185.5 10.5 %collective-permute-start.15 = (bf16[256,1024]{1,0:T(8,128)(2,1)S(1)}, bf16[256,1024]{1,0:T(8,128)(2,1)S(1)}, u32[]{:S(2)}, u32[]{:S(2)}) collective-permute-start(bf16[256,1024]{1,0:T(8,128)(2,1)S(1)} %fusion.27), channel_id=1, source_target_pairs={{0,1},{1,0},{2,3},{3,2},{4,5},{5,4},{6,7},{7,6},{8,9},{9,8},{10,11... | collective-permute-start | bytes 1572872 | tf_op jit(solution)/shard_map/ppermute | solution.py:43
  196.8 21.4 %collective-permute-start.17 = (bf16[256,1024]{1,0:T(8,128)(2,1)S(1)}, bf16[256,1024]{1,0:T(8,128)(2,1)S(1)}, u32[]{:S(2)}, u32[]{:S(2)}) collective-permute-start(bf16[256,1024]{1,0:T(8,128)(2,1)S(1)} %add_convert_fusion.4), channel_id=1, source_target_pairs={{0,2},{1,3},{2,0},{3,1},{4,6},{5,7},{6,4},{7,5},{8,10},{9,11},{10,... | collective-permute-start | bytes 1572872 | tf_op jit(solution)/shard_map/ppermute | solution.py:43
  198.7 19.6 %collective-permute-start.16 = (bf16[256,1024]{1,0:T(8,128)(2,1)S(1)}, bf16[256,1024]{1,0:T(8,128)(2,1)S(1)}, u32[]{:S(2)}, u32[]{:S(2)}) collective-permute-start(bf16[256,1024]{1,0:T(8,128)(2,1)S(1)} %convolution_add_fusion), channel_id=1, source_target_pairs={{0,1},{1,0},{2,3},{3,2},{4,5},{5,4},{6,7},{7,6},{8,9},{9,8},{10,11... | collective-permute-start | bytes 1572872 | tf_op jit(solution)/shard_map/ppermute | solution.py:43
  220.5 25.5 %collective-permute-start.20 = (bf16[4,1,64,1024]{3,2,1,0:T(8,128)(2,1)}, bf16[4,1,64,1024]{3,2,1,0:T(8,128)(2,1)}, u32[]{:S(2)}, u32[]{:S(2)}) collective-permute-start(bf16[4,1,64,1024]{3,2,1,0:T(8,128)(2,1)} %bitcast.39), channel_id=1, source_target_pairs={{0,2},{1,3},{2,0},{3,1},{4,6},{5,7},{6,4},{7,5},{8,10},{9,11},{10,... | collective-permute-start | bytes 1572872 | tf_op jit(solution)/shard_map/ppermute | solution.py:43
  221.8 41.1 %collective-permute-start.19 = (bf16[4,1,64,1024]{3,2,1,0:T(8,128)(2,1)}, bf16[4,1,64,1024]{3,2,1,0:T(8,128)(2,1)}, u32[]{:S(2)}, u32[]{:S(2)}) collective-permute-start(bf16[4,1,64,1024]{3,2,1,0:T(8,128)(2,1)} %bitcast.39), channel_id=1, source_target_pairs={{0,1},{1,0},{2,3},{3,2},{4,5},{5,4},{6,7},{7,6},{8,9},{9,8},{10,11... | collective-permute-start | bytes 1572872 | tf_op jit(solution)/shard_map/ppermute | solution.py:43
  225.1 34.2 %collective-permute-start.18 = (bf16[256,1024]{1,0:T(8,128)(2,1)}, bf16[256,1024]{1,0:T(8,128)(2,1)}, u32[]{:S(2)}, u32[]{:S(2)}) collective-permute-start(bf16[256,1024]{1,0:T(8,128)(2,1)} %convolution_convert_fusion.3), channel_id=1, source_target_pairs={{0,1},{1,0},{2,3},{3,2},{4,5},{5,4},{6,7},{7,6},{8,9},{9,8},{10,11... | collective-permute-start | bytes 1572872 | tf_op jit(solution)/shard_map/ppermute | solution.py:43
  246.0 22.5 %collective-permute-start.21 = (bf16[4,1,64,1024]{3,2,1,0:T(8,128)(2,1)}, bf16[4,1,64,1024]{3,2,1,0:T(8,128)(2,1)S(1)}, u32[]{:S(2)}, u32[]{:S(2)}) collective-permute-start(bf16[4,1,64,1024]{3,2,1,0:T(8,128)(2,1)} %collective-permute-done.20), channel_id=1, source_target_pairs={{0,1},{1,0},{2,3},{3,2},{4,5},{5,4},{6,7},{7,6},{8,9},{9,8},{10,11... | collective-permute-start | bytes 1572872 | tf_op jit(solution)/shard_map/ppermute | solution.py:43
  279.5 38.5 %collective-permute-start.23 = (bf16[256,1024]{1,0:T(8,128)(2,1)}, bf16[256,1024]{1,0:T(8,128)(2,1)}, u32[]{:S(2)}, u32[]{:S(2)}) collective-permute-start(bf16[256,1024]{1,0:T(8,128)(2,1)} %add_convert_fusion.3), channel_id=1, source_target_pairs={{0,2},{1,3},{2,0},{3,1},{4,6},{5,7},{6,4},{7,5},{8,10},{9,11},{10,... | collective-permute-start | bytes 1572872 | tf_op jit(solution)/shard_map/ppermute | solution.py:43
  280.3 23.3 %collective-permute-start.22 = (bf16[256,1024]{1,0:T(8,128)(2,1)}, bf16[256,1024]{1,0:T(8,128)(2,1)}, u32[]{:S(2)}, u32[]{:S(2)}) collective-permute-start(bf16[256,1024]{1,0:T(8,128)(2,1)} %fusion.63), channel_id=1, source_target_pairs={{0,1},{1,0},{2,3},{3,2},{4,5},{5,4},{6,7},{7,6},{8,9},{9,8},{10,11... | collective-permute-start | bytes 1572872 | tf_op jit(solution)/shard_map/ppermute | solution.py:43
  309.7 10.7 %collective-permute-start.24 = (bf16[256,1024]{1,0:T(8,128)(2,1)}, bf16[256,1024]{1,0:T(8,128)(2,1)}, u32[]{:S(2)}, u32[]{:S(2)}) collective-permute-start(bf16[256,1024]{1,0:T(8,128)(2,1)} %fusion.117), channel_id=1, source_target_pairs={{0,1},{1,0},{2,3},{3,2},{4,5},{5,4},{6,7},{7,6},{8,9},{9,8},{10,11... | collective-permute-start | bytes 1572872 | tf_op jit(solution)/shard_map/ppermute | solution.py:43
  313.3 17.4 %collective-permute-start.27 = (bf16[512,768]{0,1:T(8,128)(2,1)}, bf16[512,768]{0,1:T(8,128)(2,1)}, u32[]{:S(2)}, u32[]{:S(2)}) collective-permute-start(bf16[512,768]{0,1:T(8,128)(2,1)} %fusion.98), channel_id=1, source_target_pairs={{0,16},{4,20},{8,24},{12,28},{16,0},{20,4},{24,8},{28,12},{1,17},{... | collective-permute-start | bytes 2359304 | tf_op jit(solution)/shard_map/ppermute | solution.py:43
  324.1 13.3 %collective-permute-start.25 = (bf16[256,1024]{1,0:T(8,128)(2,1)}, bf16[256,1024]{1,0:T(8,128)(2,1)S(1)}, u32[]{:S(2)}, u32[]{:S(2)}) collective-permute-start(bf16[256,1024]{1,0:T(8,128)(2,1)} %fusion.115), channel_id=1, source_target_pairs={{0,1},{1,0},{2,3},{3,2},{4,5},{5,4},{6,7},{7,6},{8,9},{9,8},{10,11... | collective-permute-start | bytes 1572872 | tf_op jit(solution)/shard_map/ppermute | solution.py:43
  333.0 24.0 %collective-permute-start.26 = (bf16[256,1024]{1,0:T(8,128)(2,1)}, bf16[256,1024]{1,0:T(8,128)(2,1)}, u32[]{:S(2)}, u32[]{:S(2)}) collective-permute-start(bf16[256,1024]{1,0:T(8,128)(2,1)} %add_convert_fusion.1), channel_id=1, source_target_pairs={{0,2},{1,3},{2,0},{3,1},{4,6},{5,7},{6,4},{7,5},{8,10},{9,11},{10,... | collective-permute-start | bytes 1572872 | tf_op jit(solution)/shard_map/ppermute | solution.py:43
  337.4 7.5 %collective-permute-start.28 = (f32[2176]{0:T(1024)S(1)}, f32[2176]{0:T(1024)S(1)}, u32[]{:S(2)}, u32[]{:S(2)}) collective-permute-start(f32[2176]{0:T(1024)S(1)} %concatenate.102), channel_id=1, source_target_pairs={{0,1},{1,0},{2,3},{3,2},{4,5},{5,4},{6,7},{7,6},{8,9},{9,8},{10,11... | collective-permute-start | bytes 26120 | tf_op jit(solution)/shard_map/ppermute | solution.py:43
  344.8 10.7 %collective-permute-start.29 = (f32[2176]{0:T(1024)S(1)}, f32[2176]{0:T(1024)S(1)}, u32[]{:S(2)}, u32[]{:S(2)}) collective-permute-start(f32[2176]{0:T(1024)S(1)} %add.320), channel_id=1, source_target_pairs={{0,2},{1,3},{2,0},{3,1},{4,6},{5,7},{6,4},{7,5},{8,10},{9,11},{10,... | collective-permute-start | bytes 26120 | tf_op jit(solution)/shard_map/ppermute | solution.py:43
  348.1 18.6 %collective-permute-start.33 = (bf16[256,768]{0,1:T(8,128)(2,1)S(1)}, bf16[256,768]{0,1:T(8,128)(2,1)S(1)}, u32[]{:S(2)}, u32[]{:S(2)}) collective-permute-start(bf16[256,768]{0,1:T(8,128)(2,1)S(1)} %constant_dynamic-slice_fusion), channel_id=1, source_target_pairs={{0,8},{4,12},{8,0},{12,4},{16,24},{20,28},{24,16},{28,20},{1,9},{5... | collective-permute-start | bytes 1179656 | tf_op jit(solution)/shard_map/ppermute | solution.py:43
  (98 other events, 813.6 us)
Sparse Core Ops, SparseCore 0:
  22.3 57.1 all-gather.1
  241.6 65.5 reduce-scatter.1
